TPU v7x, 32 devices: a whole 2x2x4 slice. The times are simulated.
32 devices in a mesh: dp: 32 (over z, y, x, core), cent: 1.
Axes of the slice: x: 2, y: 2, z: 4, core: 2. Of those that a mesh axis runs over, the one named last changes fastest.
Arguments:
- hidden: bfloat16 [5632, 11008], P('dp', 'cent'), may hold values from -6 to 6
- residual: bfloat16 [5632, 4096], P('dp', 'cent'), may hold values from -6 to 6
- down_weight: bfloat16 [11008, 4096], P('cent', 'dp'), may hold values from -0.0546875 to 0.0546875
- gain: float32 [4096], P('cent'), may hold values from 0.1 to 1.9
- proj_weight: bfloat16 [4096, 1024], P('cent'), may hold values from -0.09375 to 0.09375
- centroids: bfloat16 [16384, 1024], P(('dp', 'cent')), may hold values from -24 to 24
Outputs:
- weighted: float32 [16384, 1024], P(('dp', 'cent'))
- counts: float32 [16384], P(('dp', 'cent'))
All inputs are finite; a program needn't handle non-finite values.
Results may differ from a plain program's by a relative error of at most 0.011.
Values may be sent and summed in bfloat16 or wider, within the bound.
No kernel may reach another device: no remote copies, remote signals or barrier semaphores. Data moves between devices by JAX's collectives and lax.ppermute only.
A program may use at most 192 MiB of HBM per device.

v0:
```python
import math

import jax
import jax.numpy as jnp
from jax import lax
from jax.experimental import pallas as pl
from jax.experimental.pallas import tpu as pltpu
from jax.sharding import PartitionSpec as P


F32 = jnp.float32
BF16 = jnp.bfloat16
PLANE = 8
QUAD = 4


def dot(a, b):
    return jnp.dot(a, b, preferred_element_type=F32)


def after(v, *others):
    return lax.optimization_barrier((v, *others))[0]


def lse(parts):
    top = parts[0]
    for p in parts[1:]:
        top = jnp.maximum(top, p)
    return top + jnp.log(sum(jnp.exp(p - top) for p in parts))


def padded(size):
    return -(-size // 128) * 128


def score_kernel(inverse, pair, *refs):
    blocks, (e, top, total) = refs[:-3], refs[-3:]
    count = sum(b.shape[0] for b in blocks)
    rest = jnp.zeros((e.shape[1] - count, pair.shape[1]), BF16)
    x = jnp.concatenate([b[...] for b in blocks] + [rest])
    s = lax.dot_general(pair[...], x, (((1,), (1,)), ((), ())), preferred_element_type=F32) * inverse
    most = jnp.max(s, axis=0, keepdims=True)
    weight = jnp.exp(s - most)
    column = lax.broadcasted_iota(jnp.int32, weight.shape, 1)
    e[...] = jnp.where(column < count, weight, 0.0).astype(BF16)
    top[...] = most
    total[...] = most + jnp.log(jnp.sum(weight, axis=0, keepdims=True))


def score(pair, blocks):
    cents, width = pair.shape
    count = padded(sum(b.shape[0] for b in blocks))
    return pl.pallas_call(
        lambda *refs: score_kernel(1.0 / (math.sqrt(width) * 0.05), *refs),
        out_shape=[
            jax.ShapeDtypeStruct((cents, count), BF16),
            jax.ShapeDtypeStruct((1, count), F32),
            jax.ShapeDtypeStruct((1, count), F32),
        ],
        compiler_params=pltpu.CompilerParams(vmem_limit_bytes=40 * 2**20),
        cost_estimate=pl.CostEstimate(
            flops=2 * cents * count * width,
            bytes_accessed=2 * (cents * width + count * width + cents * count),
            transcendentals=cents * count,
        ),
    )(pair, *blocks)


def weigh_kernel(sizes, scale, tiles, w, *refs):
    count, pieces = len(sizes), sum(len(s) for s in sizes)
    es, blocks = refs[:count], list(refs[count : count + pieces])
    near, far, counts, x, p = refs[count + pieces :]
    step = pl.program_id(0)

    @pl.when(step == 0)
    def _():
        at = 0
        for e, group in zip(es, sizes):
            stop = at + e.shape[1]
            for size in group:
                x[at : at + size] = blocks.pop(0)[...]
                at += size
            if at < stop:
                x[at:stop] = jnp.zeros((stop - at, x.shape[1]), BF16)
            at = stop

    at, masses = 0, 0.0
    for e in es:
        span = slice(at, at + e.shape[1])
        prob = e[...].astype(F32) * w[:, span]
        masses = masses + jnp.sum(prob, axis=1, keepdims=True)
        p[:, span] = prob.astype(BF16)
        at = span.stop
    counts[...] = jnp.transpose(jnp.broadcast_to(masses * scale, (masses.shape[0], 128)))[:1]
    sums = dot(p[...], x[...]) * scale

    @pl.when(step < tiles)
    def _():
        far[...] = sums.astype(BF16)

    @pl.when(step >= tiles)
    def _():
        near[...] = sums


def weigh(groups, es, w, scale):
    sizes = [[b.shape[0] for b in group] for group in groups]
    blocks = [b for group in groups for b in group]
    width = blocks[0].shape[1]
    cents = es[0].shape[0]
    passages = sum(e.shape[1] for e in es)
    tile = math.gcd(cents // 2, 256)
    tiles = cents // 2 // tile
    turn = lambda i: (i + tiles) % (2 * tiles)
    whole = lambda b: pl.BlockSpec(b.shape, lambda i: (0, 0), pipeline_mode=pl.Buffered(1))
    return pl.pallas_call(
        lambda *refs: weigh_kernel(sizes, scale, tiles, *refs),
        grid=(2 * tiles,),
        in_specs=[whole(w)]
        + [pl.BlockSpec((tile, e.shape[1]), lambda i: (turn(i), 0)) for e in es]
        + [whole(b) for b in blocks],
        out_specs=[
            pl.BlockSpec((tile, width), lambda i: (jnp.maximum(i - tiles, 0), 0)),
            pl.BlockSpec((tile, width), lambda i: (jnp.minimum(i, tiles - 1), 0)),
            pl.BlockSpec((1, tile), lambda i: (0, turn(i))),
        ],
        out_shape=[
            jax.ShapeDtypeStruct((cents // 2, width), F32),
            jax.ShapeDtypeStruct((cents // 2, width), BF16),
            jax.ShapeDtypeStruct((1, cents), F32),
        ],
        scratch_shapes=[pltpu.VMEM((passages, width), BF16), pltpu.VMEM((tile, passages), BF16)],
        compiler_params=pltpu.CompilerParams(vmem_limit_bytes=56 * 2**20),
        cost_estimate=pl.CostEstimate(
            flops=2 * cents * passages * width,
            bytes_accessed=2 * passages * (cents + width) + 8 * cents * width,
            transcendentals=0,
        ),
    )(w, *es, *blocks)


def deal_kernel(position, hidden, blocks):
    share = blocks.shape[2]
    for d in range(blocks.shape[0]):
        blocks[position[d]] = hidden[:, d * share : (d + 1) * share]


def deal(hidden, position):
    rows, hid = hidden.shape
    n = position.shape[0]
    vmem = pl.BlockSpec(memory_space=pltpu.VMEM)
    return pl.pallas_call(
        deal_kernel,
        in_specs=[pl.BlockSpec(memory_space=pltpu.SMEM), vmem],
        out_specs=vmem,
        out_shape=jax.ShapeDtypeStruct((n, rows, hid // n), hidden.dtype),
        compiler_params=pltpu.CompilerParams(vmem_limit_bytes=32 * 2**20),
        cost_estimate=pl.CostEstimate(flops=0, bytes_accessed=4 * rows * hid, transcendentals=0),
    )(position, hidden)


def arrivals(lines):
    table = []
    for z in range(lines):
        near = [(s, w, z - s if w == 0 else z + s) for s in range(1, lines) for w in (1, 0)]
        table.append([e for e in near if 0 <= e[2] < lines])
    return table


def make_body(n, lines):
    table = arrivals(lines)

    def hop(v, k):
        return lax.ppermute(v, "dp", [(i, i ^ k) for i in range(n)])

    def up(v):
        return lax.ppermute(v, "dp", [(i, i + PLANE) for i in range(n - PLANE)])

    def down(v):
        return lax.ppermute(v, "dp", [(i + PLANE, i) for i in range(n - PLANE)])

    def choose(line, values):
        out = values[-1]
        for z in range(lines - 2, -1, -1):
            if values[z] is not out:
                out = jnp.where(line <= z, values[z], out)
        return out

    def along(v):
        line = lax.axis_index("dp") // PLANE
        moved = {(0, 0): v, (0, 1): v}
        block = v
        for s in range(1, lines):
            ties = yield block
            below, above = moved[s - 1, 0], moved[s - 1, 1]
            if ties:
                below, above, *_ = lax.optimization_barrier((below, above, *ties))
            moved[s, 0], moved[s, 1] = up(below), down(above)
            block = choose(line, [moved[table[z][s - 1][:2]] for z in range(lines)])
        yield block

    def body(hidden, residual, down_weight, gain, proj_weight, centroids):
        me = lax.axis_index("dp")
        line, quad, core = me // PLANE, (me // 2) % QUAD, me % 2
        rows, hid = hidden.shape
        share = hid // n
        width = proj_weight.shape[1]
        cents = centroids.shape[0]

        orders = [[z] + [e[2] for e in table[z]] for z in range(lines)]
        place = jnp.array([[order.index(z) for z in range(lines)] for order in orders], jnp.int32)[line]
        d = jnp.arange(n)
        position = (((d // 2 % QUAD) ^ quad) * lines + place[d // PLANE]) * 2 + ((d % 2) ^ core)
        blocks = deal(hidden, position.astype(jnp.int32)).reshape(QUAD, lines, 2, rows, share)
        units = [blocks[0]] + [hop(blocks[k], 2 * k) for k in range(1, QUAD - 1)]

        down_rows = lax.all_to_all(down_weight, "dp", 0, 1, tiled=True)
        own = gain[:, None] * proj_weight.astype(F32)
        full = lax.all_gather(own, "cent", axis=0, tiled=True)
        high = lax.reduce_precision(full, 8, 7)
        low = (full - high).astype(BF16)
        high = high.astype(BF16)
        direct = dot(residual, own.astype(BF16))
        pair = jnp.concatenate([centroids, hop(centroids, 1)])
        last = blocks[QUAD - 1]
        down_rows, high, low, direct, pair, last, *units = lax.optimization_barrier(
            (down_rows, high, low, direct, pair, last, *units)
        )

        halves = [slice(0, width // 2), slice(width // 2, width)]
        folds = []
        for h in halves:
            source = after(down_rows, folds[0]) if folds else down_rows
            folds.append((dot(source, high[:, h]) + dot(source, low[:, h])).astype(BF16))
            if not units[QUAD - 1 :]:
                last, folds[0] = lax.optimization_barrier((last, folds[0]))
                units.append(hop(last, 2 * (QUAD - 1)))
        units = jnp.concatenate(units, axis=2)
        walks = [along(f) for f in folds]
        parts = [0.0, 0.0]
        for j in range(lines):
            for i, walk in enumerate(walks):
                block = next(walk) if j == 0 else walk.send(None)
                parts[i] = parts[i] + dot(units[j, 0], block) + dot(units[j, 1], hop(block, 1))
        raws = []
        for h, part in zip(halves, parts):
            part = part.reshape(QUAD, rows, -1)
            raw = part[0] + direct[:, h]
            for k in range(1, QUAD):
                raw = raw + hop(part[k].astype(BF16), 2 * k).astype(F32)
            raws.append(raw)
        raw = jnp.concatenate(raws, axis=1)
        raw = lax.psum(raw, "cent")
        embed = (raw * lax.rsqrt(jnp.mean(raw * raw, axis=1, keepdims=True) + 1e-06)).astype(BF16)

        def spread(block):
            return [block, hop(block, 2), hop(block, 4)]

        scale_up = cents * n * lax.axis_size("cent") / (rows * n)
        groups, tags, scored = [], [], []

        def take(blocks, names):
            groups.append(blocks)
            tags.append(names)
            scored.append(score(pair, blocks))

        first = spread(embed)
        lined = [None] + [hop(embed if k < 3 else after(embed, first[1]), k * PLANE) for k in range(1, lines)]
        take(first + [hop(first[1], 4)], [(0, q) for q in (0, 1, 2, 3)])
        late, late_names, ends, end_names = [], [], [], []
        for k in range(1, lines):
            wait = scored[k // 2 - 1][2] if k % 2 == 0 else scored[0][2] if k > 1 else None
            got = spread(lined[k] if wait is None else after(lined[k], wait))
            names = [(k, 0), (k, 1), (k, 2)]
            end = (2, 1) if k % 2 == 1 else (1, 2)
            start = got[end[0]]
            if k == 1:
                take(got + [hop(start, 2 * end[1])], names + [(k, 3)])
            else:
                late, late_names = late + got, late_names + names
                ends.append(hop(after(start, scored[1][2]), 2 * end[1]))
                end_names.append((k, 3))
        take(late, late_names)
        ends = lax.optimization_barrier((*ends, scored[-1][2]))[:-1]
        take(list(ends), end_names)

        parts = {}
        for names, (_, _, total) in zip(tags, scored):
            for i, name in enumerate(names):
                parts[name] = total[:, i * rows : (i + 1) * rows]
        v = jnp.stack([jnp.concatenate([parts[k, q] for q in range(QUAD)]) for k in range(lines)])
        got = [v] + [hop(v, 2 * k) for k in range(1, QUAD)]
        v = lse([jnp.stack([g[:, j ^ k] for j in range(QUAD)], axis=1) for k, g in enumerate(got)])
        got = [v] + [hop(v, PLANE * k) for k in range(1, lines)]
        v = lse([jnp.stack([g[j ^ k] for j in range(lines)]) for k, g in enumerate(got)])
        if lax.axis_size("cent") > 1:
            top = lax.pmax(v, "cent")
            v = top + jnp.log(lax.psum(jnp.exp(v - top), "cent"))
        tops = jnp.concatenate([top for _, top, _ in scored], axis=1)
        logs = []
        for names, (_, top, _) in zip(tags, scored):
            logs += [v[k, q] for k, q in names]
            logs.append(jnp.zeros(top.shape[1] - len(names) * rows, F32))
        w = jnp.exp(tops - jnp.concatenate(logs)[None])

        near, far, masses = weigh(groups, [e for e, _, _ in scored], w, scale_up)
        weighted = near + hop(far, 1).astype(F32)
        counts = masses[0, :cents] + hop(masses[0, cents:], 1)
        return weighted, counts

    return body


def solution(mesh):
    n = mesh.shape["dp"]
    in_specs = (
        P("dp", "cent"),
        P("dp", "cent"),
        P("cent", "dp"),
        P("cent"),
        P("cent", None),
        P(("dp", "cent"), None),
    )
    out_specs = (P(("dp", "cent"), None), P(("dp", "cent")))
    return jax.shard_map(
        make_body(n, n // PLANE), mesh=mesh, in_specs=in_specs, out_specs=out_specs, check_vma=False
    )
```

profile of v0, /device:TPU:0, one launch (start us, length us, event | category | flops | bytes accessed | tf_op | source)
XLA Modules:
  0.0 267.8 jit_solution(193065673580656228)
XLA Ops:
  0.6 7.4 %all-to-all-start = ((bf16[32,344,128]{2,1,0:T(8,128)(2,1)}), bf16[32,344,128]{2,1,0:T(8,128)(2,1)}, u32[]{:S(2)}, u32[]{:S(2)}) async-start(bf16[32,344,128]{2,1,0:T(8,128)(2,1)} %bitcast.131), calls=%async_computation | async-start | bytes 5636096 | tf_op jit(solution)/shard_map/all_to_all | solution.py:217
  9.7 2.6 fusion.56.position
  12.3 2.1 copy-done.2
  14.4 2.0 shard_map.86
  16.4 1.9 fusion.63
  18.3 1.7 collective-permute-start.1
  21.4 6.8 %fusion = (bf16[4096,1024]{1,0:T(8,128)(2,1)}, bf16[4096,1024]{1,0:T(8,128)(2,1)}) fusion(bf16[4096,1024]{1,0:T(8,128)(2,1)S(1)} %bitcast.125, f32[4096]{0:T(1024)S(1)} %copy-done.24), kind=kLoop, calls=%fused_computation.2 | loop fusion | flops 25165824 | bytes 25182208 | tf_op jit(solution)/shard_map/convert_element_type | solution.py:221
  28.2 2.9 %fusion.21 = f32[176,1024]{1,0:T(8,128)} fusion(bf16[176,4096]{1,0:T(8,128)(2,1)S(1)} %copy-done, bf16[4096,1024]{1,0:T(8,128)(2,1)S(1)} %bitcast.125, f32[4096]{0:T(1024)S(1)} %copy-done.24), kind=kOutput, calls=%fused_computation.32 | convolution fusion | flops 1488977920 | bytes 10567680 | tf_op jit(solution)/shard_map/dot_general | solution.py:18
  31.1 1.7 pad_maximum_fusion.refs_0_
  32.8 39.9 %all-to-all-done = bf16[32,344,128]{2,1,0:T(8,128)(2,1)} async-done(((bf16[32,344,128]{2,1,0:T(8,128)(2,1)}), bf16[32,344,128]{2,1,0:T(8,128)(2,1)}, u32[]{:S(2)}, u32[]{:S(2)}) %all-to-all-start) | async-done | bytes 2818080 | tf_op jit(solution)/shard_map/all_to_all | solution.py:217
  72.7 2.3 copy_bitcast_fusion
  75.0 4.0 %fusion.9 = f32[344,512]{1,0:T(8,128)S(1)} fusion(bf16[344,4096]{1,0:T(8,128)(2,1)S(1)} %copy_bitcast_fusion, bf16[4096,1024]{1,0:T(8,128)(2,1)} %get-tuple-element.43), kind=kOutput, calls=%fused_computation.11 | convolution fusion | flops 1442840576 | bytes 7716864 | tf_op jit(solution)/shard_map/dot_general | solution.py:18
  79.1 2.4 fusion.33
  83.0 2.4 fusion.30
  85.4 2.0 collective-permute-start.19
  87.5 2.0 collective-permute-start.3
  90.9 4.6 %collective-permute-start.6 = (bf16[344,512]{1,0:T(8,128)(2,1)}, bf16[344,512]{1,0:T(8,128)(2,1)S(1)}, u32[]{:S(2)}, u32[]{:S(2)}) collective-permute-start(bf16[344,512]{1,0:T(8,128)(2,1)} %fusion.33), channel_id=1, source_target_pairs={{0,8},{1,9},{2,10},{3,11},{4,12},{5,13},{6,14},{7,15},{8,16},{9,17... | collective-permute-start | bytes 1056776 | tf_op jit(solution)/shard_map/ppermute | solution.py:177
  96.9 5.0 %collective-permute-done.18 = bf16[344,512]{1,0:T(8,128)(2,1)} collective-permute-done((bf16[344,512]{1,0:T(8,128)(2,1)}, bf16[344,512]{1,0:T(8,128)(2,1)}, u32[]{:S(2)}, u32[]{:S(2)}) %collective-permute-start.18) | collective-permute-done | bytes 352288 | tf_op jit(solution)/shard_map/ppermute | solution.py:180
  101.9 2.8 %collective-permute-start.22 = (bf16[344,512]{1,0:T(8,128)(2,1)}, bf16[344,512]{1,0:T(8,128)(2,1)S(1)}, u32[]{:S(2)}, u32[]{:S(2)}) collective-permute-start(bf16[344,512]{1,0:T(8,128)(2,1)} %collective-permute-done.19), channel_id=1, source_target_pairs={{0,8},{1,9},{2,10},{3,11},{4,12},{5,13},{6,14},{7,15},{8,16},{9,17... | collective-permute-start | bytes 1056776 | tf_op jit(solution)/shard_map/ppermute | solution.py:177
  106.0 4.6 %collective-permute-start.9 = (bf16[344,512]{1,0:T(8,128)(2,1)S(1)}, bf16[344,512]{1,0:T(8,128)(2,1)S(1)}, u32[]{:S(2)}, u32[]{:S(2)}) collective-permute-start(bf16[344,512]{1,0:T(8,128)(2,1)S(1)} %collective-permute-done.6), channel_id=1, source_target_pairs={{0,8},{1,9},{2,10},{3,11},{4,12},{5,13},{6,14},{7,15},{8,16},{9,17... | collective-permute-start | bytes 1056776 | tf_op jit(solution)/shard_map/ppermute | solution.py:177
  116.4 4.6 %collective-permute-start.25 = (bf16[344,512]{1,0:T(8,128)(2,1)S(1)}, bf16[344,512]{1,0:T(8,128)(2,1)S(1)}, u32[]{:S(2)}, u32[]{:S(2)}) collective-permute-start(bf16[344,512]{1,0:T(8,128)(2,1)S(1)} %collective-permute-done.22), channel_id=1, source_target_pairs={{0,8},{1,9},{2,10},{3,11},{4,12},{5,13},{6,14},{7,15},{8,16},{9,17... | collective-permute-start | bytes 1056776 | tf_op jit(solution)/shard_map/ppermute | solution.py:177
  122.3 4.6 %collective-permute-start.12 = (bf16[344,512]{1,0:T(8,128)(2,1)S(1)}, bf16[344,512]{1,0:T(8,128)(2,1)S(1)}, u32[]{:S(2)}, u32[]{:S(2)}) collective-permute-start(bf16[344,512]{1,0:T(8,128)(2,1)S(1)} %collective-permute-done.9), channel_id=1, source_target_pairs={{0,8},{1,9},{2,10},{3,11},{4,12},{5,13},{6,14},{7,15},{8,16},{9,17... | collective-permute-start | bytes 1056776 | tf_op jit(solution)/shard_map/ppermute | solution.py:177
  130.4 3.5 %collective-permute-done.24 = bf16[344,512]{1,0:T(8,128)(2,1)S(1)} collective-permute-done((bf16[344,512]{1,0:T(8,128)(2,1)S(1)}, bf16[344,512]{1,0:T(8,128)(2,1)S(1)}, u32[]{:S(2)}, u32[]{:S(2)}) %collective-permute-start.24) | collective-permute-done | bytes 352288 | tf_op jit(solution)/shard_map/ppermute | solution.py:180
  136.6 4.1 %collective-permute-done.11 = bf16[344,512]{1,0:T(8,128)(2,1)S(1)} collective-permute-done((bf16[344,512]{1,0:T(8,128)(2,1)S(1)}, bf16[344,512]{1,0:T(8,128)(2,1)S(1)}, u32[]{:S(2)}, u32[]{:S(2)}) %collective-permute-start.11) | collective-permute-done | bytes 352288 | tf_op jit(solution)/shard_map/ppermute | solution.py:180
  147.6 1.6 collective-permute-start.29
  149.2 1.9 collective-permute-start.28
  157.1 1.9 collective-permute-start.15
  160.1 2.9 %collective-permute-done.14 = bf16[176,512]{1,0:T(8,128)(2,1)S(1)} collective-permute-done((bf16[176,512]{1,0:T(8,128)(2,1)S(1)}, bf16[176,512]{1,0:T(8,128)(2,1)S(1)}, u32[]{:S(2)}, u32[]{:S(2)}) %collective-permute-start.14) | collective-permute-done | bytes 180256 | tf_op jit(solution)/shard_map/ppermute | solution.py:174
  163.0 2.8 %collective-permute-done.16 = bf16[176,512]{1,0:T(8,128)(2,1)S(1)} collective-permute-done((bf16[176,512]{1,0:T(8,128)(2,1)S(1)}, bf16[176,512]{1,0:T(8,128)(2,1)S(1)}, u32[]{:S(2)}, u32[]{:S(2)}) %collective-permute-start.16) | collective-permute-done | bytes 180256 | tf_op jit(solution)/shard_map/ppermute | solution.py:174
  167.8 1.8 collective-permute-start.33
  171.6 5.6 %collective-permute-done.33.refs_1_.refs_9_ = bf16[176,1024]{1,0:T(8,128)(2,1)S(1)} collective-permute-done((bf16[176,1024]{1,0:T(8,128)(2,1)S(1)}, bf16[176,1024]{1,0:T(8,128)(2,1)S(1)}, u32[]{:S(2)}, u32[]{:S(2)}) %collective-permute-start.33) | collective-permute-done | bytes 360480 | tf_op jit(solution)/shard_map/ppermute | solution.py:174
  180.6 2.8 %collective-permute-start.40 = (bf16[176,1024]{1,0:T(8,128)(2,1)S(1)}, bf16[176,1024]{1,0:T(8,128)(2,1)S(1)}, u32[]{:S(2)}, u32[]{:S(2)}) collective-permute-start(bf16[176,1024]{1,0:T(8,128)(2,1)S(1)} %multiply_convert_fusion.refs_1_.refs_5_), channel_id=1, source_target_pairs={{0,24},{1,25},{2,26},{3,27},{4,28},{5,29},{6,30},{7,31},{8,16},{9,... | collective-permute-start | bytes 1081352 | tf_op jit(solution)/shard_map/ppermute | solution.py:174
  183.4 5.1 %collective-permute-done.35.refs_3_.refs_11_ = bf16[176,1024]{1,0:T(8,128)(2,1)S(1)} collective-permute-done((bf16[176,1024]{1,0:T(8,128)(2,1)S(1)}, bf16[176,1024]{1,0:T(8,128)(2,1)S(1)}, u32[]{:S(2)}, u32[]{:S(2)}) %collective-permute-start.35) | collective-permute-done | bytes 360480 | tf_op jit(solution)/shard_map/ppermute | solution.py:174
  188.5 1.7 collective-permute-start.36
  190.2 3.9 %collective-permute-done.32.refs_4_.refs_8_ = bf16[176,1024]{1,0:T(8,128)(2,1)S(1)} collective-permute-done((bf16[176,1024]{1,0:T(8,128)(2,1)S(1)}, bf16[176,1024]{1,0:T(8,128)(2,1)S(1)}, u32[]{:S(2)}, u32[]{:S(2)}) %collective-permute-start.32) | collective-permute-done | bytes 360480 | tf_op jit(solution)/shard_map/ppermute | solution.py:174
  194.1 2.6 shard_map.87
  197.9 6.9 %collective-permute-done.37.refs_1_.refs_13_ = bf16[176,1024]{1,0:T(8,128)(2,1)S(1)} collective-permute-done((bf16[176,1024]{1,0:T(8,128)(2,1)S(1)}, bf16[176,1024]{1,0:T(8,128)(2,1)S(1)}, u32[]{:S(2)}, u32[]{:S(2)}) %collective-permute-start.37) | collective-permute-done | bytes 360480 | tf_op jit(solution)/shard_map/ppermute | solution.py:174
  205.1 1.7 collective-permute-start.38
  207.1 1.8 collective-permute-start.41
  209.0 2.6 shard_map.88
  212.8 8.4 %collective-permute-done.42.refs_6_.refs_18_ = bf16[176,1024]{1,0:T(8,128)(2,1)S(1)} collective-permute-done((bf16[176,1024]{1,0:T(8,128)(2,1)S(1)}, bf16[176,1024]{1,0:T(8,128)(2,1)S(1)}, u32[]{:S(2)}, u32[]{:S(2)}) %collective-permute-start.42) | collective-permute-done | bytes 360480 | tf_op jit(solution)/shard_map/ppermute | solution.py:174
  221.2 1.8 collective-permute-start.43
  223.3 4.2 %shard_map.89 = (bf16[1024,1152]{1,0:T(8,128)(2,1)S(1)}, f32[1,1152]{1,0:T(1,128)S(1)}, f32[1,1152]{1,0:T(1,128)S(1)}) custom-call(bf16[1024,1024]{1,0:T(8,128)(2,1)S(1)} %pad_maximum_fusion.refs_0_, bf16[176,1024]{1,0:T(8,128)(2,1)S(1)} %collective-permute-done.37.refs_1_.refs_13_, bf16[176,1024]{1,0:T(8,128)(2,1)S(1)} %collective-permute-done.38.refs_2_.refs_14_, ...), custom_call_target="tpu_custom_call" | custom-call | flops 2415919104 | bytes 6815744 | tf_op jit(solution)/shard_map/pallas_call | solution.py:53
  231.9 1.8 shard_map.90
  236.6 1.7 collective-permute-start.45
  241.0 2.6 collective-permute-start.50
  248.2 12.9 %shard_map.91 = (f32[512,1024]{1,0:T(8,128)}, bf16[512,1024]{1,0:T(8,128)(2,1)}, f32[1,1024]{1,0:T(1,128)}) custom-call(f32[1,3072]{1,0:T(1,128)} %fusion.54.refs_0_, bf16[1024,768]{1,0:T(8,128)(2,1)} %copy-done.20, bf16[1024,768]{1,0:T(8,128)(2,1)} %copy-done.21, bf16[1024,1152]{1,0:T(8,128)(2,1)} %copy-done.22, bf16[1024,384]{1,0:T(8,128)(2,1)} %copy-done.19, ...), custom_call_target="tpu_custom_call" | custom-call | flops 6442450944 | bytes 20971520 | tf_op jit(solution)/shard_map/pallas_call | solution.py:116
  264.4 3.4 %convert_add_fusion = f32[512,1024]{1,0:T(8,128)} fusion(f32[512,1024]{1,0:T(8,128)} %get-tuple-element.67, bf16[512,1024]{1,0:T(8,128)(2,1)S(1)} %collective-permute-done.51), kind=kLoop, calls=%fused_computation.17 | loop fusion | flops 1048576 | bytes 5242880 | tf_op jit(solution)/shard_map/add | solution.py:307
  (195 shorter events, 64.5 us)
Async XLA Ops:
  0.6 72.0 %all-to-all-start = ((bf16[32,344,128]{2,1,0:T(8,128)(2,1)}), bf16[32,344,128]{2,1,0:T(8,128)(2,1)}, u32[]{:S(2)}, u32[]{:S(2)}) async-start(bf16[32,344,128]{2,1,0:T(8,128)(2,1)} %bitcast.131), calls=%async_computation | async-start | bytes 5636096 | tf_op jit(solution)/shard_map/all_to_all | solution.py:217
  8.1 23.0 %collective-permute-start = (bf16[512,1024]{1,0:T(8,128)(2,1)}, bf16[512,1024]{1,0:T(8,128)(2,1)}, u32[]{:S(2)}, u32[]{:S(2)}) collective-permute-start(bf16[512,1024]{1,0:T(8,128)(2,1)} %param.12), channel_id=1, source_target_pairs={{0,1},{1,0},{2,3},{3,2},{4,5},{5,4},{6,7},{7,6},{8,9},{9,8},{10,11... | collective-permute-start | bytes 3145736 | tf_op jit(solution)/shard_map/ppermute | solution.py:174
  18.3 56.7 %collective-permute-start.1 = (bf16[4,2,176,344]{3,2,1,0:T(8,128)(2,1)}, bf16[4,2,176,344]{3,2,1,0:T(8,128)(2,1)}, u32[]{:S(2)}, u32[]{:S(2)}) collective-permute-start(bf16[4,2,176,344]{3,2,1,0:T(8,128)(2,1)} %bitcast.10), channel_id=1, source_target_pairs={{0,2},{1,3},{2,0},{3,1},{4,6},{5,7},{6,4},{7,5},{8,10},{9,11},{10,... | collective-permute-start | bytes 2906120 | tf_op jit(solution)/shard_map/ppermute | solution.py:174
  19.9 55.0 %collective-permute-start.2 = (bf16[4,2,176,344]{3,2,1,0:T(8,128)(2,1)}, bf16[4,2,176,344]{3,2,1,0:T(8,128)(2,1)}, u32[]{:S(2)}, u32[]{:S(2)}) collective-permute-start(bf16[4,2,176,344]{3,2,1,0:T(8,128)(2,1)} %bitcast.11), channel_id=1, source_target_pairs={{0,4},{1,5},{2,6},{3,7},{4,0},{5,1},{6,2},{7,3},{8,12},{9,13},{10,... | collective-permute-start | bytes 2906120 | tf_op jit(solution)/shard_map/ppermute | solution.py:174
  85.4 10.0 %collective-permute-start.19 = (bf16[344,512]{1,0:T(8,128)(2,1)}, bf16[344,512]{1,0:T(8,128)(2,1)}, u32[]{:S(2)}, u32[]{:S(2)}) collective-permute-start(bf16[344,512]{1,0:T(8,128)(2,1)} %fusion.30), channel_id=1, source_target_pairs={{0,8},{1,9},{2,10},{3,11},{4,12},{5,13},{6,14},{7,15},{8,16},{9,17... | collective-permute-start | bytes 1056776 | tf_op jit(solution)/shard_map/ppermute | solution.py:177
  87.5 27.4 %collective-permute-start.3 = (bf16[4,2,176,344]{3,2,1,0:T(8,128)(2,1)}, bf16[4,2,176,344]{3,2,1,0:T(8,128)(2,1)}, u32[]{:S(2)}, u32[]{:S(2)}) collective-permute-start(bf16[4,2,176,344]{3,2,1,0:T(8,128)(2,1)} %bitcast.8), channel_id=1, source_target_pairs={{0,6},{1,7},{2,4},{3,5},{4,2},{5,3},{6,0},{7,1},{8,14},{9,15},{10,... | collective-permute-start | bytes 2906120 | tf_op jit(solution)/shard_map/ppermute | solution.py:174
  89.5 12.4 %collective-permute-start.18 = (bf16[344,512]{1,0:T(8,128)(2,1)}, bf16[344,512]{1,0:T(8,128)(2,1)}, u32[]{:S(2)}, u32[]{:S(2)}) collective-permute-start(bf16[344,512]{1,0:T(8,128)(2,1)} %fusion.30), channel_id=1, source_target_pairs={{8,0},{9,1},{10,2},{11,3},{12,4},{13,5},{14,6},{15,7},{16,8},{17,9... | collective-permute-start | bytes 1056776 | tf_op jit(solution)/shard_map/ppermute | solution.py:180
  90.8 13.9 %collective-permute-start.17 = (bf16[344,512]{1,0:T(8,128)(2,1)}, bf16[344,512]{1,0:T(8,128)(2,1)}, u32[]{:S(2)}, u32[]{:S(2)}) collective-permute-start(bf16[344,512]{1,0:T(8,128)(2,1)} %fusion.30), channel_id=1, source_target_pairs={{0,1},{1,0},{2,3},{3,2},{4,5},{5,4},{6,7},{7,6},{8,9},{9,8},{10,11... | collective-permute-start | bytes 1056776 | tf_op jit(solution)/shard_map/ppermute | solution.py:174
  90.9 15.2 %collective-permute-start.6 = (bf16[344,512]{1,0:T(8,128)(2,1)}, bf16[344,512]{1,0:T(8,128)(2,1)S(1)}, u32[]{:S(2)}, u32[]{:S(2)}) collective-permute-start(bf16[344,512]{1,0:T(8,128)(2,1)} %fusion.33), channel_id=1, source_target_pairs={{0,8},{1,9},{2,10},{3,11},{4,12},{5,13},{6,14},{7,15},{8,16},{9,17... | collective-permute-start | bytes 1056776 | tf_op jit(solution)/shard_map/ppermute | solution.py:177
  95.5 15.2 %collective-permute-start.5 = (bf16[344,512]{1,0:T(8,128)(2,1)}, bf16[344,512]{1,0:T(8,128)(2,1)}, u32[]{:S(2)}, u32[]{:S(2)}) collective-permute-start(bf16[344,512]{1,0:T(8,128)(2,1)} %fusion.33), channel_id=1, source_target_pairs={{8,0},{9,1},{10,2},{11,3},{12,4},{13,5},{14,6},{15,7},{16,8},{17,9... | collective-permute-start | bytes 1056776 | tf_op jit(solution)/shard_map/ppermute | solution.py:180
  101.9 14.5 %collective-permute-start.22 = (bf16[344,512]{1,0:T(8,128)(2,1)}, bf16[344,512]{1,0:T(8,128)(2,1)S(1)}, u32[]{:S(2)}, u32[]{:S(2)}) collective-permute-start(bf16[344,512]{1,0:T(8,128)(2,1)} %collective-permute-done.19), channel_id=1, source_target_pairs={{0,8},{1,9},{2,10},{3,11},{4,12},{5,13},{6,14},{7,15},{8,16},{9,17... | collective-permute-start | bytes 1056776 | tf_op jit(solution)/shard_map/ppermute | solution.py:177
  104.7 16.2 %collective-permute-start.21 = (bf16[344,512]{1,0:T(8,128)(2,1)}, bf16[344,512]{1,0:T(8,128)(2,1)S(1)}, u32[]{:S(2)}, u32[]{:S(2)}) collective-permute-start(bf16[344,512]{1,0:T(8,128)(2,1)} %collective-permute-done.18), channel_id=1, source_target_pairs={{8,0},{9,1},{10,2},{11,3},{12,4},{13,5},{14,6},{15,7},{16,8},{17,9... | collective-permute-start | bytes 1056776 | tf_op jit(solution)/shard_map/ppermute | solution.py:180
  106.0 16.2 %collective-permute-start.9 = (bf16[344,512]{1,0:T(8,128)(2,1)S(1)}, bf16[344,512]{1,0:T(8,128)(2,1)S(1)}, u32[]{:S(2)}, u32[]{:S(2)}) collective-permute-start(bf16[344,512]{1,0:T(8,128)(2,1)S(1)} %collective-permute-done.6), channel_id=1, source_target_pairs={{0,8},{1,9},{2,10},{3,11},{4,12},{5,13},{6,14},{7,15},{8,16},{9,17... | collective-permute-start | bytes 1056776 | tf_op jit(solution)/shard_map/ppermute | solution.py:177
  110.6 16.2 %collective-permute-start.8 = (bf16[344,512]{1,0:T(8,128)(2,1)}, bf16[344,512]{1,0:T(8,128)(2,1)S(1)}, u32[]{:S(2)}, u32[]{:S(2)}) collective-permute-start(bf16[344,512]{1,0:T(8,128)(2,1)} %collective-permute-done.5), channel_id=1, source_target_pairs={{8,0},{9,1},{10,2},{11,3},{12,4},{13,5},{14,6},{15,7},{16,8},{17,9... | collective-permute-start | bytes 1056776 | tf_op jit(solution)/shard_map/ppermute | solution.py:180
  114.9 15.0 %collective-permute-start.4 = (bf16[344,512]{1,0:T(8,128)(2,1)}, bf16[344,512]{1,0:T(8,128)(2,1)S(1)}, u32[]{:S(2)}, u32[]{:S(2)}) collective-permute-start(bf16[344,512]{1,0:T(8,128)(2,1)} %fusion.33), channel_id=1, source_target_pairs={{0,1},{1,0},{2,3},{3,2},{4,5},{5,4},{6,7},{7,6},{8,9},{9,8},{10,11... | collective-permute-start | bytes 1056776 | tf_op jit(solution)/shard_map/ppermute | solution.py:174
  116.4 14.0 %collective-permute-start.25 = (bf16[344,512]{1,0:T(8,128)(2,1)S(1)}, bf16[344,512]{1,0:T(8,128)(2,1)S(1)}, u32[]{:S(2)}, u32[]{:S(2)}) collective-permute-start(bf16[344,512]{1,0:T(8,128)(2,1)S(1)} %collective-permute-done.22), channel_id=1, source_target_pairs={{0,8},{1,9},{2,10},{3,11},{4,12},{5,13},{6,14},{7,15},{8,16},{9,17... | collective-permute-start | bytes 1056776 | tf_op jit(solution)/shard_map/ppermute | solution.py:177
  121.0 13.0 %collective-permute-start.24 = (bf16[344,512]{1,0:T(8,128)(2,1)S(1)}, bf16[344,512]{1,0:T(8,128)(2,1)S(1)}, u32[]{:S(2)}, u32[]{:S(2)}) collective-permute-start(bf16[344,512]{1,0:T(8,128)(2,1)S(1)} %collective-permute-done.21), channel_id=1, source_target_pairs={{8,0},{9,1},{10,2},{11,3},{12,4},{13,5},{14,6},{15,7},{16,8},{17,9... | collective-permute-start | bytes 1056776 | tf_op jit(solution)/shard_map/ppermute | solution.py:180
  122.3 14.3 %collective-permute-start.12 = (bf16[344,512]{1,0:T(8,128)(2,1)S(1)}, bf16[344,512]{1,0:T(8,128)(2,1)S(1)}, u32[]{:S(2)}, u32[]{:S(2)}) collective-permute-start(bf16[344,512]{1,0:T(8,128)(2,1)S(1)} %collective-permute-done.9), channel_id=1, source_target_pairs={{0,8},{1,9},{2,10},{3,11},{4,12},{5,13},{6,14},{7,15},{8,16},{9,17... | collective-permute-start | bytes 1056776 | tf_op jit(solution)/shard_map/ppermute | solution.py:177
  126.9 13.9 %collective-permute-start.11 = (bf16[344,512]{1,0:T(8,128)(2,1)S(1)}, bf16[344,512]{1,0:T(8,128)(2,1)S(1)}, u32[]{:S(2)}, u32[]{:S(2)}) collective-permute-start(bf16[344,512]{1,0:T(8,128)(2,1)S(1)} %collective-permute-done.8), channel_id=1, source_target_pairs={{8,0},{9,1},{10,2},{11,3},{12,4},{13,5},{14,6},{15,7},{16,8},{17,9... | collective-permute-start | bytes 1056776 | tf_op jit(solution)/shard_map/ppermute | solution.py:180
  135.2 10.1 %collective-permute-start.23 = (bf16[344,512]{1,0:T(8,128)(2,1)S(1)}, bf16[344,512]{1,0:T(8,128)(2,1)S(1)}, u32[]{:S(2)}, u32[]{:S(2)}) collective-permute-start(bf16[344,512]{1,0:T(8,128)(2,1)S(1)} %get-tuple-element.86), channel_id=1, source_target_pairs={{0,1},{1,0},{2,3},{3,2},{4,5},{5,4},{6,7},{7,6},{8,9},{9,8},{10,11... | collective-permute-start | bytes 1056776 | tf_op jit(solution)/shard_map/ppermute | solution.py:174
  135.3 11.1 %collective-permute-start.26 = (bf16[344,512]{1,0:T(8,128)(2,1)S(1)}, bf16[344,512]{1,0:T(8,128)(2,1)S(1)}, u32[]{:S(2)}, u32[]{:S(2)}) collective-permute-start(bf16[344,512]{1,0:T(8,128)(2,1)S(1)} %get-tuple-element.87), channel_id=1, source_target_pairs={{0,1},{1,0},{2,3},{3,2},{4,5},{5,4},{6,7},{7,6},{8,9},{9,8},{10,11... | collective-permute-start | bytes 1056776 | tf_op jit(solution)/shard_map/ppermute | solution.py:174
  135.8 7.3 %collective-permute-start.20 = (bf16[344,512]{1,0:T(8,128)(2,1)S(1)}, bf16[344,512]{1,0:T(8,128)(2,1)S(1)}, u32[]{:S(2)}, u32[]{:S(2)}) collective-permute-start(bf16[344,512]{1,0:T(8,128)(2,1)S(1)} %get-tuple-element.89), channel_id=1, source_target_pairs={{0,1},{1,0},{2,3},{3,2},{4,5},{5,4},{6,7},{7,6},{8,9},{9,8},{10,11... | collective-permute-start | bytes 1056776 | tf_op jit(solution)/shard_map/ppermute | solution.py:174
  142.0 11.2 %collective-permute-start.10 = (bf16[344,512]{1,0:T(8,128)(2,1)S(1)}, bf16[344,512]{1,0:T(8,128)(2,1)S(1)}, u32[]{:S(2)}, u32[]{:S(2)}) collective-permute-start(bf16[344,512]{1,0:T(8,128)(2,1)S(1)} %get-tuple-element.84), channel_id=1, source_target_pairs={{0,1},{1,0},{2,3},{3,2},{4,5},{5,4},{6,7},{7,6},{8,9},{9,8},{10,11... | collective-permute-start | bytes 1056776 | tf_op jit(solution)/shard_map/ppermute | solution.py:174
  142.0 7.2 %collective-permute-start.7 = (bf16[344,512]{1,0:T(8,128)(2,1)S(1)}, bf16[344,512]{1,0:T(8,128)(2,1)S(1)}, u32[]{:S(2)}, u32[]{:S(2)}) collective-permute-start(bf16[344,512]{1,0:T(8,128)(2,1)S(1)} %get-tuple-element.88), channel_id=1, source_target_pairs={{0,1},{1,0},{2,3},{3,2},{4,5},{5,4},{6,7},{7,6},{8,9},{9,8},{10,11... | collective-permute-start | bytes 1056776 | tf_op jit(solution)/shard_map/ppermute | solution.py:174
  143.1 11.2 %collective-permute-start.13 = (bf16[344,512]{1,0:T(8,128)(2,1)S(1)}, bf16[344,512]{1,0:T(8,128)(2,1)S(1)}, u32[]{:S(2)}, u32[]{:S(2)}) collective-permute-start(bf16[344,512]{1,0:T(8,128)(2,1)S(1)} %get-tuple-element.85), channel_id=1, source_target_pairs={{0,1},{1,0},{2,3},{3,2},{4,5},{5,4},{6,7},{7,6},{8,9},{9,8},{10,11... | collective-permute-start | bytes 1056776 | tf_op jit(solution)/shard_map/ppermute | solution.py:174
  147.5 9.6 %collective-permute-start.27 = (bf16[176,512]{1,0:T(8,128)(2,1)S(1)}, bf16[176,512]{1,0:T(8,128)(2,1)S(1)}, u32[]{:S(2)}, u32[]{:S(2)}) collective-permute-start(bf16[176,512]{1,0:T(8,128)(2,1)S(1)} %get-tuple-element.81), channel_id=1, source_target_pairs={{0,2},{1,3},{2,0},{3,1},{4,6},{5,7},{6,4},{7,5},{8,10},{9,11},{10,... | collective-permute-start | bytes 540680 | tf_op jit(solution)/shard_map/ppermute | solution.py:174
  147.6 11.4 %collective-permute-start.29 = (bf16[176,512]{1,0:T(8,128)(2,1)S(1)}, bf16[176,512]{1,0:T(8,128)(2,1)S(1)}, u32[]{:S(2)}, u32[]{:S(2)}) collective-permute-start(bf16[176,512]{1,0:T(8,128)(2,1)S(1)} %get-tuple-element.82), channel_id=1, source_target_pairs={{0,6},{1,7},{2,4},{3,5},{4,2},{5,3},{6,0},{7,1},{8,14},{9,15},{10,... | collective-permute-start | bytes 540680 | tf_op jit(solution)/shard_map/ppermute | solution.py:174
  149.2 10.9 %collective-permute-start.28 = (bf16[176,512]{1,0:T(8,128)(2,1)S(1)}, bf16[176,512]{1,0:T(8,128)(2,1)S(1)}, u32[]{:S(2)}, u32[]{:S(2)}) collective-permute-start(bf16[176,512]{1,0:T(8,128)(2,1)S(1)} %get-tuple-element.83), channel_id=1, source_target_pairs={{0,4},{1,5},{2,6},{3,7},{4,0},{5,1},{6,2},{7,3},{8,12},{9,13},{10,... | collective-permute-start | bytes 540680 | tf_op jit(solution)/shard_map/ppermute | solution.py:174
  155.4 7.6 %collective-permute-start.14 = (bf16[176,512]{1,0:T(8,128)(2,1)S(1)}, bf16[176,512]{1,0:T(8,128)(2,1)S(1)}, u32[]{:S(2)}, u32[]{:S(2)}) collective-permute-start(bf16[176,512]{1,0:T(8,128)(2,1)S(1)} %get-tuple-element.78), channel_id=1, source_target_pairs={{0,2},{1,3},{2,0},{3,1},{4,6},{5,7},{6,4},{7,5},{8,10},{9,11},{10,... | collective-permute-start | bytes 540680 | tf_op jit(solution)/shard_map/ppermute | solution.py:174
  155.6 10.2 %collective-permute-start.16 = (bf16[176,512]{1,0:T(8,128)(2,1)S(1)}, bf16[176,512]{1,0:T(8,128)(2,1)S(1)}, u32[]{:S(2)}, u32[]{:S(2)}) collective-permute-start(bf16[176,512]{1,0:T(8,128)(2,1)S(1)} %get-tuple-element.79), channel_id=1, source_target_pairs={{0,6},{1,7},{2,4},{3,5},{4,2},{5,3},{6,0},{7,1},{8,14},{9,15},{10,... | collective-permute-start | bytes 540680 | tf_op jit(solution)/shard_map/ppermute | solution.py:174
  157.1 10.1 %collective-permute-start.15 = (bf16[176,512]{1,0:T(8,128)(2,1)S(1)}, bf16[176,512]{1,0:T(8,128)(2,1)S(1)}, u32[]{:S(2)}, u32[]{:S(2)}) collective-permute-start(bf16[176,512]{1,0:T(8,128)(2,1)S(1)} %get-tuple-element.80), channel_id=1, source_target_pairs={{0,4},{1,5},{2,6},{3,7},{4,0},{5,1},{6,2},{7,3},{8,12},{9,13},{10,... | collective-permute-start | bytes 540680 | tf_op jit(solution)/shard_map/ppermute | solution.py:174
  167.8 9.4 %collective-permute-start.33 = (bf16[176,1024]{1,0:T(8,128)(2,1)S(1)}, bf16[176,1024]{1,0:T(8,128)(2,1)S(1)}, u32[]{:S(2)}, u32[]{:S(2)}) collective-permute-start(bf16[176,1024]{1,0:T(8,128)(2,1)S(1)} %multiply_convert_fusion.refs_1_.refs_5_), channel_id=1, source_target_pairs={{0,8},{1,9},{2,10},{3,11},{4,12},{5,13},{6,14},{7,15},{8,0},{9,1},... | collective-permute-start | bytes 1081352 | tf_op jit(solution)/shard_map/ppermute | solution.py:174
  169.5 9.1 %collective-permute-start.30 = (bf16[176,1024]{1,0:T(8,128)(2,1)S(1)}, bf16[176,1024]{1,0:T(8,128)(2,1)S(1)}, u32[]{:S(2)}, u32[]{:S(2)}) collective-permute-start(bf16[176,1024]{1,0:T(8,128)(2,1)S(1)} %multiply_convert_fusion.refs_1_.refs_5_), channel_id=1, source_target_pairs={{0,2},{1,3},{2,0},{3,1},{4,6},{5,7},{6,4},{7,5},{8,10},{9,11},{10,... | collective-permute-start | bytes 1081352 | tf_op jit(solution)/shard_map/ppermute | solution.py:174
  170.5 12.8 %collective-permute-start.31 = (bf16[176,1024]{1,0:T(8,128)(2,1)S(1)}, bf16[176,1024]{1,0:T(8,128)(2,1)S(1)}, u32[]{:S(2)}, u32[]{:S(2)}) collective-permute-start(bf16[176,1024]{1,0:T(8,128)(2,1)S(1)} %multiply_convert_fusion.refs_1_.refs_5_), channel_id=1, source_target_pairs={{0,4},{1,5},{2,6},{3,7},{4,0},{5,1},{6,2},{7,3},{8,12},{9,13},{10,... | collective-permute-start | bytes 1081352 | tf_op jit(solution)/shard_map/ppermute | solution.py:174
  177.2 11.4 %collective-permute-start.35 = (bf16[176,1024]{1,0:T(8,128)(2,1)S(1)}, bf16[176,1024]{1,0:T(8,128)(2,1)S(1)}, u32[]{:S(2)}, u32[]{:S(2)}) collective-permute-start(bf16[176,1024]{1,0:T(8,128)(2,1)S(1)} %collective-permute-done.33.refs_1_.refs_9_), channel_id=1, source_target_pairs={{0,4},{1,5},{2,6},{3,7},{4,0},{5,1},{6,2},{7,3},{8,12},{9,13},{10,... | collective-permute-start | bytes 1081352 | tf_op jit(solution)/shard_map/ppermute | solution.py:174
  178.6 15.5 %collective-permute-start.32 = (bf16[176,1024]{1,0:T(8,128)(2,1)S(1)}, bf16[176,1024]{1,0:T(8,128)(2,1)S(1)}, u32[]{:S(2)}, u32[]{:S(2)}) collective-permute-start(bf16[176,1024]{1,0:T(8,128)(2,1)S(1)} %collective-permute-done.30.refs_2_.refs_6_), channel_id=1, source_target_pairs={{0,4},{1,5},{2,6},{3,7},{4,0},{5,1},{6,2},{7,3},{8,12},{9,13},{10,... | collective-permute-start | bytes 1081352 | tf_op jit(solution)/shard_map/ppermute | solution.py:174
  179.3 25.6 %collective-permute-start.37 = (bf16[176,1024]{1,0:T(8,128)(2,1)S(1)}, bf16[176,1024]{1,0:T(8,128)(2,1)S(1)}, u32[]{:S(2)}, u32[]{:S(2)}) collective-permute-start(bf16[176,1024]{1,0:T(8,128)(2,1)S(1)} %multiply_convert_fusion.refs_1_.refs_5_), channel_id=1, source_target_pairs={{0,16},{1,17},{2,18},{3,19},{4,20},{5,21},{6,22},{7,23},{8,24},{9,... | collective-permute-start | bytes 1081352 | tf_op jit(solution)/shard_map/ppermute | solution.py:174
  180.6 26.2 %collective-permute-start.40 = (bf16[176,1024]{1,0:T(8,128)(2,1)S(1)}, bf16[176,1024]{1,0:T(8,128)(2,1)S(1)}, u32[]{:S(2)}, u32[]{:S(2)}) collective-permute-start(bf16[176,1024]{1,0:T(8,128)(2,1)S(1)} %multiply_convert_fusion.refs_1_.refs_5_), channel_id=1, source_target_pairs={{0,24},{1,25},{2,26},{3,27},{4,28},{5,29},{6,30},{7,31},{8,16},{9,... | collective-permute-start | bytes 1081352 | tf_op jit(solution)/shard_map/ppermute | solution.py:174
  183.3 23.8 %collective-permute-start.34 = (bf16[176,1024]{1,0:T(8,128)(2,1)S(1)}, bf16[176,1024]{1,0:T(8,128)(2,1)S(1)}, u32[]{:S(2)}, u32[]{:S(2)}) collective-permute-start(bf16[176,1024]{1,0:T(8,128)(2,1)S(1)} %collective-permute-done.33.refs_1_.refs_9_), channel_id=1, source_target_pairs={{0,2},{1,3},{2,0},{3,1},{4,6},{5,7},{6,4},{7,5},{8,10},{9,11},{10,... | collective-permute-start | bytes 1081352 | tf_op jit(solution)/shard_map/ppermute | solution.py:174
  188.5 20.4 %collective-permute-start.36 = (bf16[176,1024]{1,0:T(8,128)(2,1)S(1)}, bf16[176,1024]{1,0:T(8,128)(2,1)S(1)}, u32[]{:S(2)}, u32[]{:S(2)}) collective-permute-start(bf16[176,1024]{1,0:T(8,128)(2,1)S(1)} %collective-permute-done.35.refs_3_.refs_11_), channel_id=1, source_target_pairs={{0,2},{1,3},{2,0},{3,1},{4,6},{5,7},{6,4},{7,5},{8,10},{9,11},{10,... | collective-permute-start | bytes 1081352 | tf_op jit(solution)/shard_map/ppermute | solution.py:174
  204.8 18.4 %collective-permute-start.39 = (bf16[176,1024]{1,0:T(8,128)(2,1)S(1)}, bf16[176,1024]{1,0:T(8,128)(2,1)S(1)}, u32[]{:S(2)}, u32[]{:S(2)}) collective-permute-start(bf16[176,1024]{1,0:T(8,128)(2,1)S(1)} %collective-permute-done.37.refs_1_.refs_13_), channel_id=1, source_target_pairs={{0,4},{1,5},{2,6},{3,7},{4,0},{5,1},{6,2},{7,3},{8,12},{9,13},{10,... | collective-permute-start | bytes 1081352 | tf_op jit(solution)/shard_map/ppermute | solution.py:174
  205.1 16.1 %collective-permute-start.38 = (bf16[176,1024]{1,0:T(8,128)(2,1)S(1)}, bf16[176,1024]{1,0:T(8,128)(2,1)S(1)}, u32[]{:S(2)}, u32[]{:S(2)}) collective-permute-start(bf16[176,1024]{1,0:T(8,128)(2,1)S(1)} %collective-permute-done.37.refs_1_.refs_13_), channel_id=1, source_target_pairs={{0,2},{1,3},{2,0},{3,1},{4,6},{5,7},{6,4},{7,5},{8,10},{9,11},{10,... | collective-permute-start | bytes 1081352 | tf_op jit(solution)/shard_map/ppermute | solution.py:174
  206.8 14.4 %collective-permute-start.42 = (bf16[176,1024]{1,0:T(8,128)(2,1)S(1)}, bf16[176,1024]{1,0:T(8,128)(2,1)S(1)}, u32[]{:S(2)}, u32[]{:S(2)}) collective-permute-start(bf16[176,1024]{1,0:T(8,128)(2,1)S(1)} %collective-permute-done.40.refs_4_.refs_16_), channel_id=1, source_target_pairs={{0,4},{1,5},{2,6},{3,7},{4,0},{5,1},{6,2},{7,3},{8,12},{9,13},{10,... | collective-permute-start | bytes 1081352 | tf_op jit(solution)/shard_map/ppermute | solution.py:174
  207.1 16.1 %collective-permute-start.41 = (bf16[176,1024]{1,0:T(8,128)(2,1)S(1)}, bf16[176,1024]{1,0:T(8,128)(2,1)S(1)}, u32[]{:S(2)}, u32[]{:S(2)}) collective-permute-start(bf16[176,1024]{1,0:T(8,128)(2,1)S(1)} %collective-permute-done.40.refs_4_.refs_16_), channel_id=1, source_target_pairs={{0,2},{1,3},{2,0},{3,1},{4,6},{5,7},{6,4},{7,5},{8,10},{9,11},{10,... | collective-permute-start | bytes 1081352 | tf_op jit(solution)/shard_map/ppermute | solution.py:174
  221.2 9.3 %collective-permute-start.43 = (bf16[176,1024]{1,0:T(8,128)(2,1)S(1)}, bf16[176,1024]{1,0:T(8,128)(2,1)S(1)}, u32[]{:S(2)}, u32[]{:S(2)}) collective-permute-start(bf16[176,1024]{1,0:T(8,128)(2,1)S(1)} %collective-permute-done.38.refs_2_.refs_14_), channel_id=1, source_target_pairs={{0,4},{1,5},{2,6},{3,7},{4,0},{5,1},{6,2},{7,3},{8,12},{9,13},{10,... | collective-permute-start | bytes 1081352 | tf_op jit(solution)/shard_map/ppermute | solution.py:174
  223.0 8.9 %collective-permute-start.44 = (bf16[176,1024]{1,0:T(8,128)(2,1)S(1)}, bf16[176,1024]{1,0:T(8,128)(2,1)S(1)}, u32[]{:S(2)}, u32[]{:S(2)}) collective-permute-start(bf16[176,1024]{1,0:T(8,128)(2,1)S(1)} %collective-permute-done.42.refs_6_.refs_18_), channel_id=1, source_target_pairs={{0,2},{1,3},{2,0},{3,1},{4,6},{5,7},{6,4},{7,5},{8,10},{9,11},{10,... | collective-permute-start | bytes 1081352 | tf_op jit(solution)/shard_map/ppermute | solution.py:174
  240.4 4.7 %collective-permute-start.49 = (f32[4,4,176]{2,1,0:T(4,128)S(1)}, f32[4,4,176]{2,1,0:T(4,128)S(1)}, u32[]{:S(2)}, u32[]{:S(2)}) collective-permute-start(f32[4,4,176]{2,1,0:T(4,128)S(1)} %log_add_fusion.1), channel_id=1, source_target_pairs={{0,16},{1,17},{2,18},{3,19},{4,20},{5,21},{6,22},{7,23},{8,24},{9,... | collective-permute-start | bytes 33800 | tf_op jit(solution)/shard_map/ppermute | solution.py:174
  241.0 5.5 %collective-permute-start.50 = (f32[4,4,176]{2,1,0:T(4,128)S(1)}, f32[4,4,176]{2,1,0:T(4,128)S(1)}, u32[]{:S(2)}, u32[]{:S(2)}) collective-permute-start(f32[4,4,176]{2,1,0:T(4,128)S(1)} %log_add_fusion.1), channel_id=1, source_target_pairs={{0,24},{1,25},{2,26},{3,27},{4,28},{5,29},{6,30},{7,31},{8,16},{9,... | collective-permute-start | bytes 33800 | tf_op jit(solution)/shard_map/ppermute | solution.py:174
  (37 other events, 322.6 us)
where the time goes:
time: 269 us; the launch traced here: 268 us
  waiting for transfers between devices  101 us (38%)
  starting transfers between devices  77.3 us (29%)
  Pallas kernels  26 us (10%)
  matrix products  24.8 us (9%)
  other arithmetic  18.7 us (7%)
  local copies, waits for them, and re-layouts  18.1 us (7%)
    ppermute x41, waiting for transfers between devices, hop(): return lax.ppermute(v, 'dp', [(i, i ^ k) for i in range(n)])  48.6 us
    all_to_all x1, waiting for transfers between devices, body(): down_rows = lax.all_to_all(down_weight, 'dp', 0, 1, tiled=True)  39.9 us
    ppermute x41, starting transfers between devices, hop(): return lax.ppermute(v, 'dp', [(i, i ^ k) for i in range(n)])  38.8 us
    dot_general x21, matrix products, dot(): return jnp.dot(a, b, preferred_element_type=F32)  24.8 us
    ppermute x6, starting transfers between devices, up(): return lax.ppermute(v, 'dp', [(i, i + PLANE) for i in range(n - PLANE)])  23.2 us
    pallas_call x1, Pallas kernels, weigh(): pl.pallas_call(lambda *refs: weigh_kernel(sizes, scale, tiles, *refs), gr...  12.9 us
    ppermute x6, waiting for transfers between devices, down(): return lax.ppermute(v, 'dp', [(i + PLANE, i) for i in range(n - PLANE)])  12.6 us
    pallas_call x4, Pallas kernels, score(): pl.pallas_call(lambda *refs: score_kernel(1.0 / (math.sqrt(width) * 0.05)...  11.1 us
  transfers between devices with their start and end apart: 54, of which 24 were waited for; matrix products, arithmetic and copies ran while one was open for 15% of the time, Pallas kernels for 4%

commit v1 on v0

--- a/solution.py
+++ b/solution.py
@@ -196,7 +196,7 @@
             if ties:
                 below, above, *_ = lax.optimization_barrier((below, above, *ties))
             moved[s, 0], moved[s, 1] = up(below), down(above)
-            block = choose(line, [moved[table[z][s - 1][:2]] for z in range(lines)])
+            block = lax.optimization_barrier(choose(line, [moved[table[z][s - 1][:2]] for z in range(lines)]))
         yield block
 
     def body(hidden, residual, down_weight, gain, proj_weight, centroids):
@@ -217,21 +217,19 @@
         down_rows = lax.all_to_all(down_weight, "dp", 0, 1, tiled=True)
         own = gain[:, None] * proj_weight.astype(F32)
         full = lax.all_gather(own, "cent", axis=0, tiled=True)
-        high = lax.reduce_precision(full, 8, 7)
-        low = (full - high).astype(BF16)
-        high = high.astype(BF16)
+        full = full.astype(BF16)
         direct = dot(residual, own.astype(BF16))
         pair = jnp.concatenate([centroids, hop(centroids, 1)])
         last = blocks[QUAD - 1]
-        down_rows, high, low, direct, pair, last, *units = lax.optimization_barrier(
-            (down_rows, high, low, direct, pair, last, *units)
+        down_rows, full, direct, pair, last, *units = lax.optimization_barrier(
+            (down_rows, full, direct, pair, last, *units)
         )
 
         halves = [slice(0, width // 2), slice(width // 2, width)]
         folds = []
         for h in halves:
             source = after(down_rows, folds[0]) if folds else down_rows
-            folds.append((dot(source, high[:, h]) + dot(source, low[:, h])).astype(BF16))
+            folds.append(dot(source, full[:, h]).astype(BF16))
             if not units[QUAD - 1 :]:
                 last, folds[0] = lax.optimization_barrier((last, folds[0]))
                 units.append(hop(last, 2 * (QUAD - 1)))

time: 269 us -> 265 us (0.985)
  waiting for transfers between devices: 101 us -> 97 us
    all_to_all x1, waiting for transfers between devices: 39.9 us -> 35.4 us  [body(): down_rows = lax.all_to_all(down_weight, 'dp', 0, 1, tiled=True)]
    dot_general x21 -> x19, matrix products: 24.8 us -> 24.7 us  [dot(): return jnp.dot(a, b, preferred_element_type=F32)]
    unnamed x65 -> x67, local copies, waits for them, and re-layouts: 9.9 us -> 9.9 us
  transfers between devices with their start and end apart: 54 -> 54, of which waited for: 24 -> 24; matrix products, arithmetic and copies ran while one was open for 15% -> 17% of each run, Pallas kernels for 4% -> 4%
where the time goes in v1:
time: 265 us; the launch traced here: 264 us
  waiting for transfers between devices  97 us (37%)
  starting transfers between devices  77.1 us (29%)
  Pallas kernels  25.9 us (10%)
  matrix products  24.7 us (9%)
  other arithmetic  19.8 us (7%)
  local copies, waits for them, and re-layouts  18.4 us (7%)
    ppermute x41, waiting for transfers between devices, hop(): return lax.ppermute(v, 'dp', [(i, i ^ k) for i in range(n)])  48.7 us
    ppermute x41, starting transfers between devices, hop(): return lax.ppermute(v, 'dp', [(i, i ^ k) for i in range(n)])  38.6 us
    all_to_all x1, waiting for transfers between devices, body(): down_rows = lax.all_to_all(down_weight, 'dp', 0, 1, tiled=True)  35.4 us
    dot_general x19, matrix products, dot(): return jnp.dot(a, b, preferred_element_type=F32)  24.7 us
    ppermute x6, starting transfers between devices, up(): return lax.ppermute(v, 'dp', [(i, i + PLANE) for i in range(n - PLANE)])  23.2 us
    pallas_call x1, Pallas kernels, weigh(): pl.pallas_call(lambda *refs: weigh_kernel(sizes, scale, tiles, *refs), gr...  12.8 us
    ppermute x6, waiting for transfers between devices, down(): return lax.ppermute(v, 'dp', [(i + PLANE, i) for i in range(n - PLANE)])  12.6 us
    pallas_call x4, Pallas kernels, score(): pl.pallas_call(lambda *refs: score_kernel(1.0 / (math.sqrt(width) * 0.05)...  11.1 us
  transfers between devices with their start and end apart: 54, of which 24 were waited for; matrix products, arithmetic and copies ran while one was open for 17% of the time, Pallas kernels for 4%

profile of v1, /device:TPU:0, one launch (start us, length us, event | category | flops | bytes accessed | tf_op | source)
XLA Modules:
  0.0 264.4 jit_solution(171066592965051607)
XLA Ops:
  0.7 7.4 %all-to-all-start = ((bf16[32,344,128]{2,1,0:T(8,128)(2,1)}), bf16[32,344,128]{2,1,0:T(8,128)(2,1)}, u32[]{:S(2)}, u32[]{:S(2)}) async-start(bf16[32,344,128]{2,1,0:T(8,128)(2,1)} %bitcast.126), calls=%async_computation | async-start | bytes 5636096 | tf_op jit(solution)/shard_map/all_to_all | solution.py:217
  9.7 2.5 fusion.38.position
  12.2 2.1 copy-done.2
  14.3 2.0 shard_map.86
  16.3 2.2 fusion.45
  18.5 1.7 collective-permute-start.1
  21.7 8.2 %multiply_convert_fusion = bf16[4096,1024]{1,0:T(8,128)(2,1)} fusion(bf16[4096,1024]{1,0:T(8,128)(2,1)} %param.11, f32[4096]{0:T(1024)S(1)} %copy-done.29), kind=kLoop, calls=%fused_computation | loop fusion | flops 12582912 | bytes 16793600 | tf_op jit(solution)/shard_map/convert_element_type | solution.py:220
  29.8 6.0 %convolution_bitcast_fusion = f32[176,1024]{1,0:T(8,128)} fusion(bf16[176,4096]{1,0:T(8,128)(2,1)S(1)} %copy-done, bf16[4096,1024]{1,0:T(8,128)(2,1)} %multiply_convert_fusion), kind=kOutput, calls=%fused_computation.22 | convolution fusion | flops 1476395008 | bytes 10551296 | tf_op jit(solution)/shard_map/dot_general | solution.py:18
  37.2 35.4 %all-to-all-done = bf16[32,344,128]{2,1,0:T(8,128)(2,1)} async-done(((bf16[32,344,128]{2,1,0:T(8,128)(2,1)}), bf16[32,344,128]{2,1,0:T(8,128)(2,1)}, u32[]{:S(2)}, u32[]{:S(2)}) %all-to-all-start) | async-done | bytes 2818080 | tf_op jit(solution)/shard_map/all_to_all | solution.py:217
  72.7 2.3 copy_bitcast_fusion
  75.0 4.7 %fusion.12 = bf16[344,512]{1,0:T(8,128)(2,1)} fusion(bf16[344,4096]{1,0:T(8,128)(2,1)S(1)} %copy_bitcast_fusion, bf16[4096,1024]{1,0:T(8,128)(2,1)} %multiply_convert_fusion), kind=kOutput, calls=%fused_computation.23 | convolution fusion | flops 1443016704 | bytes 7364608 | tf_op jit(solution)/shard_map/dot_general | solution.py:18
  79.7 2.4 fusion.15
  82.1 2.0 collective-permute-start.19
  84.1 2.1 collective-permute-start.3
  87.6 4.6 %collective-permute-start.6 = (bf16[344,512]{1,0:T(8,128)(2,1)}, bf16[344,512]{1,0:T(8,128)(2,1)S(1)}, u32[]{:S(2)}, u32[]{:S(2)}) collective-permute-start(bf16[344,512]{1,0:T(8,128)(2,1)} %fusion.12), channel_id=1, source_target_pairs={{0,8},{1,9},{2,10},{3,11},{4,12},{5,13},{6,14},{7,15},{8,16},{9,17... | collective-permute-start | bytes 1056776 | tf_op jit(solution)/shard_map/ppermute | solution.py:177
  93.6 5.0 %collective-permute-done.18 = bf16[344,512]{1,0:T(8,128)(2,1)} collective-permute-done((bf16[344,512]{1,0:T(8,128)(2,1)}, bf16[344,512]{1,0:T(8,128)(2,1)}, u32[]{:S(2)}, u32[]{:S(2)}) %collective-permute-start.18) | collective-permute-done | bytes 352288 | tf_op jit(solution)/shard_map/ppermute | solution.py:180
  98.6 2.8 %collective-permute-start.22 = (bf16[344,512]{1,0:T(8,128)(2,1)}, bf16[344,512]{1,0:T(8,128)(2,1)S(1)}, u32[]{:S(2)}, u32[]{:S(2)}) collective-permute-start(bf16[344,512]{1,0:T(8,128)(2,1)} %collective-permute-done.19), channel_id=1, source_target_pairs={{0,8},{1,9},{2,10},{3,11},{4,12},{5,13},{6,14},{7,15},{8,16},{9,17... | collective-permute-start | bytes 1056776 | tf_op jit(solution)/shard_map/ppermute | solution.py:177
  102.8 4.6 %collective-permute-start.9 = (bf16[344,512]{1,0:T(8,128)(2,1)S(1)}, bf16[344,512]{1,0:T(8,128)(2,1)S(1)}, u32[]{:S(2)}, u32[]{:S(2)}) collective-permute-start(bf16[344,512]{1,0:T(8,128)(2,1)S(1)} %collective-permute-done.6), channel_id=1, source_target_pairs={{0,8},{1,9},{2,10},{3,11},{4,12},{5,13},{6,14},{7,15},{8,16},{9,17... | collective-permute-start | bytes 1056776 | tf_op jit(solution)/shard_map/ppermute | solution.py:177
  113.1 4.6 %collective-permute-start.25 = (bf16[344,512]{1,0:T(8,128)(2,1)S(1)}, bf16[344,512]{1,0:T(8,128)(2,1)S(1)}, u32[]{:S(2)}, u32[]{:S(2)}) collective-permute-start(bf16[344,512]{1,0:T(8,128)(2,1)S(1)} %collective-permute-done.22), channel_id=1, source_target_pairs={{0,8},{1,9},{2,10},{3,11},{4,12},{5,13},{6,14},{7,15},{8,16},{9,17... | collective-permute-start | bytes 1056776 | tf_op jit(solution)/shard_map/ppermute | solution.py:177
  119.0 4.6 %collective-permute-start.12 = (bf16[344,512]{1,0:T(8,128)(2,1)S(1)}, bf16[344,512]{1,0:T(8,128)(2,1)S(1)}, u32[]{:S(2)}, u32[]{:S(2)}) collective-permute-start(bf16[344,512]{1,0:T(8,128)(2,1)S(1)} %collective-permute-done.9), channel_id=1, source_target_pairs={{0,8},{1,9},{2,10},{3,11},{4,12},{5,13},{6,14},{7,15},{8,16},{9,17... | collective-permute-start | bytes 1056776 | tf_op jit(solution)/shard_map/ppermute | solution.py:177
  127.2 3.5 %collective-permute-done.24 = bf16[344,512]{1,0:T(8,128)(2,1)S(1)} collective-permute-done((bf16[344,512]{1,0:T(8,128)(2,1)S(1)}, bf16[344,512]{1,0:T(8,128)(2,1)S(1)}, u32[]{:S(2)}, u32[]{:S(2)}) %collective-permute-start.24) | collective-permute-done | bytes 352288 | tf_op jit(solution)/shard_map/ppermute | solution.py:180
  133.4 4.1 %collective-permute-done.11 = bf16[344,512]{1,0:T(8,128)(2,1)S(1)} collective-permute-done((bf16[344,512]{1,0:T(8,128)(2,1)S(1)}, bf16[344,512]{1,0:T(8,128)(2,1)S(1)}, u32[]{:S(2)}, u32[]{:S(2)}) %collective-permute-start.11) | collective-permute-done | bytes 352288 | tf_op jit(solution)/shard_map/ppermute | solution.py:180
  140.4 1.5 fusion.9
  144.3 1.6 collective-permute-start.29
  145.9 1.9 collective-permute-start.28
  148.3 1.6 fusion.5
  153.9 1.9 collective-permute-start.15
  156.7 3.1 %collective-permute-done.14 = bf16[176,512]{1,0:T(8,128)(2,1)S(1)} collective-permute-done((bf16[176,512]{1,0:T(8,128)(2,1)S(1)}, bf16[176,512]{1,0:T(8,128)(2,1)S(1)}, u32[]{:S(2)}, u32[]{:S(2)}) %collective-permute-start.14) | collective-permute-done | bytes 180256 | tf_op jit(solution)/shard_map/ppermute | solution.py:174
  159.8 2.7 %collective-permute-done.16 = bf16[176,512]{1,0:T(8,128)(2,1)S(1)} collective-permute-done((bf16[176,512]{1,0:T(8,128)(2,1)S(1)}, bf16[176,512]{1,0:T(8,128)(2,1)S(1)}, u32[]{:S(2)}, u32[]{:S(2)}) %collective-permute-start.16) | collective-permute-done | bytes 180256 | tf_op jit(solution)/shard_map/ppermute | solution.py:174
  164.4 1.7 collective-permute-start.33
  168.3 5.6 %collective-permute-done.33.refs_1_.refs_9_ = bf16[176,1024]{1,0:T(8,128)(2,1)S(1)} collective-permute-done((bf16[176,1024]{1,0:T(8,128)(2,1)S(1)}, bf16[176,1024]{1,0:T(8,128)(2,1)S(1)}, u32[]{:S(2)}, u32[]{:S(2)}) %collective-permute-start.33) | collective-permute-done | bytes 360480 | tf_op jit(solution)/shard_map/ppermute | solution.py:174
  177.1 2.8 %collective-permute-start.40 = (bf16[176,1024]{1,0:T(8,128)(2,1)S(1)}, bf16[176,1024]{1,0:T(8,128)(2,1)S(1)}, u32[]{:S(2)}, u32[]{:S(2)}) collective-permute-start(bf16[176,1024]{1,0:T(8,128)(2,1)S(1)} %multiply_convert_fusion.1.refs_1_.refs_5_), channel_id=1, source_target_pairs={{0,24},{1,25},{2,26},{3,27},{4,28},{5,29},{6,30},{7,31},{8,16},{9,... | collective-permute-start | bytes 1081352 | tf_op jit(solution)/shard_map/ppermute | solution.py:174
  180.0 5.2 %collective-permute-done.35.refs_3_.refs_11_ = bf16[176,1024]{1,0:T(8,128)(2,1)S(1)} collective-permute-done((bf16[176,1024]{1,0:T(8,128)(2,1)S(1)}, bf16[176,1024]{1,0:T(8,128)(2,1)S(1)}, u32[]{:S(2)}, u32[]{:S(2)}) %collective-permute-start.35) | collective-permute-done | bytes 360480 | tf_op jit(solution)/shard_map/ppermute | solution.py:174
  185.2 1.8 collective-permute-start.36
  187.0 3.8 %collective-permute-done.32.refs_4_.refs_8_ = bf16[176,1024]{1,0:T(8,128)(2,1)S(1)} collective-permute-done((bf16[176,1024]{1,0:T(8,128)(2,1)S(1)}, bf16[176,1024]{1,0:T(8,128)(2,1)S(1)}, u32[]{:S(2)}, u32[]{:S(2)}) %collective-permute-start.32) | collective-permute-done | bytes 360480 | tf_op jit(solution)/shard_map/ppermute | solution.py:174
  190.7 2.6 shard_map.87
  194.6 6.9 %collective-permute-done.37.refs_1_.refs_13_ = bf16[176,1024]{1,0:T(8,128)(2,1)S(1)} collective-permute-done((bf16[176,1024]{1,0:T(8,128)(2,1)S(1)}, bf16[176,1024]{1,0:T(8,128)(2,1)S(1)}, u32[]{:S(2)}, u32[]{:S(2)}) %collective-permute-start.37) | collective-permute-done | bytes 360480 | tf_op jit(solution)/shard_map/ppermute | solution.py:174
  203.6 2.0 collective-permute-start.41
  205.6 2.6 shard_map.88
  209.4 8.4 %collective-permute-done.42.refs_6_.refs_18_ = bf16[176,1024]{1,0:T(8,128)(2,1)S(1)} collective-permute-done((bf16[176,1024]{1,0:T(8,128)(2,1)S(1)}, bf16[176,1024]{1,0:T(8,128)(2,1)S(1)}, u32[]{:S(2)}, u32[]{:S(2)}) %collective-permute-start.42) | collective-permute-done | bytes 360480 | tf_op jit(solution)/shard_map/ppermute | solution.py:174
  217.8 1.8 collective-permute-start.43
  219.7 4.1 %shard_map.89 = (bf16[1024,1152]{1,0:T(8,128)(2,1)S(1)}, f32[1,1152]{1,0:T(1,128)S(1)}, f32[1,1152]{1,0:T(1,128)S(1)}) custom-call(bf16[1024,1024]{1,0:T(8,128)(2,1)S(1)} %pad_maximum_fusion.refs_0_, bf16[176,1024]{1,0:T(8,128)(2,1)S(1)} %collective-permute-done.37.refs_1_.refs_13_, bf16[176,1024]{1,0:T(8,128)(2,1)S(1)} %collective-permute-done.38.refs_2_.refs_14_, ...), custom_call_target="tpu_custom_call" | custom-call | flops 2415919104 | bytes 6815744 | tf_op jit(solution)/shard_map/pallas_call | solution.py:53
  225.4 1.6 collective-permute-done.43.refs_1_.refs_19_
  228.5 1.8 shard_map.90
  233.2 1.7 collective-permute-start.45
  237.4 2.8 %collective-permute-start.50 = (f32[4,4,176]{2,1,0:T(4,128)S(1)}, f32[4,4,176]{2,1,0:T(4,128)S(1)}, u32[]{:S(2)}, u32[]{:S(2)}) collective-permute-start(f32[4,4,176]{2,1,0:T(4,128)S(1)} %log_add_fusion.1), channel_id=1, source_target_pairs={{0,24},{1,25},{2,26},{3,27},{4,28},{5,29},{6,30},{7,31},{8,16},{9,... | collective-permute-start | bytes 33800 | tf_op jit(solution)/shard_map/ppermute | solution.py:174
  244.8 12.8 %shard_map.91 = (f32[512,1024]{1,0:T(8,128)}, bf16[512,1024]{1,0:T(8,128)(2,1)}, f32[1,1024]{1,0:T(1,128)}) custom-call(f32[1,3072]{1,0:T(1,128)} %fusion.36.refs_0_, bf16[1024,768]{1,0:T(8,128)(2,1)} %copy-done.20, bf16[1024,768]{1,0:T(8,128)(2,1)} %copy-done.21, bf16[1024,1152]{1,0:T(8,128)(2,1)} %copy-done.22, bf16[1024,384]{1,0:T(8,128)(2,1)} %copy-done.19, ...), custom_call_target="tpu_custom_call" | custom-call | flops 6442450944 | bytes 20971520 | tf_op jit(solution)/shard_map/pallas_call | solution.py:116
  260.9 3.5 %convert_add_fusion = f32[512,1024]{1,0:T(8,128)} fusion(f32[512,1024]{1,0:T(8,128)} %get-tuple-element.65, bf16[512,1024]{1,0:T(8,128)(2,1)S(1)} %collective-permute-done.51), kind=kLoop, calls=%fused_computation.7 | loop fusion | flops 1048576 | bytes 5242880 | tf_op jit(solution)/shard_map/add | solution.py:305
  (193 shorter events, 60.5 us)
Async XLA Ops:
  0.7 72.0 %all-to-all-start = ((bf16[32,344,128]{2,1,0:T(8,128)(2,1)}), bf16[32,344,128]{2,1,0:T(8,128)(2,1)}, u32[]{:S(2)}, u32[]{:S(2)}) async-start(bf16[32,344,128]{2,1,0:T(8,128)(2,1)} %bitcast.126), calls=%async_computation | async-start | bytes 5636096 | tf_op jit(solution)/shard_map/all_to_all | solution.py:217
  8.1 27.7 %collective-permute-start = (bf16[512,1024]{1,0:T(8,128)(2,1)S(1)}, bf16[512,1024]{1,0:T(8,128)(2,1)}, u32[]{:S(2)}, u32[]{:S(2)}) collective-permute-start(bf16[512,1024]{1,0:T(8,128)(2,1)S(1)} %copy-done.24), channel_id=1, source_target_pairs={{0,1},{1,0},{2,3},{3,2},{4,5},{5,4},{6,7},{7,6},{8,9},{9,8},{10,11... | collective-permute-start | bytes 3145736 | tf_op jit(solution)/shard_map/ppermute | solution.py:174
  18.5 56.4 %collective-permute-start.1 = (bf16[4,2,176,344]{3,2,1,0:T(8,128)(2,1)}, bf16[4,2,176,344]{3,2,1,0:T(8,128)(2,1)}, u32[]{:S(2)}, u32[]{:S(2)}) collective-permute-start(bf16[4,2,176,344]{3,2,1,0:T(8,128)(2,1)} %bitcast.10), channel_id=1, source_target_pairs={{0,2},{1,3},{2,0},{3,1},{4,6},{5,7},{6,4},{7,5},{8,10},{9,11},{10,... | collective-permute-start | bytes 2906120 | tf_op jit(solution)/shard_map/ppermute | solution.py:174
  20.2 54.8 %collective-permute-start.2 = (bf16[4,2,176,344]{3,2,1,0:T(8,128)(2,1)}, bf16[4,2,176,344]{3,2,1,0:T(8,128)(2,1)}, u32[]{:S(2)}, u32[]{:S(2)}) collective-permute-start(bf16[4,2,176,344]{3,2,1,0:T(8,128)(2,1)} %bitcast.11), channel_id=1, source_target_pairs={{0,4},{1,5},{2,6},{3,7},{4,0},{5,1},{6,2},{7,3},{8,12},{9,13},{10,... | collective-permute-start | bytes 2906120 | tf_op jit(solution)/shard_map/ppermute | solution.py:174
  82.1 10.0 %collective-permute-start.19 = (bf16[344,512]{1,0:T(8,128)(2,1)}, bf16[344,512]{1,0:T(8,128)(2,1)}, u32[]{:S(2)}, u32[]{:S(2)}) collective-permute-start(bf16[344,512]{1,0:T(8,128)(2,1)} %fusion.15), channel_id=1, source_target_pairs={{0,8},{1,9},{2,10},{3,11},{4,12},{5,13},{6,14},{7,15},{8,16},{9,17... | collective-permute-start | bytes 1056776 | tf_op jit(solution)/shard_map/ppermute | solution.py:177
  84.1 27.4 %collective-permute-start.3 = (bf16[4,2,176,344]{3,2,1,0:T(8,128)(2,1)}, bf16[4,2,176,344]{3,2,1,0:T(8,128)(2,1)}, u32[]{:S(2)}, u32[]{:S(2)}) collective-permute-start(bf16[4,2,176,344]{3,2,1,0:T(8,128)(2,1)} %bitcast.8), channel_id=1, source_target_pairs={{0,6},{1,7},{2,4},{3,5},{4,2},{5,3},{6,0},{7,1},{8,14},{9,15},{10,... | collective-permute-start | bytes 2906120 | tf_op jit(solution)/shard_map/ppermute | solution.py:174
  86.2 12.4 %collective-permute-start.18 = (bf16[344,512]{1,0:T(8,128)(2,1)}, bf16[344,512]{1,0:T(8,128)(2,1)}, u32[]{:S(2)}, u32[]{:S(2)}) collective-permute-start(bf16[344,512]{1,0:T(8,128)(2,1)} %fusion.15), channel_id=1, source_target_pairs={{8,0},{9,1},{10,2},{11,3},{12,4},{13,5},{14,6},{15,7},{16,8},{17,9... | collective-permute-start | bytes 1056776 | tf_op jit(solution)/shard_map/ppermute | solution.py:180
  87.5 13.9 %collective-permute-start.17 = (bf16[344,512]{1,0:T(8,128)(2,1)}, bf16[344,512]{1,0:T(8,128)(2,1)}, u32[]{:S(2)}, u32[]{:S(2)}) collective-permute-start(bf16[344,512]{1,0:T(8,128)(2,1)} %fusion.15), channel_id=1, source_target_pairs={{0,1},{1,0},{2,3},{3,2},{4,5},{5,4},{6,7},{7,6},{8,9},{9,8},{10,11... | collective-permute-start | bytes 1056776 | tf_op jit(solution)/shard_map/ppermute | solution.py:174
  87.6 15.2 %collective-permute-start.6 = (bf16[344,512]{1,0:T(8,128)(2,1)}, bf16[344,512]{1,0:T(8,128)(2,1)S(1)}, u32[]{:S(2)}, u32[]{:S(2)}) collective-permute-start(bf16[344,512]{1,0:T(8,128)(2,1)} %fusion.12), channel_id=1, source_target_pairs={{0,8},{1,9},{2,10},{3,11},{4,12},{5,13},{6,14},{7,15},{8,16},{9,17... | collective-permute-start | bytes 1056776 | tf_op jit(solution)/shard_map/ppermute | solution.py:177
  92.2 15.2 %collective-permute-start.5 = (bf16[344,512]{1,0:T(8,128)(2,1)}, bf16[344,512]{1,0:T(8,128)(2,1)}, u32[]{:S(2)}, u32[]{:S(2)}) collective-permute-start(bf16[344,512]{1,0:T(8,128)(2,1)} %fusion.12), channel_id=1, source_target_pairs={{8,0},{9,1},{10,2},{11,3},{12,4},{13,5},{14,6},{15,7},{16,8},{17,9... | collective-permute-start | bytes 1056776 | tf_op jit(solution)/shard_map/ppermute | solution.py:180
  98.6 14.5 %collective-permute-start.22 = (bf16[344,512]{1,0:T(8,128)(2,1)}, bf16[344,512]{1,0:T(8,128)(2,1)S(1)}, u32[]{:S(2)}, u32[]{:S(2)}) collective-permute-start(bf16[344,512]{1,0:T(8,128)(2,1)} %collective-permute-done.19), channel_id=1, source_target_pairs={{0,8},{1,9},{2,10},{3,11},{4,12},{5,13},{6,14},{7,15},{8,16},{9,17... | collective-permute-start | bytes 1056776 | tf_op jit(solution)/shard_map/ppermute | solution.py:177
  101.4 16.3 %collective-permute-start.21 = (bf16[344,512]{1,0:T(8,128)(2,1)}, bf16[344,512]{1,0:T(8,128)(2,1)S(1)}, u32[]{:S(2)}, u32[]{:S(2)}) collective-permute-start(bf16[344,512]{1,0:T(8,128)(2,1)} %collective-permute-done.18), channel_id=1, source_target_pairs={{8,0},{9,1},{10,2},{11,3},{12,4},{13,5},{14,6},{15,7},{16,8},{17,9... | collective-permute-start | bytes 1056776 | tf_op jit(solution)/shard_map/ppermute | solution.py:180
  102.8 16.2 %collective-permute-start.9 = (bf16[344,512]{1,0:T(8,128)(2,1)S(1)}, bf16[344,512]{1,0:T(8,128)(2,1)S(1)}, u32[]{:S(2)}, u32[]{:S(2)}) collective-permute-start(bf16[344,512]{1,0:T(8,128)(2,1)S(1)} %collective-permute-done.6), channel_id=1, source_target_pairs={{0,8},{1,9},{2,10},{3,11},{4,12},{5,13},{6,14},{7,15},{8,16},{9,17... | collective-permute-start | bytes 1056776 | tf_op jit(solution)/shard_map/ppermute | solution.py:177
  107.3 16.2 %collective-permute-start.8 = (bf16[344,512]{1,0:T(8,128)(2,1)}, bf16[344,512]{1,0:T(8,128)(2,1)S(1)}, u32[]{:S(2)}, u32[]{:S(2)}) collective-permute-start(bf16[344,512]{1,0:T(8,128)(2,1)} %collective-permute-done.5), channel_id=1, source_target_pairs={{8,0},{9,1},{10,2},{11,3},{12,4},{13,5},{14,6},{15,7},{16,8},{17,9... | collective-permute-start | bytes 1056776 | tf_op jit(solution)/shard_map/ppermute | solution.py:180
  111.6 15.0 %collective-permute-start.4 = (bf16[344,512]{1,0:T(8,128)(2,1)}, bf16[344,512]{1,0:T(8,128)(2,1)S(1)}, u32[]{:S(2)}, u32[]{:S(2)}) collective-permute-start(bf16[344,512]{1,0:T(8,128)(2,1)} %fusion.12), channel_id=1, source_target_pairs={{0,1},{1,0},{2,3},{3,2},{4,5},{5,4},{6,7},{7,6},{8,9},{9,8},{10,11... | collective-permute-start | bytes 1056776 | tf_op jit(solution)/shard_map/ppermute | solution.py:174
  113.1 14.0 %collective-permute-start.25 = (bf16[344,512]{1,0:T(8,128)(2,1)S(1)}, bf16[344,512]{1,0:T(8,128)(2,1)S(1)}, u32[]{:S(2)}, u32[]{:S(2)}) collective-permute-start(bf16[344,512]{1,0:T(8,128)(2,1)S(1)} %collective-permute-done.22), channel_id=1, source_target_pairs={{0,8},{1,9},{2,10},{3,11},{4,12},{5,13},{6,14},{7,15},{8,16},{9,17... | collective-permute-start | bytes 1056776 | tf_op jit(solution)/shard_map/ppermute | solution.py:177
  117.7 13.0 %collective-permute-start.24 = (bf16[344,512]{1,0:T(8,128)(2,1)S(1)}, bf16[344,512]{1,0:T(8,128)(2,1)S(1)}, u32[]{:S(2)}, u32[]{:S(2)}) collective-permute-start(bf16[344,512]{1,0:T(8,128)(2,1)S(1)} %collective-permute-done.21), channel_id=1, source_target_pairs={{8,0},{9,1},{10,2},{11,3},{12,4},{13,5},{14,6},{15,7},{16,8},{17,9... | collective-permute-start | bytes 1056776 | tf_op jit(solution)/shard_map/ppermute | solution.py:180
  119.0 14.3 %collective-permute-start.12 = (bf16[344,512]{1,0:T(8,128)(2,1)S(1)}, bf16[344,512]{1,0:T(8,128)(2,1)S(1)}, u32[]{:S(2)}, u32[]{:S(2)}) collective-permute-start(bf16[344,512]{1,0:T(8,128)(2,1)S(1)} %collective-permute-done.9), channel_id=1, source_target_pairs={{0,8},{1,9},{2,10},{3,11},{4,12},{5,13},{6,14},{7,15},{8,16},{9,17... | collective-permute-start | bytes 1056776 | tf_op jit(solution)/shard_map/ppermute | solution.py:177
  123.6 13.9 %collective-permute-start.11 = (bf16[344,512]{1,0:T(8,128)(2,1)S(1)}, bf16[344,512]{1,0:T(8,128)(2,1)S(1)}, u32[]{:S(2)}, u32[]{:S(2)}) collective-permute-start(bf16[344,512]{1,0:T(8,128)(2,1)S(1)} %collective-permute-done.8), channel_id=1, source_target_pairs={{8,0},{9,1},{10,2},{11,3},{12,4},{13,5},{14,6},{15,7},{16,8},{17,9... | collective-permute-start | bytes 1056776 | tf_op jit(solution)/shard_map/ppermute | solution.py:180
  131.9 11.1 %collective-permute-start.26 = (bf16[344,512]{1,0:T(8,128)(2,1)S(1)}, bf16[344,512]{1,0:T(8,128)(2,1)S(1)}, u32[]{:S(2)}, u32[]{:S(2)}) collective-permute-start(bf16[344,512]{1,0:T(8,128)(2,1)S(1)} %get-tuple-element.83), channel_id=1, source_target_pairs={{0,1},{1,0},{2,3},{3,2},{4,5},{5,4},{6,7},{7,6},{8,9},{9,8},{10,11... | collective-permute-start | bytes 1056776 | tf_op jit(solution)/shard_map/ppermute | solution.py:174
  132.0 9.9 %collective-permute-start.23 = (bf16[344,512]{1,0:T(8,128)(2,1)S(1)}, bf16[344,512]{1,0:T(8,128)(2,1)S(1)}, u32[]{:S(2)}, u32[]{:S(2)}) collective-permute-start(bf16[344,512]{1,0:T(8,128)(2,1)S(1)} %get-tuple-element.82), channel_id=1, source_target_pairs={{0,1},{1,0},{2,3},{3,2},{4,5},{5,4},{6,7},{7,6},{8,9},{9,8},{10,11... | collective-permute-start | bytes 1056776 | tf_op jit(solution)/shard_map/ppermute | solution.py:174
  132.5 7.2 %collective-permute-start.20 = (bf16[344,512]{1,0:T(8,128)(2,1)S(1)}, bf16[344,512]{1,0:T(8,128)(2,1)S(1)}, u32[]{:S(2)}, u32[]{:S(2)}) collective-permute-start(bf16[344,512]{1,0:T(8,128)(2,1)S(1)} %get-tuple-element.85), channel_id=1, source_target_pairs={{0,1},{1,0},{2,3},{3,2},{4,5},{5,4},{6,7},{7,6},{8,9},{9,8},{10,11... | collective-permute-start | bytes 1056776 | tf_op jit(solution)/shard_map/ppermute | solution.py:174
  138.6 12.4 %collective-permute-start.13 = (bf16[344,512]{1,0:T(8,128)(2,1)S(1)}, bf16[344,512]{1,0:T(8,128)(2,1)S(1)}, u32[]{:S(2)}, u32[]{:S(2)}) collective-permute-start(bf16[344,512]{1,0:T(8,128)(2,1)S(1)} %get-tuple-element.81), channel_id=1, source_target_pairs={{0,1},{1,0},{2,3},{3,2},{4,5},{5,4},{6,7},{7,6},{8,9},{9,8},{10,11... | collective-permute-start | bytes 1056776 | tf_op jit(solution)/shard_map/ppermute | solution.py:174
  138.7 7.1 %collective-permute-start.7 = (bf16[344,512]{1,0:T(8,128)(2,1)S(1)}, bf16[344,512]{1,0:T(8,128)(2,1)S(1)}, u32[]{:S(2)}, u32[]{:S(2)}) collective-permute-start(bf16[344,512]{1,0:T(8,128)(2,1)S(1)} %get-tuple-element.84), channel_id=1, source_target_pairs={{0,1},{1,0},{2,3},{3,2},{4,5},{5,4},{6,7},{7,6},{8,9},{9,8},{10,11... | collective-permute-start | bytes 1056776 | tf_op jit(solution)/shard_map/ppermute | solution.py:174
  139.7 10.1 %collective-permute-start.10 = (bf16[344,512]{1,0:T(8,128)(2,1)S(1)}, bf16[344,512]{1,0:T(8,128)(2,1)S(1)}, u32[]{:S(2)}, u32[]{:S(2)}) collective-permute-start(bf16[344,512]{1,0:T(8,128)(2,1)S(1)} %get-tuple-element.80), channel_id=1, source_target_pairs={{0,1},{1,0},{2,3},{3,2},{4,5},{5,4},{6,7},{7,6},{8,9},{9,8},{10,11... | collective-permute-start | bytes 1056776 | tf_op jit(solution)/shard_map/ppermute | solution.py:174
  144.2 9.7 %collective-permute-start.27 = (bf16[176,512]{1,0:T(8,128)(2,1)S(1)}, bf16[176,512]{1,0:T(8,128)(2,1)S(1)}, u32[]{:S(2)}, u32[]{:S(2)}) collective-permute-start(bf16[176,512]{1,0:T(8,128)(2,1)S(1)} %get-tuple-element.77), channel_id=1, source_target_pairs={{0,2},{1,3},{2,0},{3,1},{4,6},{5,7},{6,4},{7,5},{8,10},{9,11},{10,... | collective-permute-start | bytes 540680 | tf_op jit(solution)/shard_map/ppermute | solution.py:174
  144.3 11.5 %collective-permute-start.29 = (bf16[176,512]{1,0:T(8,128)(2,1)S(1)}, bf16[176,512]{1,0:T(8,128)(2,1)S(1)}, u32[]{:S(2)}, u32[]{:S(2)}) collective-permute-start(bf16[176,512]{1,0:T(8,128)(2,1)S(1)} %get-tuple-element.78), channel_id=1, source_target_pairs={{0,6},{1,7},{2,4},{3,5},{4,2},{5,3},{6,0},{7,1},{8,14},{9,15},{10,... | collective-permute-start | bytes 540680 | tf_op jit(solution)/shard_map/ppermute | solution.py:174
  145.9 10.8 %collective-permute-start.28 = (bf16[176,512]{1,0:T(8,128)(2,1)S(1)}, bf16[176,512]{1,0:T(8,128)(2,1)S(1)}, u32[]{:S(2)}, u32[]{:S(2)}) collective-permute-start(bf16[176,512]{1,0:T(8,128)(2,1)S(1)} %get-tuple-element.79), channel_id=1, source_target_pairs={{0,4},{1,5},{2,6},{3,7},{4,0},{5,1},{6,2},{7,3},{8,12},{9,13},{10,... | collective-permute-start | bytes 540680 | tf_op jit(solution)/shard_map/ppermute | solution.py:174
  152.2 7.6 %collective-permute-start.14 = (bf16[176,512]{1,0:T(8,128)(2,1)S(1)}, bf16[176,512]{1,0:T(8,128)(2,1)S(1)}, u32[]{:S(2)}, u32[]{:S(2)}) collective-permute-start(bf16[176,512]{1,0:T(8,128)(2,1)S(1)} %get-tuple-element.74), channel_id=1, source_target_pairs={{0,2},{1,3},{2,0},{3,1},{4,6},{5,7},{6,4},{7,5},{8,10},{9,11},{10,... | collective-permute-start | bytes 540680 | tf_op jit(solution)/shard_map/ppermute | solution.py:174
  152.4 10.1 %collective-permute-start.16 = (bf16[176,512]{1,0:T(8,128)(2,1)S(1)}, bf16[176,512]{1,0:T(8,128)(2,1)S(1)}, u32[]{:S(2)}, u32[]{:S(2)}) collective-permute-start(bf16[176,512]{1,0:T(8,128)(2,1)S(1)} %get-tuple-element.75), channel_id=1, source_target_pairs={{0,6},{1,7},{2,4},{3,5},{4,2},{5,3},{6,0},{7,1},{8,14},{9,15},{10,... | collective-permute-start | bytes 540680 | tf_op jit(solution)/shard_map/ppermute | solution.py:174
  153.9 10.1 %collective-permute-start.15 = (bf16[176,512]{1,0:T(8,128)(2,1)S(1)}, bf16[176,512]{1,0:T(8,128)(2,1)S(1)}, u32[]{:S(2)}, u32[]{:S(2)}) collective-permute-start(bf16[176,512]{1,0:T(8,128)(2,1)S(1)} %get-tuple-element.76), channel_id=1, source_target_pairs={{0,4},{1,5},{2,6},{3,7},{4,0},{5,1},{6,2},{7,3},{8,12},{9,13},{10,... | collective-permute-start | bytes 540680 | tf_op jit(solution)/shard_map/ppermute | solution.py:174
  164.4 9.4 %collective-permute-start.33 = (bf16[176,1024]{1,0:T(8,128)(2,1)S(1)}, bf16[176,1024]{1,0:T(8,128)(2,1)S(1)}, u32[]{:S(2)}, u32[]{:S(2)}) collective-permute-start(bf16[176,1024]{1,0:T(8,128)(2,1)S(1)} %multiply_convert_fusion.1.refs_1_.refs_5_), channel_id=1, source_target_pairs={{0,8},{1,9},{2,10},{3,11},{4,12},{5,13},{6,14},{7,15},{8,0},{9,1},... | collective-permute-start | bytes 1081352 | tf_op jit(solution)/shard_map/ppermute | solution.py:174
  166.2 9.1 %collective-permute-start.30 = (bf16[176,1024]{1,0:T(8,128)(2,1)S(1)}, bf16[176,1024]{1,0:T(8,128)(2,1)S(1)}, u32[]{:S(2)}, u32[]{:S(2)}) collective-permute-start(bf16[176,1024]{1,0:T(8,128)(2,1)S(1)} %multiply_convert_fusion.1.refs_1_.refs_5_), channel_id=1, source_target_pairs={{0,2},{1,3},{2,0},{3,1},{4,6},{5,7},{6,4},{7,5},{8,10},{9,11},{10,... | collective-permute-start | bytes 1081352 | tf_op jit(solution)/shard_map/ppermute | solution.py:174
  167.2 12.8 %collective-permute-start.31 = (bf16[176,1024]{1,0:T(8,128)(2,1)S(1)}, bf16[176,1024]{1,0:T(8,128)(2,1)S(1)}, u32[]{:S(2)}, u32[]{:S(2)}) collective-permute-start(bf16[176,1024]{1,0:T(8,128)(2,1)S(1)} %multiply_convert_fusion.1.refs_1_.refs_5_), channel_id=1, source_target_pairs={{0,4},{1,5},{2,6},{3,7},{4,0},{5,1},{6,2},{7,3},{8,12},{9,13},{10,... | collective-permute-start | bytes 1081352 | tf_op jit(solution)/shard_map/ppermute | solution.py:174
  173.8 11.4 %collective-permute-start.35 = (bf16[176,1024]{1,0:T(8,128)(2,1)S(1)}, bf16[176,1024]{1,0:T(8,128)(2,1)S(1)}, u32[]{:S(2)}, u32[]{:S(2)}) collective-permute-start(bf16[176,1024]{1,0:T(8,128)(2,1)S(1)} %collective-permute-done.33.refs_1_.refs_9_), channel_id=1, source_target_pairs={{0,4},{1,5},{2,6},{3,7},{4,0},{5,1},{6,2},{7,3},{8,12},{9,13},{10,... | collective-permute-start | bytes 1081352 | tf_op jit(solution)/shard_map/ppermute | solution.py:174
  175.3 15.4 %collective-permute-start.32 = (bf16[176,1024]{1,0:T(8,128)(2,1)S(1)}, bf16[176,1024]{1,0:T(8,128)(2,1)S(1)}, u32[]{:S(2)}, u32[]{:S(2)}) collective-permute-start(bf16[176,1024]{1,0:T(8,128)(2,1)S(1)} %collective-permute-done.30.refs_2_.refs_6_), channel_id=1, source_target_pairs={{0,4},{1,5},{2,6},{3,7},{4,0},{5,1},{6,2},{7,3},{8,12},{9,13},{10,... | collective-permute-start | bytes 1081352 | tf_op jit(solution)/shard_map/ppermute | solution.py:174
  175.9 25.6 %collective-permute-start.37 = (bf16[176,1024]{1,0:T(8,128)(2,1)S(1)}, bf16[176,1024]{1,0:T(8,128)(2,1)S(1)}, u32[]{:S(2)}, u32[]{:S(2)}) collective-permute-start(bf16[176,1024]{1,0:T(8,128)(2,1)S(1)} %multiply_convert_fusion.1.refs_1_.refs_5_), channel_id=1, source_target_pairs={{0,16},{1,17},{2,18},{3,19},{4,20},{5,21},{6,22},{7,23},{8,24},{9,... | collective-permute-start | bytes 1081352 | tf_op jit(solution)/shard_map/ppermute | solution.py:174
  177.1 26.1 %collective-permute-start.40 = (bf16[176,1024]{1,0:T(8,128)(2,1)S(1)}, bf16[176,1024]{1,0:T(8,128)(2,1)S(1)}, u32[]{:S(2)}, u32[]{:S(2)}) collective-permute-start(bf16[176,1024]{1,0:T(8,128)(2,1)S(1)} %multiply_convert_fusion.1.refs_1_.refs_5_), channel_id=1, source_target_pairs={{0,24},{1,25},{2,26},{3,27},{4,28},{5,29},{6,30},{7,31},{8,16},{9,... | collective-permute-start | bytes 1081352 | tf_op jit(solution)/shard_map/ppermute | solution.py:174
  180.0 23.6 %collective-permute-start.34 = (bf16[176,1024]{1,0:T(8,128)(2,1)S(1)}, bf16[176,1024]{1,0:T(8,128)(2,1)S(1)}, u32[]{:S(2)}, u32[]{:S(2)}) collective-permute-start(bf16[176,1024]{1,0:T(8,128)(2,1)S(1)} %collective-permute-done.33.refs_1_.refs_9_), channel_id=1, source_target_pairs={{0,2},{1,3},{2,0},{3,1},{4,6},{5,7},{6,4},{7,5},{8,10},{9,11},{10,... | collective-permute-start | bytes 1081352 | tf_op jit(solution)/shard_map/ppermute | solution.py:174
  185.2 20.4 %collective-permute-start.36 = (bf16[176,1024]{1,0:T(8,128)(2,1)S(1)}, bf16[176,1024]{1,0:T(8,128)(2,1)S(1)}, u32[]{:S(2)}, u32[]{:S(2)}) collective-permute-start(bf16[176,1024]{1,0:T(8,128)(2,1)S(1)} %collective-permute-done.35.refs_3_.refs_11_), channel_id=1, source_target_pairs={{0,2},{1,3},{2,0},{3,1},{4,6},{5,7},{6,4},{7,5},{8,10},{9,11},{10,... | collective-permute-start | bytes 1081352 | tf_op jit(solution)/shard_map/ppermute | solution.py:174
  201.5 18.2 %collective-permute-start.39 = (bf16[176,1024]{1,0:T(8,128)(2,1)S(1)}, bf16[176,1024]{1,0:T(8,128)(2,1)S(1)}, u32[]{:S(2)}, u32[]{:S(2)}) collective-permute-start(bf16[176,1024]{1,0:T(8,128)(2,1)S(1)} %collective-permute-done.37.refs_1_.refs_13_), channel_id=1, source_target_pairs={{0,4},{1,5},{2,6},{3,7},{4,0},{5,1},{6,2},{7,3},{8,12},{9,13},{10,... | collective-permute-start | bytes 1081352 | tf_op jit(solution)/shard_map/ppermute | solution.py:174
  201.8 16.1 %collective-permute-start.38 = (bf16[176,1024]{1,0:T(8,128)(2,1)S(1)}, bf16[176,1024]{1,0:T(8,128)(2,1)S(1)}, u32[]{:S(2)}, u32[]{:S(2)}) collective-permute-start(bf16[176,1024]{1,0:T(8,128)(2,1)S(1)} %collective-permute-done.37.refs_1_.refs_13_), channel_id=1, source_target_pairs={{0,2},{1,3},{2,0},{3,1},{4,6},{5,7},{6,4},{7,5},{8,10},{9,11},{10,... | collective-permute-start | bytes 1081352 | tf_op jit(solution)/shard_map/ppermute | solution.py:174
  203.3 14.5 %collective-permute-start.42 = (bf16[176,1024]{1,0:T(8,128)(2,1)S(1)}, bf16[176,1024]{1,0:T(8,128)(2,1)S(1)}, u32[]{:S(2)}, u32[]{:S(2)}) collective-permute-start(bf16[176,1024]{1,0:T(8,128)(2,1)S(1)} %collective-permute-done.40.refs_4_.refs_16_), channel_id=1, source_target_pairs={{0,4},{1,5},{2,6},{3,7},{4,0},{5,1},{6,2},{7,3},{8,12},{9,13},{10,... | collective-permute-start | bytes 1081352 | tf_op jit(solution)/shard_map/ppermute | solution.py:174
  203.6 16.1 %collective-permute-start.41 = (bf16[176,1024]{1,0:T(8,128)(2,1)S(1)}, bf16[176,1024]{1,0:T(8,128)(2,1)S(1)}, u32[]{:S(2)}, u32[]{:S(2)}) collective-permute-start(bf16[176,1024]{1,0:T(8,128)(2,1)S(1)} %collective-permute-done.40.refs_4_.refs_16_), channel_id=1, source_target_pairs={{0,2},{1,3},{2,0},{3,1},{4,6},{5,7},{6,4},{7,5},{8,10},{9,11},{10,... | collective-permute-start | bytes 1081352 | tf_op jit(solution)/shard_map/ppermute | solution.py:174
  217.8 9.3 %collective-permute-start.43 = (bf16[176,1024]{1,0:T(8,128)(2,1)S(1)}, bf16[176,1024]{1,0:T(8,128)(2,1)S(1)}, u32[]{:S(2)}, u32[]{:S(2)}) collective-permute-start(bf16[176,1024]{1,0:T(8,128)(2,1)S(1)} %collective-permute-done.38.refs_2_.refs_14_), channel_id=1, source_target_pairs={{0,4},{1,5},{2,6},{3,7},{4,0},{5,1},{6,2},{7,3},{8,12},{9,13},{10,... | collective-permute-start | bytes 1081352 | tf_op jit(solution)/shard_map/ppermute | solution.py:174
  219.6 8.9 %collective-permute-start.44 = (bf16[176,1024]{1,0:T(8,128)(2,1)S(1)}, bf16[176,1024]{1,0:T(8,128)(2,1)S(1)}, u32[]{:S(2)}, u32[]{:S(2)}) collective-permute-start(bf16[176,1024]{1,0:T(8,128)(2,1)S(1)} %collective-permute-done.42.refs_6_.refs_18_), channel_id=1, source_target_pairs={{0,2},{1,3},{2,0},{3,1},{4,6},{5,7},{6,4},{7,5},{8,10},{9,11},{10,... | collective-permute-start | bytes 1081352 | tf_op jit(solution)/shard_map/ppermute | solution.py:174
  237.0 4.7 %collective-permute-start.49 = (f32[4,4,176]{2,1,0:T(4,128)S(1)}, f32[4,4,176]{2,1,0:T(4,128)S(1)}, u32[]{:S(2)}, u32[]{:S(2)}) collective-permute-start(f32[4,4,176]{2,1,0:T(4,128)S(1)} %log_add_fusion.1), channel_id=1, source_target_pairs={{0,16},{1,17},{2,18},{3,19},{4,20},{5,21},{6,22},{7,23},{8,24},{9,... | collective-permute-start | bytes 33800 | tf_op jit(solution)/shard_map/ppermute | solution.py:174
  237.4 5.5 %collective-permute-start.50 = (f32[4,4,176]{2,1,0:T(4,128)S(1)}, f32[4,4,176]{2,1,0:T(4,128)S(1)}, u32[]{:S(2)}, u32[]{:S(2)}) collective-permute-start(f32[4,4,176]{2,1,0:T(4,128)S(1)} %log_add_fusion.1), channel_id=1, source_target_pairs={{0,24},{1,25},{2,26},{3,27},{4,28},{5,29},{6,30},{7,31},{8,16},{9,... | collective-permute-start | bytes 33800 | tf_op jit(solution)/shard_map/ppermute | solution.py:174
  (38 other events, 334.7 us)

commit v2 on v1

--- a/solution.py
+++ b/solution.py
@@ -100,7 +100,7 @@
 
     @pl.when(step >= tiles)
     def _():
-        near[...] = sums
+        near[...] = sums.astype(BF16)
 
 
 def weigh(groups, es, w, scale):
@@ -125,7 +125,7 @@
             pl.BlockSpec((1, tile), lambda i: (0, turn(i))),
         ],
         out_shape=[
-            jax.ShapeDtypeStruct((cents // 2, width), F32),
+            jax.ShapeDtypeStruct((cents // 2, width), BF16),
             jax.ShapeDtypeStruct((cents // 2, width), BF16),
             jax.ShapeDtypeStruct((1, cents), F32),
         ],
@@ -221,15 +221,15 @@
         direct = dot(residual, own.astype(BF16))
         pair = jnp.concatenate([centroids, hop(centroids, 1)])
         last = blocks[QUAD - 1]
-        down_rows, full, direct, pair, last, *units = lax.optimization_barrier(
-            (down_rows, full, direct, pair, last, *units)
+        halves = [slice(0, width // 2), slice(width // 2, width)]
+        down_rows, heads, direct, pair, last, units = lax.optimization_barrier(
+            (down_rows, [full[:, h] for h in halves], direct, pair, last, units)
         )
 
-        halves = [slice(0, width // 2), slice(width // 2, width)]
         folds = []
-        for h in halves:
+        for head in heads:
             source = after(down_rows, folds[0]) if folds else down_rows
-            folds.append(dot(source, full[:, h]).astype(BF16))
+            folds.append(dot(source, head).astype(BF16))
             if not units[QUAD - 1 :]:
                 last, folds[0] = lax.optimization_barrier((last, folds[0]))
                 units.append(hop(last, 2 * (QUAD - 1)))
@@ -302,7 +302,7 @@
         w = jnp.exp(tops - jnp.concatenate(logs)[None])
 
         near, far, masses = weigh(groups, [e for e, _, _ in scored], w, scale_up)
-        weighted = near + hop(far, 1).astype(F32)
+        weighted = near.astype(F32) + hop(far, 1).astype(F32)
         counts = masses[0, :cents] + hop(masses[0, cents:], 1)
         return weighted, counts
 

time: 265 us -> 262 us (0.989)
  waiting for transfers between devices: 97 us -> 81.9 us
  starting transfers between devices: 77.1 us -> 87.4 us
  local copies, waits for them, and re-layouts: 18.4 us -> 23 us
    ppermute x6, waiting for transfers between devices: 12.6 us -> 4.71 us  [down(): return lax.ppermute(v, 'dp', [(i + PLANE, i) for i in range(n - PLANE)])]
    ppermute x6, starting transfers between devices: 23.2 us -> 28.8 us  [up(): return lax.ppermute(v, 'dp', [(i, i + PLANE) for i in range(n - PLANE)])]
    ppermute x41, waiting for transfers between devices: 48.7 us -> 43.6 us  [hop(): return lax.ppermute(v, 'dp', [(i, i ^ k) for i in range(n)])]
    ppermute x41, starting transfers between devices: 38.6 us -> 43.5 us  [hop(): return lax.ppermute(v, 'dp', [(i, i ^ k) for i in range(n)])]
    slice x0 -> x1, local copies, waits for them, and re-layouts: none -> 3.89 us  [body(): full[:, h]]
    all_to_all x1, waiting for transfers between devices: 35.4 us -> 31.6 us  [body(): down_rows = lax.all_to_all(down_weight, 'dp', 0, 1, tiled=True)]
    unnamed x67 -> x69, local copies, waits for them, and re-layouts: 9.9 us -> 10.6 us
  transfers between devices with their start and end apart: 54 -> 54, of which waited for: 24 -> 20; matrix products, arithmetic and copies ran while one was open for 17% -> 18% of each run, Pallas kernels for 4% -> 4%
where the time goes in v2:
time: 262 us; the launch traced here: 261 us
  starting transfers between devices  87.4 us (33%)
  waiting for transfers between devices  81.9 us (31%)
  Pallas kernels  25.7 us (10%)
  local copies, waits for them, and re-layouts  23 us (9%)
  matrix products  22.4 us (9%)
  other arithmetic  19.5 us (7%)
    ppermute x41, waiting for transfers between devices, hop(): return lax.ppermute(v, 'dp', [(i, i ^ k) for i in range(n)])  43.6 us
    ppermute x41, starting transfers between devices, hop(): return lax.ppermute(v, 'dp', [(i, i ^ k) for i in range(n)])  43.5 us
    all_to_all x1, waiting for transfers between devices, body(): down_rows = lax.all_to_all(down_weight, 'dp', 0, 1, tiled=True)  31.6 us
    ppermute x6, starting transfers between devices, up(): return lax.ppermute(v, 'dp', [(i, i + PLANE) for i in range(n - PLANE)])  28.8 us
    dot_general x19, matrix products, dot(): return jnp.dot(a, b, preferred_element_type=F32)  22.4 us
    pallas_call x1, Pallas kernels, weigh(): pl.pallas_call(lambda *refs: weigh_kernel(sizes, scale, tiles, *refs), gr...  12.6 us
    pallas_call x4, Pallas kernels, score(): pl.pallas_call(lambda *refs: score_kernel(1.0 / (math.sqrt(width) * 0.05)...  11.1 us
    unnamed x69, local copies, waits for them, and re-layouts  10.6 us
  transfers between devices with their start and end apart: 54, of which 20 were waited for; matrix products, arithmetic and copies ran while one was open for 18% of the time, Pallas kernels for 4%

profile of v2, /device:TPU:0, one launch (start us, length us, event | category | flops | bytes accessed | tf_op | source)
XLA Modules:
  0.0 261.4 jit_solution(9340187749276607607)
XLA Ops:
  0.6 7.4 %all-to-all-start = ((bf16[32,344,128]{2,1,0:T(8,128)(2,1)}), bf16[32,344,128]{2,1,0:T(8,128)(2,1)}, u32[]{:S(2)}, u32[]{:S(2)}) async-start(bf16[32,344,128]{2,1,0:T(8,128)(2,1)} %bitcast.126), calls=%async_computation | async-start | bytes 5636096 | tf_op jit(solution)/shard_map/all_to_all | solution.py:217
  9.5 2.6 fusion.28.position
  12.1 2.1 copy-done.2
  14.2 2.0 shard_map.86
  16.2 2.2 fusion.36
  18.4 1.7 collective-permute-start.1
  21.6 8.2 %multiply_convert_fusion = bf16[4096,1024]{1,0:T(8,128)(2,1)} fusion(bf16[4096,1024]{1,0:T(8,128)(2,1)} %param.11, f32[4096]{0:T(1024)S(1)} %copy-done.32), kind=kLoop, calls=%fused_computation | loop fusion | flops 12582912 | bytes 16793600 | tf_op jit(solution)/shard_map/convert_element_type | solution.py:220
  29.7 6.0 %convolution_bitcast_fusion = f32[176,1024]{1,0:T(8,128)} fusion(bf16[176,4096]{1,0:T(8,128)(2,1)S(1)} %copy-done, bf16[4096,1024]{1,0:T(8,128)(2,1)} %multiply_convert_fusion), kind=kOutput, calls=%fused_computation.18 | convolution fusion | flops 1476395008 | bytes 10551296 | tf_op jit(solution)/shard_map/dot_general | solution.py:18
  35.8 3.9 %fusion.35 = (bf16[4096,512]{1,0:T(8,128)(2,1)}, bf16[4096,512]{1,0:T(8,128)(2,1)}) fusion(bf16[4096,1024]{1,0:T(8,128)(2,1)S(1)} %copy-done.23), kind=kLoop, calls=%fused_computation.119 | loop fusion | bytes 16777216 | tf_op jit(solution)/shard_map/slice | solution.py:226
  41.1 31.6 %all-to-all-done = bf16[32,344,128]{2,1,0:T(8,128)(2,1)} async-done(((bf16[32,344,128]{2,1,0:T(8,128)(2,1)}), bf16[32,344,128]{2,1,0:T(8,128)(2,1)}, u32[]{:S(2)}, u32[]{:S(2)}) %all-to-all-start) | async-done | bytes 2818080 | tf_op jit(solution)/shard_map/all_to_all | solution.py:217
  72.7 2.3 copy_bitcast_fusion
  75.7 2.4 convolution_convert_fusion.1
  78.1 2.4 convolution_convert_fusion
  80.4 2.0 collective-permute-start.3
  83.8 5.3 %collective-permute-start.19 = (bf16[344,512]{1,0:T(8,128)(2,1)}, bf16[344,512]{1,0:T(8,128)(2,1)}, u32[]{:S(2)}, u32[]{:S(2)}) collective-permute-start(bf16[344,512]{1,0:T(8,128)(2,1)} %convolution_convert_fusion), channel_id=1, source_target_pairs={{0,8},{1,9},{2,10},{3,11},{4,12},{5,13},{6,14},{7,15},{8,16},{9,17... | collective-permute-start | bytes 1056776 | tf_op jit(solution)/shard_map/ppermute | solution.py:177
  90.4 5.3 %collective-permute-start.6 = (bf16[344,512]{1,0:T(8,128)(2,1)}, bf16[344,512]{1,0:T(8,128)(2,1)}, u32[]{:S(2)}, u32[]{:S(2)}) collective-permute-start(bf16[344,512]{1,0:T(8,128)(2,1)} %convolution_convert_fusion.1), channel_id=1, source_target_pairs={{0,8},{1,9},{2,10},{3,11},{4,12},{5,13},{6,14},{7,15},{8,16},{9,17... | collective-permute-start | bytes 1056776 | tf_op jit(solution)/shard_map/ppermute | solution.py:177
  97.2 4.5 %collective-permute-start.22 = (bf16[344,512]{1,0:T(8,128)(2,1)}, bf16[344,512]{1,0:T(8,128)(2,1)S(1)}, u32[]{:S(2)}, u32[]{:S(2)}) collective-permute-start(bf16[344,512]{1,0:T(8,128)(2,1)} %collective-permute-done.19), channel_id=1, source_target_pairs={{0,8},{1,9},{2,10},{3,11},{4,12},{5,13},{6,14},{7,15},{8,16},{9,17... | collective-permute-start | bytes 1056776 | tf_op jit(solution)/shard_map/ppermute | solution.py:177
  104.8 4.4 %collective-permute-start.9 = (bf16[344,512]{1,0:T(8,128)(2,1)}, bf16[344,512]{1,0:T(8,128)(2,1)S(1)}, u32[]{:S(2)}, u32[]{:S(2)}) collective-permute-start(bf16[344,512]{1,0:T(8,128)(2,1)} %collective-permute-done.6), channel_id=1, source_target_pairs={{0,8},{1,9},{2,10},{3,11},{4,12},{5,13},{6,14},{7,15},{8,16},{9,17... | collective-permute-start | bytes 1056776 | tf_op jit(solution)/shard_map/ppermute | solution.py:177
  115.0 4.6 %collective-permute-start.25 = (bf16[344,512]{1,0:T(8,128)(2,1)S(1)}, bf16[344,512]{1,0:T(8,128)(2,1)S(1)}, u32[]{:S(2)}, u32[]{:S(2)}) collective-permute-start(bf16[344,512]{1,0:T(8,128)(2,1)S(1)} %collective-permute-done.22), channel_id=1, source_target_pairs={{0,8},{1,9},{2,10},{3,11},{4,12},{5,13},{6,14},{7,15},{8,16},{9,17... | collective-permute-start | bytes 1056776 | tf_op jit(solution)/shard_map/ppermute | solution.py:177
  120.9 4.7 %collective-permute-start.12 = (bf16[344,512]{1,0:T(8,128)(2,1)S(1)}, bf16[344,512]{1,0:T(8,128)(2,1)S(1)}, u32[]{:S(2)}, u32[]{:S(2)}) collective-permute-start(bf16[344,512]{1,0:T(8,128)(2,1)S(1)} %collective-permute-done.9), channel_id=1, source_target_pairs={{0,8},{1,9},{2,10},{3,11},{4,12},{5,13},{6,14},{7,15},{8,16},{9,17... | collective-permute-start | bytes 1056776 | tf_op jit(solution)/shard_map/ppermute | solution.py:177
  130.5 3.2 %collective-permute-done.11 = bf16[344,512]{1,0:T(8,128)(2,1)S(1)} collective-permute-done((bf16[344,512]{1,0:T(8,128)(2,1)S(1)}, bf16[344,512]{1,0:T(8,128)(2,1)S(1)}, u32[]{:S(2)}, u32[]{:S(2)}) %collective-permute-start.11) | collective-permute-done | bytes 352288 | tf_op jit(solution)/shard_map/ppermute | solution.py:180
  137.9 1.5 fusion.5
  143.1 2.0 collective-permute-start.29
  145.7 1.6 fusion.1
  151.2 2.0 collective-permute-start.16
  153.2 4.0 %collective-permute-done.14 = bf16[176,512]{1,0:T(8,128)(2,1)S(1)} collective-permute-done((bf16[176,512]{1,0:T(8,128)(2,1)S(1)}, bf16[176,512]{1,0:T(8,128)(2,1)S(1)}, u32[]{:S(2)}, u32[]{:S(2)}) %collective-permute-start.14) | collective-permute-done | bytes 180256 | tf_op jit(solution)/shard_map/ppermute | solution.py:174
  157.2 3.2 %collective-permute-done.15 = bf16[176,512]{1,0:T(8,128)(2,1)S(1)} collective-permute-done((bf16[176,512]{1,0:T(8,128)(2,1)S(1)}, bf16[176,512]{1,0:T(8,128)(2,1)S(1)}, u32[]{:S(2)}, u32[]{:S(2)}) %collective-permute-start.15) | collective-permute-done | bytes 180256 | tf_op jit(solution)/shard_map/ppermute | solution.py:174
  160.9 2.5 collective-permute-start.33
  163.5 1.6 collective-permute-start.30
  165.5 5.6 %collective-permute-done.33.refs_1_.refs_9_ = bf16[176,1024]{1,0:T(8,128)(2,1)S(1)} collective-permute-done((bf16[176,1024]{1,0:T(8,128)(2,1)S(1)}, bf16[176,1024]{1,0:T(8,128)(2,1)S(1)}, u32[]{:S(2)}, u32[]{:S(2)}) %collective-permute-start.33) | collective-permute-done | bytes 360480 | tf_op jit(solution)/shard_map/ppermute | solution.py:174
  177.3 5.1 %collective-permute-done.35.refs_3_.refs_11_ = bf16[176,1024]{1,0:T(8,128)(2,1)S(1)} collective-permute-done((bf16[176,1024]{1,0:T(8,128)(2,1)S(1)}, bf16[176,1024]{1,0:T(8,128)(2,1)S(1)}, u32[]{:S(2)}, u32[]{:S(2)}) %collective-permute-start.35) | collective-permute-done | bytes 360480 | tf_op jit(solution)/shard_map/ppermute | solution.py:174
  183.7 5.0 %collective-permute-done.32.refs_4_.refs_8_ = bf16[176,1024]{1,0:T(8,128)(2,1)S(1)} collective-permute-done((bf16[176,1024]{1,0:T(8,128)(2,1)S(1)}, bf16[176,1024]{1,0:T(8,128)(2,1)S(1)}, u32[]{:S(2)}, u32[]{:S(2)}) %collective-permute-start.32) | collective-permute-done | bytes 360480 | tf_op jit(solution)/shard_map/ppermute | solution.py:174
  188.7 2.6 %shard_map.87 = (bf16[1024,768]{1,0:T(8,128)(2,1)S(1)}, f32[1,768]{1,0:T(1,128)S(1)}, f32[1,768]{1,0:T(1,128)S(1)}) custom-call(bf16[1024,1024]{1,0:T(8,128)(2,1)S(1)} %pad_maximum_fusion.refs_0_, bf16[176,1024]{1,0:T(8,128)(2,1)S(1)} %multiply_convert_fusion.1.refs_1_.refs_5_, bf16[176,1024]{1,0:T(8,128)(2,1)S(1)} %collective-permute-done.30.refs_2_.refs_6_, ...), custom_call_target="tpu_custom_call" | custom-call | flops 1610612736 | bytes 5242880 | tf_op jit(solution)/shard_map/pallas_call | solution.py:53
  195.0 10.4 %collective-permute-done.37.refs_1_.refs_13_ = bf16[176,1024]{1,0:T(8,128)(2,1)S(1)} collective-permute-done((bf16[176,1024]{1,0:T(8,128)(2,1)S(1)}, bf16[176,1024]{1,0:T(8,128)(2,1)S(1)}, u32[]{:S(2)}, u32[]{:S(2)}) %collective-permute-start.37) | collective-permute-done | bytes 360480 | tf_op jit(solution)/shard_map/ppermute | solution.py:174
  205.8 1.7 collective-permute-start.39
  207.6 2.6 shard_map.88
  211.4 1.5 collective-permute-start.44
  213.0 2.4 collective-permute-done.38.refs_2_.refs_14_
  215.3 3.0 %collective-permute-start.43 = (bf16[176,1024]{1,0:T(8,128)(2,1)S(1)}, bf16[176,1024]{1,0:T(8,128)(2,1)S(1)}, u32[]{:S(2)}, u32[]{:S(2)}) collective-permute-start(bf16[176,1024]{1,0:T(8,128)(2,1)S(1)} %collective-permute-done.38.refs_2_.refs_14_), channel_id=1, source_target_pairs={{0,4},{1,5},{2,6},{3,7},{4,0},{5,1},{6,2},{7,3},{8,12},{9,13},{10,... | collective-permute-start | bytes 1081352 | tf_op jit(solution)/shard_map/ppermute | solution.py:174
  218.4 4.1 %shard_map.89 = (bf16[1024,1152]{1,0:T(8,128)(2,1)S(1)}, f32[1,1152]{1,0:T(1,128)S(1)}, f32[1,1152]{1,0:T(1,128)S(1)}) custom-call(bf16[1024,1024]{1,0:T(8,128)(2,1)S(1)} %pad_maximum_fusion.refs_0_, bf16[176,1024]{1,0:T(8,128)(2,1)S(1)} %collective-permute-done.37.refs_1_.refs_13_, bf16[176,1024]{1,0:T(8,128)(2,1)S(1)} %collective-permute-done.38.refs_2_.refs_14_, ...), custom_call_target="tpu_custom_call" | custom-call | flops 2415919104 | bytes 6815744 | tf_op jit(solution)/shard_map/pallas_call | solution.py:53
  224.1 1.8 shard_map.90
  227.5 1.6 collective-permute-start.46
  231.3 2.5 collective-permute-done.47
  234.4 1.6 collective-permute-start.48
  236.0 2.4 collective-permute-start.50
  238.8 2.8 %collective-permute-done.50 = f32[4,4,176]{2,1,0:T(4,128)S(1)} collective-permute-done((f32[4,4,176]{2,1,0:T(4,128)S(1)}, f32[4,4,176]{2,1,0:T(4,128)S(1)}, u32[]{:S(2)}, u32[]{:S(2)}) %collective-permute-start.50) | collective-permute-done | bytes 11296 | tf_op jit(solution)/shard_map/ppermute | solution.py:174
  242.4 12.6 %shard_map.91 = (bf16[512,1024]{1,0:T(8,128)(2,1)}, bf16[512,1024]{1,0:T(8,128)(2,1)}, f32[1,1024]{1,0:T(1,128)}) custom-call(f32[1,3072]{1,0:T(1,128)} %fusion.26.refs_0_, bf16[1024,768]{1,0:T(8,128)(2,1)} %copy-done.20, bf16[1024,768]{1,0:T(8,128)(2,1)} %copy-done.21, bf16[1024,1152]{1,0:T(8,128)(2,1)} %copy-done.22, bf16[1024,384]{1,0:T(8,128)(2,1)} %copy-done.19, ...), custom_call_target="tpu_custom_call" | custom-call | flops 6442450944 | bytes 20971520 | tf_op jit(solution)/shard_map/pallas_call | solution.py:116
  258.4 3.0 %convert_add_fusion = f32[512,1024]{1,0:T(8,128)} fusion(bf16[512,1024]{1,0:T(8,128)(2,1)S(1)} %collective-permute-done.51, bf16[512,1024]{1,0:T(8,128)(2,1)} %get-tuple-element.67), kind=kLoop, calls=%fused_computation.3 | loop fusion | flops 1572864 | bytes 4194304 | tf_op jit(solution)/shard_map/add | solution.py:305
  (195 shorter events, 60.5 us)
Async XLA Ops:
  0.6 72.0 %all-to-all-start = ((bf16[32,344,128]{2,1,0:T(8,128)(2,1)}), bf16[32,344,128]{2,1,0:T(8,128)(2,1)}, u32[]{:S(2)}, u32[]{:S(2)}) async-start(bf16[32,344,128]{2,1,0:T(8,128)(2,1)} %bitcast.126), calls=%async_computation | async-start | bytes 5636096 | tf_op jit(solution)/shard_map/all_to_all | solution.py:217
  18.4 56.6 %collective-permute-start.1 = (bf16[4,2,176,344]{3,2,1,0:T(8,128)(2,1)}, bf16[4,2,176,344]{3,2,1,0:T(8,128)(2,1)}, u32[]{:S(2)}, u32[]{:S(2)}) collective-permute-start(bf16[4,2,176,344]{3,2,1,0:T(8,128)(2,1)} %bitcast.10), channel_id=1, source_target_pairs={{0,2},{1,3},{2,0},{3,1},{4,6},{5,7},{6,4},{7,5},{8,10},{9,11},{10,... | collective-permute-start | bytes 2906120 | tf_op jit(solution)/shard_map/ppermute | solution.py:174
  20.1 54.9 %collective-permute-start.2 = (bf16[4,2,176,344]{3,2,1,0:T(8,128)(2,1)}, bf16[4,2,176,344]{3,2,1,0:T(8,128)(2,1)}, u32[]{:S(2)}, u32[]{:S(2)}) collective-permute-start(bf16[4,2,176,344]{3,2,1,0:T(8,128)(2,1)} %bitcast.11), channel_id=1, source_target_pairs={{0,4},{1,5},{2,6},{3,7},{4,0},{5,1},{6,2},{7,3},{8,12},{9,13},{10,... | collective-permute-start | bytes 2906120 | tf_op jit(solution)/shard_map/ppermute | solution.py:174
  21.6 18.1 %collective-permute-start = (bf16[512,1024]{1,0:T(8,128)(2,1)S(1)}, bf16[512,1024]{1,0:T(8,128)(2,1)}, u32[]{:S(2)}, u32[]{:S(2)}) collective-permute-start(bf16[512,1024]{1,0:T(8,128)(2,1)S(1)} %copy-done.27), channel_id=1, source_target_pairs={{0,1},{1,0},{2,3},{3,2},{4,5},{5,4},{6,7},{7,6},{8,9},{9,8},{10,11... | collective-permute-start | bytes 3145736 | tf_op jit(solution)/shard_map/ppermute | solution.py:174
  80.4 9.9 %collective-permute-start.17 = (bf16[344,512]{1,0:T(8,128)(2,1)}, bf16[344,512]{1,0:T(8,128)(2,1)}, u32[]{:S(2)}, u32[]{:S(2)}) collective-permute-start(bf16[344,512]{1,0:T(8,128)(2,1)} %convolution_convert_fusion), channel_id=1, source_target_pairs={{0,1},{1,0},{2,3},{3,2},{4,5},{5,4},{6,7},{7,6},{8,9},{9,8},{10,11... | collective-permute-start | bytes 1056776 | tf_op jit(solution)/shard_map/ppermute | solution.py:174
  80.4 31.7 %collective-permute-start.3 = (bf16[4,2,176,344]{3,2,1,0:T(8,128)(2,1)}, bf16[4,2,176,344]{3,2,1,0:T(8,128)(2,1)}, u32[]{:S(2)}, u32[]{:S(2)}) collective-permute-start(bf16[4,2,176,344]{3,2,1,0:T(8,128)(2,1)} %bitcast.8), channel_id=1, source_target_pairs={{0,6},{1,7},{2,4},{3,5},{4,2},{5,3},{6,0},{7,1},{8,14},{9,15},{10,... | collective-permute-start | bytes 2906120 | tf_op jit(solution)/shard_map/ppermute | solution.py:174
  82.5 13.3 %collective-permute-start.18 = (bf16[344,512]{1,0:T(8,128)(2,1)}, bf16[344,512]{1,0:T(8,128)(2,1)}, u32[]{:S(2)}, u32[]{:S(2)}) collective-permute-start(bf16[344,512]{1,0:T(8,128)(2,1)} %convolution_convert_fusion), channel_id=1, source_target_pairs={{8,0},{9,1},{10,2},{11,3},{12,4},{13,5},{14,6},{15,7},{16,8},{17,9... | collective-permute-start | bytes 1056776 | tf_op jit(solution)/shard_map/ppermute | solution.py:180
  83.8 13.5 %collective-permute-start.19 = (bf16[344,512]{1,0:T(8,128)(2,1)}, bf16[344,512]{1,0:T(8,128)(2,1)}, u32[]{:S(2)}, u32[]{:S(2)}) collective-permute-start(bf16[344,512]{1,0:T(8,128)(2,1)} %convolution_convert_fusion), channel_id=1, source_target_pairs={{0,8},{1,9},{2,10},{3,11},{4,12},{5,13},{6,14},{7,15},{8,16},{9,17... | collective-permute-start | bytes 1056776 | tf_op jit(solution)/shard_map/ppermute | solution.py:177
  89.1 14.1 %collective-permute-start.5 = (bf16[344,512]{1,0:T(8,128)(2,1)}, bf16[344,512]{1,0:T(8,128)(2,1)S(1)}, u32[]{:S(2)}, u32[]{:S(2)}) collective-permute-start(bf16[344,512]{1,0:T(8,128)(2,1)} %convolution_convert_fusion.1), channel_id=1, source_target_pairs={{8,0},{9,1},{10,2},{11,3},{12,4},{13,5},{14,6},{15,7},{16,8},{17,9... | collective-permute-start | bytes 1056776 | tf_op jit(solution)/shard_map/ppermute | solution.py:180
  90.4 14.4 %collective-permute-start.6 = (bf16[344,512]{1,0:T(8,128)(2,1)}, bf16[344,512]{1,0:T(8,128)(2,1)}, u32[]{:S(2)}, u32[]{:S(2)}) collective-permute-start(bf16[344,512]{1,0:T(8,128)(2,1)} %convolution_convert_fusion.1), channel_id=1, source_target_pairs={{0,8},{1,9},{2,10},{3,11},{4,12},{5,13},{6,14},{7,15},{8,16},{9,17... | collective-permute-start | bytes 1056776 | tf_op jit(solution)/shard_map/ppermute | solution.py:177
  95.8 17.8 %collective-permute-start.21 = (bf16[344,512]{1,0:T(8,128)(2,1)}, bf16[344,512]{1,0:T(8,128)(2,1)S(1)}, u32[]{:S(2)}, u32[]{:S(2)}) collective-permute-start(bf16[344,512]{1,0:T(8,128)(2,1)} %collective-permute-done.18), channel_id=1, source_target_pairs={{8,0},{9,1},{10,2},{11,3},{12,4},{13,5},{14,6},{15,7},{16,8},{17,9... | collective-permute-start | bytes 1056776 | tf_op jit(solution)/shard_map/ppermute | solution.py:180
  97.2 17.7 %collective-permute-start.22 = (bf16[344,512]{1,0:T(8,128)(2,1)}, bf16[344,512]{1,0:T(8,128)(2,1)S(1)}, u32[]{:S(2)}, u32[]{:S(2)}) collective-permute-start(bf16[344,512]{1,0:T(8,128)(2,1)} %collective-permute-done.19), channel_id=1, source_target_pairs={{0,8},{1,9},{2,10},{3,11},{4,12},{5,13},{6,14},{7,15},{8,16},{9,17... | collective-permute-start | bytes 1056776 | tf_op jit(solution)/shard_map/ppermute | solution.py:177
  103.2 16.4 %collective-permute-start.8 = (bf16[344,512]{1,0:T(8,128)(2,1)S(1)}, bf16[344,512]{1,0:T(8,128)(2,1)S(1)}, u32[]{:S(2)}, u32[]{:S(2)}) collective-permute-start(bf16[344,512]{1,0:T(8,128)(2,1)S(1)} %collective-permute-done.5), channel_id=1, source_target_pairs={{8,0},{9,1},{10,2},{11,3},{12,4},{13,5},{14,6},{15,7},{16,8},{17,9... | collective-permute-start | bytes 1056776 | tf_op jit(solution)/shard_map/ppermute | solution.py:180
  104.8 16.1 %collective-permute-start.9 = (bf16[344,512]{1,0:T(8,128)(2,1)}, bf16[344,512]{1,0:T(8,128)(2,1)S(1)}, u32[]{:S(2)}, u32[]{:S(2)}) collective-permute-start(bf16[344,512]{1,0:T(8,128)(2,1)} %collective-permute-done.6), channel_id=1, source_target_pairs={{0,8},{1,9},{2,10},{3,11},{4,12},{5,13},{6,14},{7,15},{8,16},{9,17... | collective-permute-start | bytes 1056776 | tf_op jit(solution)/shard_map/ppermute | solution.py:177
  112.1 15.0 %collective-permute-start.4 = (bf16[344,512]{1,0:T(8,128)(2,1)}, bf16[344,512]{1,0:T(8,128)(2,1)S(1)}, u32[]{:S(2)}, u32[]{:S(2)}) collective-permute-start(bf16[344,512]{1,0:T(8,128)(2,1)} %convolution_convert_fusion.1), channel_id=1, source_target_pairs={{0,1},{1,0},{2,3},{3,2},{4,5},{5,4},{6,7},{7,6},{8,9},{9,8},{10,11... | collective-permute-start | bytes 1056776 | tf_op jit(solution)/shard_map/ppermute | solution.py:174
  113.7 14.0 %collective-permute-start.24 = (bf16[344,512]{1,0:T(8,128)(2,1)S(1)}, bf16[344,512]{1,0:T(8,128)(2,1)S(1)}, u32[]{:S(2)}, u32[]{:S(2)}) collective-permute-start(bf16[344,512]{1,0:T(8,128)(2,1)S(1)} %collective-permute-done.21), channel_id=1, source_target_pairs={{8,0},{9,1},{10,2},{11,3},{12,4},{13,5},{14,6},{15,7},{16,8},{17,9... | collective-permute-start | bytes 1056776 | tf_op jit(solution)/shard_map/ppermute | solution.py:180
  115.0 13.1 %collective-permute-start.25 = (bf16[344,512]{1,0:T(8,128)(2,1)S(1)}, bf16[344,512]{1,0:T(8,128)(2,1)S(1)}, u32[]{:S(2)}, u32[]{:S(2)}) collective-permute-start(bf16[344,512]{1,0:T(8,128)(2,1)S(1)} %collective-permute-done.22), channel_id=1, source_target_pairs={{0,8},{1,9},{2,10},{3,11},{4,12},{5,13},{6,14},{7,15},{8,16},{9,17... | collective-permute-start | bytes 1056776 | tf_op jit(solution)/shard_map/ppermute | solution.py:177
  119.6 14.2 %collective-permute-start.11 = (bf16[344,512]{1,0:T(8,128)(2,1)S(1)}, bf16[344,512]{1,0:T(8,128)(2,1)S(1)}, u32[]{:S(2)}, u32[]{:S(2)}) collective-permute-start(bf16[344,512]{1,0:T(8,128)(2,1)S(1)} %collective-permute-done.8), channel_id=1, source_target_pairs={{8,0},{9,1},{10,2},{11,3},{12,4},{13,5},{14,6},{15,7},{16,8},{17,9... | collective-permute-start | bytes 1056776 | tf_op jit(solution)/shard_map/ppermute | solution.py:180
  120.9 14.1 %collective-permute-start.12 = (bf16[344,512]{1,0:T(8,128)(2,1)S(1)}, bf16[344,512]{1,0:T(8,128)(2,1)S(1)}, u32[]{:S(2)}, u32[]{:S(2)}) collective-permute-start(bf16[344,512]{1,0:T(8,128)(2,1)S(1)} %collective-permute-done.9), channel_id=1, source_target_pairs={{0,8},{1,9},{2,10},{3,11},{4,12},{5,13},{6,14},{7,15},{8,16},{9,17... | collective-permute-start | bytes 1056776 | tf_op jit(solution)/shard_map/ppermute | solution.py:177
  129.3 7.9 %collective-permute-start.20 = (bf16[344,512]{1,0:T(8,128)(2,1)S(1)}, bf16[344,512]{1,0:T(8,128)(2,1)S(1)}, u32[]{:S(2)}, u32[]{:S(2)}) collective-permute-start(bf16[344,512]{1,0:T(8,128)(2,1)S(1)} %get-tuple-element.89), channel_id=1, source_target_pairs={{0,1},{1,0},{2,3},{3,2},{4,5},{5,4},{6,7},{7,6},{8,9},{9,8},{10,11... | collective-permute-start | bytes 1056776 | tf_op jit(solution)/shard_map/ppermute | solution.py:174
  129.4 10.0 %collective-permute-start.23 = (bf16[344,512]{1,0:T(8,128)(2,1)S(1)}, bf16[344,512]{1,0:T(8,128)(2,1)S(1)}, u32[]{:S(2)}, u32[]{:S(2)}) collective-permute-start(bf16[344,512]{1,0:T(8,128)(2,1)S(1)} %get-tuple-element.86), channel_id=1, source_target_pairs={{0,1},{1,0},{2,3},{3,2},{4,5},{5,4},{6,7},{7,6},{8,9},{9,8},{10,11... | collective-permute-start | bytes 1056776 | tf_op jit(solution)/shard_map/ppermute | solution.py:174
  129.9 10.6 %collective-permute-start.26 = (bf16[344,512]{1,0:T(8,128)(2,1)S(1)}, bf16[344,512]{1,0:T(8,128)(2,1)S(1)}, u32[]{:S(2)}, u32[]{:S(2)}) collective-permute-start(bf16[344,512]{1,0:T(8,128)(2,1)S(1)} %get-tuple-element.87), channel_id=1, source_target_pairs={{0,1},{1,0},{2,3},{3,2},{4,5},{5,4},{6,7},{7,6},{8,9},{9,8},{10,11... | collective-permute-start | bytes 1056776 | tf_op jit(solution)/shard_map/ppermute | solution.py:174
  136.1 7.0 %collective-permute-start.7 = (bf16[344,512]{1,0:T(8,128)(2,1)S(1)}, bf16[344,512]{1,0:T(8,128)(2,1)S(1)}, u32[]{:S(2)}, u32[]{:S(2)}) collective-permute-start(bf16[344,512]{1,0:T(8,128)(2,1)S(1)} %get-tuple-element.88), channel_id=1, source_target_pairs={{0,1},{1,0},{2,3},{3,2},{4,5},{5,4},{6,7},{7,6},{8,9},{9,8},{10,11... | collective-permute-start | bytes 1056776 | tf_op jit(solution)/shard_map/ppermute | solution.py:174
  136.2 11.2 %collective-permute-start.10 = (bf16[344,512]{1,0:T(8,128)(2,1)S(1)}, bf16[344,512]{1,0:T(8,128)(2,1)S(1)}, u32[]{:S(2)}, u32[]{:S(2)}) collective-permute-start(bf16[344,512]{1,0:T(8,128)(2,1)S(1)} %get-tuple-element.84), channel_id=1, source_target_pairs={{0,1},{1,0},{2,3},{3,2},{4,5},{5,4},{6,7},{7,6},{8,9},{9,8},{10,11... | collective-permute-start | bytes 1056776 | tf_op jit(solution)/shard_map/ppermute | solution.py:174
  137.2 11.3 %collective-permute-start.13 = (bf16[344,512]{1,0:T(8,128)(2,1)S(1)}, bf16[344,512]{1,0:T(8,128)(2,1)S(1)}, u32[]{:S(2)}, u32[]{:S(2)}) collective-permute-start(bf16[344,512]{1,0:T(8,128)(2,1)S(1)} %get-tuple-element.85), channel_id=1, source_target_pairs={{0,1},{1,0},{2,3},{3,2},{4,5},{5,4},{6,7},{7,6},{8,9},{9,8},{10,11... | collective-permute-start | bytes 1056776 | tf_op jit(solution)/shard_map/ppermute | solution.py:174
  141.6 9.5 %collective-permute-start.27 = (bf16[176,512]{1,0:T(8,128)(2,1)S(1)}, bf16[176,512]{1,0:T(8,128)(2,1)S(1)}, u32[]{:S(2)}, u32[]{:S(2)}) collective-permute-start(bf16[176,512]{1,0:T(8,128)(2,1)S(1)} %get-tuple-element.81), channel_id=1, source_target_pairs={{0,2},{1,3},{2,0},{3,1},{4,6},{5,7},{6,4},{7,5},{8,10},{9,11},{10,... | collective-permute-start | bytes 540680 | tf_op jit(solution)/shard_map/ppermute | solution.py:174
  142.2 11.0 %collective-permute-start.28 = (bf16[176,512]{1,0:T(8,128)(2,1)S(1)}, bf16[176,512]{1,0:T(8,128)(2,1)S(1)}, u32[]{:S(2)}, u32[]{:S(2)}) collective-permute-start(bf16[176,512]{1,0:T(8,128)(2,1)S(1)} %get-tuple-element.83), channel_id=1, source_target_pairs={{0,4},{1,5},{2,6},{3,7},{4,0},{5,1},{6,2},{7,3},{8,12},{9,13},{10,... | collective-permute-start | bytes 540680 | tf_op jit(solution)/shard_map/ppermute | solution.py:174
  143.1 10.1 %collective-permute-start.29 = (bf16[176,512]{1,0:T(8,128)(2,1)S(1)}, bf16[176,512]{1,0:T(8,128)(2,1)S(1)}, u32[]{:S(2)}, u32[]{:S(2)}) collective-permute-start(bf16[176,512]{1,0:T(8,128)(2,1)S(1)} %get-tuple-element.82), channel_id=1, source_target_pairs={{0,6},{1,7},{2,4},{3,5},{4,2},{5,3},{6,0},{7,1},{8,14},{9,15},{10,... | collective-permute-start | bytes 540680 | tf_op jit(solution)/shard_map/ppermute | solution.py:174
  149.7 7.6 %collective-permute-start.14 = (bf16[176,512]{1,0:T(8,128)(2,1)S(1)}, bf16[176,512]{1,0:T(8,128)(2,1)S(1)}, u32[]{:S(2)}, u32[]{:S(2)}) collective-permute-start(bf16[176,512]{1,0:T(8,128)(2,1)S(1)} %get-tuple-element.78), channel_id=1, source_target_pairs={{0,2},{1,3},{2,0},{3,1},{4,6},{5,7},{6,4},{7,5},{8,10},{9,11},{10,... | collective-permute-start | bytes 540680 | tf_op jit(solution)/shard_map/ppermute | solution.py:174
  150.2 10.2 %collective-permute-start.15 = (bf16[176,512]{1,0:T(8,128)(2,1)S(1)}, bf16[176,512]{1,0:T(8,128)(2,1)S(1)}, u32[]{:S(2)}, u32[]{:S(2)}) collective-permute-start(bf16[176,512]{1,0:T(8,128)(2,1)S(1)} %get-tuple-element.80), channel_id=1, source_target_pairs={{0,4},{1,5},{2,6},{3,7},{4,0},{5,1},{6,2},{7,3},{8,12},{9,13},{10,... | collective-permute-start | bytes 540680 | tf_op jit(solution)/shard_map/ppermute | solution.py:174
  151.2 9.2 %collective-permute-start.16 = (bf16[176,512]{1,0:T(8,128)(2,1)S(1)}, bf16[176,512]{1,0:T(8,128)(2,1)S(1)}, u32[]{:S(2)}, u32[]{:S(2)}) collective-permute-start(bf16[176,512]{1,0:T(8,128)(2,1)S(1)} %get-tuple-element.79), channel_id=1, source_target_pairs={{0,6},{1,7},{2,4},{3,5},{4,2},{5,3},{6,0},{7,1},{8,14},{9,15},{10,... | collective-permute-start | bytes 540680 | tf_op jit(solution)/shard_map/ppermute | solution.py:174
  160.9 10.2 %collective-permute-start.33 = (bf16[176,1024]{1,0:T(8,128)(2,1)S(1)}, bf16[176,1024]{1,0:T(8,128)(2,1)S(1)}, u32[]{:S(2)}, u32[]{:S(2)}) collective-permute-start(bf16[176,1024]{1,0:T(8,128)(2,1)S(1)} %multiply_convert_fusion.1.refs_1_.refs_5_), channel_id=1, source_target_pairs={{0,8},{1,9},{2,10},{3,11},{4,12},{5,13},{6,14},{7,15},{8,0},{9,1},... | collective-permute-start | bytes 1081352 | tf_op jit(solution)/shard_map/ppermute | solution.py:174
  163.5 9.1 %collective-permute-start.30 = (bf16[176,1024]{1,0:T(8,128)(2,1)S(1)}, bf16[176,1024]{1,0:T(8,128)(2,1)S(1)}, u32[]{:S(2)}, u32[]{:S(2)}) collective-permute-start(bf16[176,1024]{1,0:T(8,128)(2,1)S(1)} %multiply_convert_fusion.1.refs_1_.refs_5_), channel_id=1, source_target_pairs={{0,2},{1,3},{2,0},{3,1},{4,6},{5,7},{6,4},{7,5},{8,10},{9,11},{10,... | collective-permute-start | bytes 1081352 | tf_op jit(solution)/shard_map/ppermute | solution.py:174
  165.0 11.3 %collective-permute-start.31 = (bf16[176,1024]{1,0:T(8,128)(2,1)S(1)}, bf16[176,1024]{1,0:T(8,128)(2,1)S(1)}, u32[]{:S(2)}, u32[]{:S(2)}) collective-permute-start(bf16[176,1024]{1,0:T(8,128)(2,1)S(1)} %multiply_convert_fusion.1.refs_1_.refs_5_), channel_id=1, source_target_pairs={{0,4},{1,5},{2,6},{3,7},{4,0},{5,1},{6,2},{7,3},{8,12},{9,13},{10,... | collective-permute-start | bytes 1081352 | tf_op jit(solution)/shard_map/ppermute | solution.py:174
  171.1 11.3 %collective-permute-start.35 = (bf16[176,1024]{1,0:T(8,128)(2,1)S(1)}, bf16[176,1024]{1,0:T(8,128)(2,1)S(1)}, u32[]{:S(2)}, u32[]{:S(2)}) collective-permute-start(bf16[176,1024]{1,0:T(8,128)(2,1)S(1)} %collective-permute-done.33.refs_1_.refs_9_), channel_id=1, source_target_pairs={{0,4},{1,5},{2,6},{3,7},{4,0},{5,1},{6,2},{7,3},{8,12},{9,13},{10,... | collective-permute-start | bytes 1081352 | tf_op jit(solution)/shard_map/ppermute | solution.py:174
  172.6 16.2 %collective-permute-start.32 = (bf16[176,1024]{1,0:T(8,128)(2,1)S(1)}, bf16[176,1024]{1,0:T(8,128)(2,1)S(1)}, u32[]{:S(2)}, u32[]{:S(2)}) collective-permute-start(bf16[176,1024]{1,0:T(8,128)(2,1)S(1)} %collective-permute-done.30.refs_2_.refs_6_), channel_id=1, source_target_pairs={{0,4},{1,5},{2,6},{3,7},{4,0},{5,1},{6,2},{7,3},{8,12},{9,13},{10,... | collective-permute-start | bytes 1081352 | tf_op jit(solution)/shard_map/ppermute | solution.py:174
  174.0 18.5 %collective-permute-start.40 = (bf16[176,1024]{1,0:T(8,128)(2,1)S(1)}, bf16[176,1024]{1,0:T(8,128)(2,1)S(1)}, u32[]{:S(2)}, u32[]{:S(2)}) collective-permute-start(bf16[176,1024]{1,0:T(8,128)(2,1)S(1)} %multiply_convert_fusion.1.refs_1_.refs_5_), channel_id=1, source_target_pairs={{0,24},{1,25},{2,26},{3,27},{4,28},{5,29},{6,30},{7,31},{8,16},{9,... | collective-permute-start | bytes 1081352 | tf_op jit(solution)/shard_map/ppermute | solution.py:174
  175.2 30.1 %collective-permute-start.37 = (bf16[176,1024]{1,0:T(8,128)(2,1)S(1)}, bf16[176,1024]{1,0:T(8,128)(2,1)S(1)}, u32[]{:S(2)}, u32[]{:S(2)}) collective-permute-start(bf16[176,1024]{1,0:T(8,128)(2,1)S(1)} %multiply_convert_fusion.1.refs_1_.refs_5_), channel_id=1, source_target_pairs={{0,16},{1,17},{2,18},{3,19},{4,20},{5,21},{6,22},{7,23},{8,24},{9,... | collective-permute-start | bytes 1081352 | tf_op jit(solution)/shard_map/ppermute | solution.py:174
  176.3 29.5 %collective-permute-start.34 = (bf16[176,1024]{1,0:T(8,128)(2,1)S(1)}, bf16[176,1024]{1,0:T(8,128)(2,1)S(1)}, u32[]{:S(2)}, u32[]{:S(2)}) collective-permute-start(bf16[176,1024]{1,0:T(8,128)(2,1)S(1)} %collective-permute-done.33.refs_1_.refs_9_), channel_id=1, source_target_pairs={{0,2},{1,3},{2,0},{3,1},{4,6},{5,7},{6,4},{7,5},{8,10},{9,11},{10,... | collective-permute-start | bytes 1081352 | tf_op jit(solution)/shard_map/ppermute | solution.py:174
  182.5 25.1 %collective-permute-start.36 = (bf16[176,1024]{1,0:T(8,128)(2,1)S(1)}, bf16[176,1024]{1,0:T(8,128)(2,1)S(1)}, u32[]{:S(2)}, u32[]{:S(2)}) collective-permute-start(bf16[176,1024]{1,0:T(8,128)(2,1)S(1)} %collective-permute-done.35.refs_3_.refs_11_), channel_id=1, source_target_pairs={{0,2},{1,3},{2,0},{3,1},{4,6},{5,7},{6,4},{7,5},{8,10},{9,11},{10,... | collective-permute-start | bytes 1081352 | tf_op jit(solution)/shard_map/ppermute | solution.py:174
  192.5 25.8 %collective-permute-start.41 = (bf16[176,1024]{1,0:T(8,128)(2,1)S(1)}, bf16[176,1024]{1,0:T(8,128)(2,1)S(1)}, u32[]{:S(2)}, u32[]{:S(2)}) collective-permute-start(bf16[176,1024]{1,0:T(8,128)(2,1)S(1)} %collective-permute-done.40.refs_4_.refs_16_), channel_id=1, source_target_pairs={{0,2},{1,3},{2,0},{3,1},{4,6},{5,7},{6,4},{7,5},{8,10},{9,11},{10,... | collective-permute-start | bytes 1081352 | tf_op jit(solution)/shard_map/ppermute | solution.py:174
  193.6 17.9 %collective-permute-start.42 = (bf16[176,1024]{1,0:T(8,128)(2,1)S(1)}, bf16[176,1024]{1,0:T(8,128)(2,1)S(1)}, u32[]{:S(2)}, u32[]{:S(2)}) collective-permute-start(bf16[176,1024]{1,0:T(8,128)(2,1)S(1)} %collective-permute-done.40.refs_4_.refs_16_), channel_id=1, source_target_pairs={{0,4},{1,5},{2,6},{3,7},{4,0},{5,1},{6,2},{7,3},{8,12},{9,13},{10,... | collective-permute-start | bytes 1081352 | tf_op jit(solution)/shard_map/ppermute | solution.py:174
  205.4 10.0 %collective-permute-start.38 = (bf16[176,1024]{1,0:T(8,128)(2,1)S(1)}, bf16[176,1024]{1,0:T(8,128)(2,1)S(1)}, u32[]{:S(2)}, u32[]{:S(2)}) collective-permute-start(bf16[176,1024]{1,0:T(8,128)(2,1)S(1)} %collective-permute-done.37.refs_1_.refs_13_), channel_id=1, source_target_pairs={{0,2},{1,3},{2,0},{3,1},{4,6},{5,7},{6,4},{7,5},{8,10},{9,11},{10,... | collective-permute-start | bytes 1081352 | tf_op jit(solution)/shard_map/ppermute | solution.py:174
  205.8 12.5 %collective-permute-start.39 = (bf16[176,1024]{1,0:T(8,128)(2,1)S(1)}, bf16[176,1024]{1,0:T(8,128)(2,1)S(1)}, u32[]{:S(2)}, u32[]{:S(2)}) collective-permute-start(bf16[176,1024]{1,0:T(8,128)(2,1)S(1)} %collective-permute-done.37.refs_1_.refs_13_), channel_id=1, source_target_pairs={{0,4},{1,5},{2,6},{3,7},{4,0},{5,1},{6,2},{7,3},{8,12},{9,13},{10,... | collective-permute-start | bytes 1081352 | tf_op jit(solution)/shard_map/ppermute | solution.py:174
  211.4 12.7 %collective-permute-start.44 = (bf16[176,1024]{1,0:T(8,128)(2,1)S(1)}, bf16[176,1024]{1,0:T(8,128)(2,1)S(1)}, u32[]{:S(2)}, u32[]{:S(2)}) collective-permute-start(bf16[176,1024]{1,0:T(8,128)(2,1)S(1)} %collective-permute-done.42.refs_6_.refs_18_), channel_id=1, source_target_pairs={{0,2},{1,3},{2,0},{3,1},{4,6},{5,7},{6,4},{7,5},{8,10},{9,11},{10,... | collective-permute-start | bytes 1081352 | tf_op jit(solution)/shard_map/ppermute | solution.py:174
  215.3 8.8 %collective-permute-start.43 = (bf16[176,1024]{1,0:T(8,128)(2,1)S(1)}, bf16[176,1024]{1,0:T(8,128)(2,1)S(1)}, u32[]{:S(2)}, u32[]{:S(2)}) collective-permute-start(bf16[176,1024]{1,0:T(8,128)(2,1)S(1)} %collective-permute-done.38.refs_2_.refs_14_), channel_id=1, source_target_pairs={{0,4},{1,5},{2,6},{3,7},{4,0},{5,1},{6,2},{7,3},{8,12},{9,13},{10,... | collective-permute-start | bytes 1081352 | tf_op jit(solution)/shard_map/ppermute | solution.py:174
  233.9 4.8 %collective-permute-start.49 = (f32[4,4,176]{2,1,0:T(4,128)S(1)}, f32[4,4,176]{2,1,0:T(4,128)S(1)}, u32[]{:S(2)}, u32[]{:S(2)}) collective-permute-start(f32[4,4,176]{2,1,0:T(4,128)S(1)} %log_add_fusion.1), channel_id=1, source_target_pairs={{0,16},{1,17},{2,18},{3,19},{4,20},{5,21},{6,22},{7,23},{8,24},{9,... | collective-permute-start | bytes 33800 | tf_op jit(solution)/shard_map/ppermute | solution.py:174
  236.0 5.5 %collective-permute-start.50 = (f32[4,4,176]{2,1,0:T(4,128)S(1)}, f32[4,4,176]{2,1,0:T(4,128)S(1)}, u32[]{:S(2)}, u32[]{:S(2)}) collective-permute-start(f32[4,4,176]{2,1,0:T(4,128)S(1)} %log_add_fusion.1), channel_id=1, source_target_pairs={{0,24},{1,25},{2,26},{3,27},{4,28},{5,29},{6,30},{7,31},{8,16},{9,... | collective-permute-start | bytes 33800 | tf_op jit(solution)/shard_map/ppermute | solution.py:174
  (39 other events, 354.1 us)

commit v3 on v2

--- a/solution.py
+++ b/solution.py
@@ -263,7 +263,7 @@
             scored.append(score(pair, blocks))
 
         first = spread(embed)
-        lined = [None] + [hop(embed if k < 3 else after(embed, first[1]), k * PLANE) for k in range(1, lines)]
+        lined = [None] + [hop(embed, k * PLANE) for k in range(1, lines)]
         take(first + [hop(first[1], 4)], [(0, q) for q in (0, 1, 2, 3)])
         late, late_names, ends, end_names = [], [], [], []
         for k in range(1, lines):

time: 262 us -> 262 us (level)
  no operation moved by 1% of the time
where the time goes in v3:
time: 262 us; the launch traced here: 261 us
  starting transfers between devices  87.4 us (33%)
  waiting for transfers between devices  81.9 us (31%)
  Pallas kernels  25.7 us (10%)
  local copies, waits for them, and re-layouts  23 us (9%)
  matrix products  22.4 us (9%)
  other arithmetic  19.5 us (7%)
    ppermute x41, waiting for transfers between devices, hop(): return lax.ppermute(v, 'dp', [(i, i ^ k) for i in range(n)])  43.6 us
    ppermute x41, starting transfers between devices, hop(): return lax.ppermute(v, 'dp', [(i, i ^ k) for i in range(n)])  43.5 us
    all_to_all x1, waiting for transfers between devices, body(): down_rows = lax.all_to_all(down_weight, 'dp', 0, 1, tiled=True)  31.6 us
    ppermute x6, starting transfers between devices, up(): return lax.ppermute(v, 'dp', [(i, i + PLANE) for i in range(n - PLANE)])  28.8 us
    dot_general x19, matrix products, dot(): return jnp.dot(a, b, preferred_element_type=F32)  22.4 us
    pallas_call x1, Pallas kernels, weigh(): pl.pallas_call(lambda *refs: weigh_kernel(sizes, scale, tiles, *refs), gr...  12.6 us
    pallas_call x4, Pallas kernels, score(): pl.pallas_call(lambda *refs: score_kernel(1.0 / (math.sqrt(width) * 0.05)...  11.1 us
    unnamed x69, local copies, waits for them, and re-layouts  10.6 us
  transfers between devices with their start and end apart: 54, of which 20 were waited for; matrix products, arithmetic and copies ran while one was open for 18% of the time, Pallas kernels for 4%

profile of v3, /device:TPU:0, one launch (start us, length us, event | category | flops | bytes accessed | tf_op | source)
XLA Modules:
  0.0 261.4 jit_solution(9340187749276607607)
XLA Ops:
  0.6 7.4 %all-to-all-start = ((bf16[32,344,128]{2,1,0:T(8,128)(2,1)}), bf16[32,344,128]{2,1,0:T(8,128)(2,1)}, u32[]{:S(2)}, u32[]{:S(2)}) async-start(bf16[32,344,128]{2,1,0:T(8,128)(2,1)} %bitcast.126), calls=%async_computation | async-start | bytes 5636096 | tf_op jit(solution)/shard_map/all_to_all | solution.py:217
  9.5 2.6 fusion.28.position
  12.1 2.1 copy-done.2
  14.2 2.0 shard_map.86
  16.2 2.2 fusion.36
  18.4 1.7 collective-permute-start.1
  21.6 8.2 %multiply_convert_fusion = bf16[4096,1024]{1,0:T(8,128)(2,1)} fusion(bf16[4096,1024]{1,0:T(8,128)(2,1)} %param.11, f32[4096]{0:T(1024)S(1)} %copy-done.32), kind=kLoop, calls=%fused_computation | loop fusion | flops 12582912 | bytes 16793600 | tf_op jit(solution)/shard_map/convert_element_type | solution.py:220
  29.7 6.0 %convolution_bitcast_fusion = f32[176,1024]{1,0:T(8,128)} fusion(bf16[176,4096]{1,0:T(8,128)(2,1)S(1)} %copy-done, bf16[4096,1024]{1,0:T(8,128)(2,1)} %multiply_convert_fusion), kind=kOutput, calls=%fused_computation.18 | convolution fusion | flops 1476395008 | bytes 10551296 | tf_op jit(solution)/shard_map/dot_general | solution.py:18
  35.8 3.9 %fusion.35 = (bf16[4096,512]{1,0:T(8,128)(2,1)}, bf16[4096,512]{1,0:T(8,128)(2,1)}) fusion(bf16[4096,1024]{1,0:T(8,128)(2,1)S(1)} %copy-done.23), kind=kLoop, calls=%fused_computation.119 | loop fusion | bytes 16777216 | tf_op jit(solution)/shard_map/slice | solution.py:226
  41.1 31.6 %all-to-all-done = bf16[32,344,128]{2,1,0:T(8,128)(2,1)} async-done(((bf16[32,344,128]{2,1,0:T(8,128)(2,1)}), bf16[32,344,128]{2,1,0:T(8,128)(2,1)}, u32[]{:S(2)}, u32[]{:S(2)}) %all-to-all-start) | async-done | bytes 2818080 | tf_op jit(solution)/shard_map/all_to_all | solution.py:217
  72.7 2.3 copy_bitcast_fusion
  75.7 2.4 convolution_convert_fusion.1
  78.1 2.4 convolution_convert_fusion
  80.4 2.0 collective-permute-start.3
  83.8 5.3 %collective-permute-start.19 = (bf16[344,512]{1,0:T(8,128)(2,1)}, bf16[344,512]{1,0:T(8,128)(2,1)}, u32[]{:S(2)}, u32[]{:S(2)}) collective-permute-start(bf16[344,512]{1,0:T(8,128)(2,1)} %convolution_convert_fusion), channel_id=1, source_target_pairs={{0,8},{1,9},{2,10},{3,11},{4,12},{5,13},{6,14},{7,15},{8,16},{9,17... | collective-permute-start | bytes 1056776 | tf_op jit(solution)/shard_map/ppermute | solution.py:177
  90.4 5.3 %collective-permute-start.6 = (bf16[344,512]{1,0:T(8,128)(2,1)}, bf16[344,512]{1,0:T(8,128)(2,1)}, u32[]{:S(2)}, u32[]{:S(2)}) collective-permute-start(bf16[344,512]{1,0:T(8,128)(2,1)} %convolution_convert_fusion.1), channel_id=1, source_target_pairs={{0,8},{1,9},{2,10},{3,11},{4,12},{5,13},{6,14},{7,15},{8,16},{9,17... | collective-permute-start | bytes 1056776 | tf_op jit(solution)/shard_map/ppermute | solution.py:177
  97.2 4.5 %collective-permute-start.22 = (bf16[344,512]{1,0:T(8,128)(2,1)}, bf16[344,512]{1,0:T(8,128)(2,1)S(1)}, u32[]{:S(2)}, u32[]{:S(2)}) collective-permute-start(bf16[344,512]{1,0:T(8,128)(2,1)} %collective-permute-done.19), channel_id=1, source_target_pairs={{0,8},{1,9},{2,10},{3,11},{4,12},{5,13},{6,14},{7,15},{8,16},{9,17... | collective-permute-start | bytes 1056776 | tf_op jit(solution)/shard_map/ppermute | solution.py:177
  104.8 4.4 %collective-permute-start.9 = (bf16[344,512]{1,0:T(8,128)(2,1)}, bf16[344,512]{1,0:T(8,128)(2,1)S(1)}, u32[]{:S(2)}, u32[]{:S(2)}) collective-permute-start(bf16[344,512]{1,0:T(8,128)(2,1)} %collective-permute-done.6), channel_id=1, source_target_pairs={{0,8},{1,9},{2,10},{3,11},{4,12},{5,13},{6,14},{7,15},{8,16},{9,17... | collective-permute-start | bytes 1056776 | tf_op jit(solution)/shard_map/ppermute | solution.py:177
  115.0 4.6 %collective-permute-start.25 = (bf16[344,512]{1,0:T(8,128)(2,1)S(1)}, bf16[344,512]{1,0:T(8,128)(2,1)S(1)}, u32[]{:S(2)}, u32[]{:S(2)}) collective-permute-start(bf16[344,512]{1,0:T(8,128)(2,1)S(1)} %collective-permute-done.22), channel_id=1, source_target_pairs={{0,8},{1,9},{2,10},{3,11},{4,12},{5,13},{6,14},{7,15},{8,16},{9,17... | collective-permute-start | bytes 1056776 | tf_op jit(solution)/shard_map/ppermute | solution.py:177
  120.9 4.7 %collective-permute-start.12 = (bf16[344,512]{1,0:T(8,128)(2,1)S(1)}, bf16[344,512]{1,0:T(8,128)(2,1)S(1)}, u32[]{:S(2)}, u32[]{:S(2)}) collective-permute-start(bf16[344,512]{1,0:T(8,128)(2,1)S(1)} %collective-permute-done.9), channel_id=1, source_target_pairs={{0,8},{1,9},{2,10},{3,11},{4,12},{5,13},{6,14},{7,15},{8,16},{9,17... | collective-permute-start | bytes 1056776 | tf_op jit(solution)/shard_map/ppermute | solution.py:177
  130.5 3.2 %collective-permute-done.11 = bf16[344,512]{1,0:T(8,128)(2,1)S(1)} collective-permute-done((bf16[344,512]{1,0:T(8,128)(2,1)S(1)}, bf16[344,512]{1,0:T(8,128)(2,1)S(1)}, u32[]{:S(2)}, u32[]{:S(2)}) %collective-permute-start.11) | collective-permute-done | bytes 352288 | tf_op jit(solution)/shard_map/ppermute | solution.py:180
  137.9 1.5 fusion.5
  143.1 2.0 collective-permute-start.29
  145.7 1.6 fusion.1
  151.2 2.0 collective-permute-start.16
  153.2 4.0 %collective-permute-done.14 = bf16[176,512]{1,0:T(8,128)(2,1)S(1)} collective-permute-done((bf16[176,512]{1,0:T(8,128)(2,1)S(1)}, bf16[176,512]{1,0:T(8,128)(2,1)S(1)}, u32[]{:S(2)}, u32[]{:S(2)}) %collective-permute-start.14) | collective-permute-done | bytes 180256 | tf_op jit(solution)/shard_map/ppermute | solution.py:174
  157.2 3.2 %collective-permute-done.15 = bf16[176,512]{1,0:T(8,128)(2,1)S(1)} collective-permute-done((bf16[176,512]{1,0:T(8,128)(2,1)S(1)}, bf16[176,512]{1,0:T(8,128)(2,1)S(1)}, u32[]{:S(2)}, u32[]{:S(2)}) %collective-permute-start.15) | collective-permute-done | bytes 180256 | tf_op jit(solution)/shard_map/ppermute | solution.py:174
  160.9 2.5 collective-permute-start.33
  163.5 1.6 collective-permute-start.30
  165.5 5.6 %collective-permute-done.33.refs_1_.refs_9_ = bf16[176,1024]{1,0:T(8,128)(2,1)S(1)} collective-permute-done((bf16[176,1024]{1,0:T(8,128)(2,1)S(1)}, bf16[176,1024]{1,0:T(8,128)(2,1)S(1)}, u32[]{:S(2)}, u32[]{:S(2)}) %collective-permute-start.33) | collective-permute-done | bytes 360480 | tf_op jit(solution)/shard_map/ppermute | solution.py:174
  177.3 5.1 %collective-permute-done.35.refs_3_.refs_11_ = bf16[176,1024]{1,0:T(8,128)(2,1)S(1)} collective-permute-done((bf16[176,1024]{1,0:T(8,128)(2,1)S(1)}, bf16[176,1024]{1,0:T(8,128)(2,1)S(1)}, u32[]{:S(2)}, u32[]{:S(2)}) %collective-permute-start.35) | collective-permute-done | bytes 360480 | tf_op jit(solution)/shard_map/ppermute | solution.py:174
  183.7 5.0 %collective-permute-done.32.refs_4_.refs_8_ = bf16[176,1024]{1,0:T(8,128)(2,1)S(1)} collective-permute-done((bf16[176,1024]{1,0:T(8,128)(2,1)S(1)}, bf16[176,1024]{1,0:T(8,128)(2,1)S(1)}, u32[]{:S(2)}, u32[]{:S(2)}) %collective-permute-start.32) | collective-permute-done | bytes 360480 | tf_op jit(solution)/shard_map/ppermute | solution.py:174
  188.7 2.6 %shard_map.87 = (bf16[1024,768]{1,0:T(8,128)(2,1)S(1)}, f32[1,768]{1,0:T(1,128)S(1)}, f32[1,768]{1,0:T(1,128)S(1)}) custom-call(bf16[1024,1024]{1,0:T(8,128)(2,1)S(1)} %pad_maximum_fusion.refs_0_, bf16[176,1024]{1,0:T(8,128)(2,1)S(1)} %multiply_convert_fusion.1.refs_1_.refs_5_, bf16[176,1024]{1,0:T(8,128)(2,1)S(1)} %collective-permute-done.30.refs_2_.refs_6_, ...), custom_call_target="tpu_custom_call" | custom-call | flops 1610612736 | bytes 5242880 | tf_op jit(solution)/shard_map/pallas_call | solution.py:53
  195.0 10.4 %collective-permute-done.37.refs_1_.refs_13_ = bf16[176,1024]{1,0:T(8,128)(2,1)S(1)} collective-permute-done((bf16[176,1024]{1,0:T(8,128)(2,1)S(1)}, bf16[176,1024]{1,0:T(8,128)(2,1)S(1)}, u32[]{:S(2)}, u32[]{:S(2)}) %collective-permute-start.37) | collective-permute-done | bytes 360480 | tf_op jit(solution)/shard_map/ppermute | solution.py:174
  205.8 1.7 collective-permute-start.39
  207.6 2.6 shard_map.88
  211.4 1.5 collective-permute-start.44
  213.0 2.4 collective-permute-done.38.refs_2_.refs_14_
  215.3 3.0 %collective-permute-start.43 = (bf16[176,1024]{1,0:T(8,128)(2,1)S(1)}, bf16[176,1024]{1,0:T(8,128)(2,1)S(1)}, u32[]{:S(2)}, u32[]{:S(2)}) collective-permute-start(bf16[176,1024]{1,0:T(8,128)(2,1)S(1)} %collective-permute-done.38.refs_2_.refs_14_), channel_id=1, source_target_pairs={{0,4},{1,5},{2,6},{3,7},{4,0},{5,1},{6,2},{7,3},{8,12},{9,13},{10,... | collective-permute-start | bytes 1081352 | tf_op jit(solution)/shard_map/ppermute | solution.py:174
  218.4 4.1 %shard_map.89 = (bf16[1024,1152]{1,0:T(8,128)(2,1)S(1)}, f32[1,1152]{1,0:T(1,128)S(1)}, f32[1,1152]{1,0:T(1,128)S(1)}) custom-call(bf16[1024,1024]{1,0:T(8,128)(2,1)S(1)} %pad_maximum_fusion.refs_0_, bf16[176,1024]{1,0:T(8,128)(2,1)S(1)} %collective-permute-done.37.refs_1_.refs_13_, bf16[176,1024]{1,0:T(8,128)(2,1)S(1)} %collective-permute-done.38.refs_2_.refs_14_, ...), custom_call_target="tpu_custom_call" | custom-call | flops 2415919104 | bytes 6815744 | tf_op jit(solution)/shard_map/pallas_call | solution.py:53
  224.1 1.8 shard_map.90
  227.5 1.6 collective-permute-start.46
  231.3 2.5 collective-permute-done.47
  234.4 1.6 collective-permute-start.48
  236.0 2.4 collective-permute-start.50
  238.8 2.8 %collective-permute-done.50 = f32[4,4,176]{2,1,0:T(4,128)S(1)} collective-permute-done((f32[4,4,176]{2,1,0:T(4,128)S(1)}, f32[4,4,176]{2,1,0:T(4,128)S(1)}, u32[]{:S(2)}, u32[]{:S(2)}) %collective-permute-start.50) | collective-permute-done | bytes 11296 | tf_op jit(solution)/shard_map/ppermute | solution.py:174
  242.4 12.6 %shard_map.91 = (bf16[512,1024]{1,0:T(8,128)(2,1)}, bf16[512,1024]{1,0:T(8,128)(2,1)}, f32[1,1024]{1,0:T(1,128)}) custom-call(f32[1,3072]{1,0:T(1,128)} %fusion.26.refs_0_, bf16[1024,768]{1,0:T(8,128)(2,1)} %copy-done.20, bf16[1024,768]{1,0:T(8,128)(2,1)} %copy-done.21, bf16[1024,1152]{1,0:T(8,128)(2,1)} %copy-done.22, bf16[1024,384]{1,0:T(8,128)(2,1)} %copy-done.19, ...), custom_call_target="tpu_custom_call" | custom-call | flops 6442450944 | bytes 20971520 | tf_op jit(solution)/shard_map/pallas_call | solution.py:116
  258.4 3.0 %convert_add_fusion = f32[512,1024]{1,0:T(8,128)} fusion(bf16[512,1024]{1,0:T(8,128)(2,1)S(1)} %collective-permute-done.51, bf16[512,1024]{1,0:T(8,128)(2,1)} %get-tuple-element.65), kind=kLoop, calls=%fused_computation.3 | loop fusion | flops 1572864 | bytes 4194304 | tf_op jit(solution)/shard_map/add | solution.py:305
  (195 shorter events, 60.5 us)
Async XLA Ops:
  0.6 72.0 %all-to-all-start = ((bf16[32,344,128]{2,1,0:T(8,128)(2,1)}), bf16[32,344,128]{2,1,0:T(8,128)(2,1)}, u32[]{:S(2)}, u32[]{:S(2)}) async-start(bf16[32,344,128]{2,1,0:T(8,128)(2,1)} %bitcast.126), calls=%async_computation | async-start | bytes 5636096 | tf_op jit(solution)/shard_map/all_to_all | solution.py:217
  18.4 56.6 %collective-permute-start.1 = (bf16[4,2,176,344]{3,2,1,0:T(8,128)(2,1)}, bf16[4,2,176,344]{3,2,1,0:T(8,128)(2,1)}, u32[]{:S(2)}, u32[]{:S(2)}) collective-permute-start(bf16[4,2,176,344]{3,2,1,0:T(8,128)(2,1)} %bitcast.10), channel_id=1, source_target_pairs={{0,2},{1,3},{2,0},{3,1},{4,6},{5,7},{6,4},{7,5},{8,10},{9,11},{10,... | collective-permute-start | bytes 2906120 | tf_op jit(solution)/shard_map/ppermute | solution.py:174
  20.1 54.9 %collective-permute-start.2 = (bf16[4,2,176,344]{3,2,1,0:T(8,128)(2,1)}, bf16[4,2,176,344]{3,2,1,0:T(8,128)(2,1)}, u32[]{:S(2)}, u32[]{:S(2)}) collective-permute-start(bf16[4,2,176,344]{3,2,1,0:T(8,128)(2,1)} %bitcast.11), channel_id=1, source_target_pairs={{0,4},{1,5},{2,6},{3,7},{4,0},{5,1},{6,2},{7,3},{8,12},{9,13},{10,... | collective-permute-start | bytes 2906120 | tf_op jit(solution)/shard_map/ppermute | solution.py:174
  21.6 18.1 %collective-permute-start = (bf16[512,1024]{1,0:T(8,128)(2,1)S(1)}, bf16[512,1024]{1,0:T(8,128)(2,1)}, u32[]{:S(2)}, u32[]{:S(2)}) collective-permute-start(bf16[512,1024]{1,0:T(8,128)(2,1)S(1)} %copy-done.27), channel_id=1, source_target_pairs={{0,1},{1,0},{2,3},{3,2},{4,5},{5,4},{6,7},{7,6},{8,9},{9,8},{10,11... | collective-permute-start | bytes 3145736 | tf_op jit(solution)/shard_map/ppermute | solution.py:174
  80.4 9.9 %collective-permute-start.17 = (bf16[344,512]{1,0:T(8,128)(2,1)}, bf16[344,512]{1,0:T(8,128)(2,1)}, u32[]{:S(2)}, u32[]{:S(2)}) collective-permute-start(bf16[344,512]{1,0:T(8,128)(2,1)} %convolution_convert_fusion), channel_id=1, source_target_pairs={{0,1},{1,0},{2,3},{3,2},{4,5},{5,4},{6,7},{7,6},{8,9},{9,8},{10,11... | collective-permute-start | bytes 1056776 | tf_op jit(solution)/shard_map/ppermute | solution.py:174
  80.4 31.7 %collective-permute-start.3 = (bf16[4,2,176,344]{3,2,1,0:T(8,128)(2,1)}, bf16[4,2,176,344]{3,2,1,0:T(8,128)(2,1)}, u32[]{:S(2)}, u32[]{:S(2)}) collective-permute-start(bf16[4,2,176,344]{3,2,1,0:T(8,128)(2,1)} %bitcast.8), channel_id=1, source_target_pairs={{0,6},{1,7},{2,4},{3,5},{4,2},{5,3},{6,0},{7,1},{8,14},{9,15},{10,... | collective-permute-start | bytes 2906120 | tf_op jit(solution)/shard_map/ppermute | solution.py:174
  82.5 13.3 %collective-permute-start.18 = (bf16[344,512]{1,0:T(8,128)(2,1)}, bf16[344,512]{1,0:T(8,128)(2,1)}, u32[]{:S(2)}, u32[]{:S(2)}) collective-permute-start(bf16[344,512]{1,0:T(8,128)(2,1)} %convolution_convert_fusion), channel_id=1, source_target_pairs={{8,0},{9,1},{10,2},{11,3},{12,4},{13,5},{14,6},{15,7},{16,8},{17,9... | collective-permute-start | bytes 1056776 | tf_op jit(solution)/shard_map/ppermute | solution.py:180
  83.8 13.5 %collective-permute-start.19 = (bf16[344,512]{1,0:T(8,128)(2,1)}, bf16[344,512]{1,0:T(8,128)(2,1)}, u32[]{:S(2)}, u32[]{:S(2)}) collective-permute-start(bf16[344,512]{1,0:T(8,128)(2,1)} %convolution_convert_fusion), channel_id=1, source_target_pairs={{0,8},{1,9},{2,10},{3,11},{4,12},{5,13},{6,14},{7,15},{8,16},{9,17... | collective-permute-start | bytes 1056776 | tf_op jit(solution)/shard_map/ppermute | solution.py:177
  89.1 14.1 %collective-permute-start.5 = (bf16[344,512]{1,0:T(8,128)(2,1)}, bf16[344,512]{1,0:T(8,128)(2,1)S(1)}, u32[]{:S(2)}, u32[]{:S(2)}) collective-permute-start(bf16[344,512]{1,0:T(8,128)(2,1)} %convolution_convert_fusion.1), channel_id=1, source_target_pairs={{8,0},{9,1},{10,2},{11,3},{12,4},{13,5},{14,6},{15,7},{16,8},{17,9... | collective-permute-start | bytes 1056776 | tf_op jit(solution)/shard_map/ppermute | solution.py:180
  90.4 14.4 %collective-permute-start.6 = (bf16[344,512]{1,0:T(8,128)(2,1)}, bf16[344,512]{1,0:T(8,128)(2,1)}, u32[]{:S(2)}, u32[]{:S(2)}) collective-permute-start(bf16[344,512]{1,0:T(8,128)(2,1)} %convolution_convert_fusion.1), channel_id=1, source_target_pairs={{0,8},{1,9},{2,10},{3,11},{4,12},{5,13},{6,14},{7,15},{8,16},{9,17... | collective-permute-start | bytes 1056776 | tf_op jit(solution)/shard_map/ppermute | solution.py:177
  95.8 17.8 %collective-permute-start.21 = (bf16[344,512]{1,0:T(8,128)(2,1)}, bf16[344,512]{1,0:T(8,128)(2,1)S(1)}, u32[]{:S(2)}, u32[]{:S(2)}) collective-permute-start(bf16[344,512]{1,0:T(8,128)(2,1)} %collective-permute-done.18), channel_id=1, source_target_pairs={{8,0},{9,1},{10,2},{11,3},{12,4},{13,5},{14,6},{15,7},{16,8},{17,9... | collective-permute-start | bytes 1056776 | tf_op jit(solution)/shard_map/ppermute | solution.py:180
  97.2 17.7 %collective-permute-start.22 = (bf16[344,512]{1,0:T(8,128)(2,1)}, bf16[344,512]{1,0:T(8,128)(2,1)S(1)}, u32[]{:S(2)}, u32[]{:S(2)}) collective-permute-start(bf16[344,512]{1,0:T(8,128)(2,1)} %collective-permute-done.19), channel_id=1, source_target_pairs={{0,8},{1,9},{2,10},{3,11},{4,12},{5,13},{6,14},{7,15},{8,16},{9,17... | collective-permute-start | bytes 1056776 | tf_op jit(solution)/shard_map/ppermute | solution.py:177
  103.2 16.4 %collective-permute-start.8 = (bf16[344,512]{1,0:T(8,128)(2,1)S(1)}, bf16[344,512]{1,0:T(8,128)(2,1)S(1)}, u32[]{:S(2)}, u32[]{:S(2)}) collective-permute-start(bf16[344,512]{1,0:T(8,128)(2,1)S(1)} %collective-permute-done.5), channel_id=1, source_target_pairs={{8,0},{9,1},{10,2},{11,3},{12,4},{13,5},{14,6},{15,7},{16,8},{17,9... | collective-permute-start | bytes 1056776 | tf_op jit(solution)/shard_map/ppermute | solution.py:180
  104.8 16.1 %collective-permute-start.9 = (bf16[344,512]{1,0:T(8,128)(2,1)}, bf16[344,512]{1,0:T(8,128)(2,1)S(1)}, u32[]{:S(2)}, u32[]{:S(2)}) collective-permute-start(bf16[344,512]{1,0:T(8,128)(2,1)} %collective-permute-done.6), channel_id=1, source_target_pairs={{0,8},{1,9},{2,10},{3,11},{4,12},{5,13},{6,14},{7,15},{8,16},{9,17... | collective-permute-start | bytes 1056776 | tf_op jit(solution)/shard_map/ppermute | solution.py:177
  112.1 15.0 %collective-permute-start.4 = (bf16[344,512]{1,0:T(8,128)(2,1)}, bf16[344,512]{1,0:T(8,128)(2,1)S(1)}, u32[]{:S(2)}, u32[]{:S(2)}) collective-permute-start(bf16[344,512]{1,0:T(8,128)(2,1)} %convolution_convert_fusion.1), channel_id=1, source_target_pairs={{0,1},{1,0},{2,3},{3,2},{4,5},{5,4},{6,7},{7,6},{8,9},{9,8},{10,11... | collective-permute-start | bytes 1056776 | tf_op jit(solution)/shard_map/ppermute | solution.py:174
  113.7 14.0 %collective-permute-start.24 = (bf16[344,512]{1,0:T(8,128)(2,1)S(1)}, bf16[344,512]{1,0:T(8,128)(2,1)S(1)}, u32[]{:S(2)}, u32[]{:S(2)}) collective-permute-start(bf16[344,512]{1,0:T(8,128)(2,1)S(1)} %collective-permute-done.21), channel_id=1, source_target_pairs={{8,0},{9,1},{10,2},{11,3},{12,4},{13,5},{14,6},{15,7},{16,8},{17,9... | collective-permute-start | bytes 1056776 | tf_op jit(solution)/shard_map/ppermute | solution.py:180
  115.0 13.1 %collective-permute-start.25 = (bf16[344,512]{1,0:T(8,128)(2,1)S(1)}, bf16[344,512]{1,0:T(8,128)(2,1)S(1)}, u32[]{:S(2)}, u32[]{:S(2)}) collective-permute-start(bf16[344,512]{1,0:T(8,128)(2,1)S(1)} %collective-permute-done.22), channel_id=1, source_target_pairs={{0,8},{1,9},{2,10},{3,11},{4,12},{5,13},{6,14},{7,15},{8,16},{9,17... | collective-permute-start | bytes 1056776 | tf_op jit(solution)/shard_map/ppermute | solution.py:177
  119.6 14.2 %collective-permute-start.11 = (bf16[344,512]{1,0:T(8,128)(2,1)S(1)}, bf16[344,512]{1,0:T(8,128)(2,1)S(1)}, u32[]{:S(2)}, u32[]{:S(2)}) collective-permute-start(bf16[344,512]{1,0:T(8,128)(2,1)S(1)} %collective-permute-done.8), channel_id=1, source_target_pairs={{8,0},{9,1},{10,2},{11,3},{12,4},{13,5},{14,6},{15,7},{16,8},{17,9... | collective-permute-start | bytes 1056776 | tf_op jit(solution)/shard_map/ppermute | solution.py:180
  120.9 14.1 %collective-permute-start.12 = (bf16[344,512]{1,0:T(8,128)(2,1)S(1)}, bf16[344,512]{1,0:T(8,128)(2,1)S(1)}, u32[]{:S(2)}, u32[]{:S(2)}) collective-permute-start(bf16[344,512]{1,0:T(8,128)(2,1)S(1)} %collective-permute-done.9), channel_id=1, source_target_pairs={{0,8},{1,9},{2,10},{3,11},{4,12},{5,13},{6,14},{7,15},{8,16},{9,17... | collective-permute-start | bytes 1056776 | tf_op jit(solution)/shard_map/ppermute | solution.py:177
  129.3 7.9 %collective-permute-start.20 = (bf16[344,512]{1,0:T(8,128)(2,1)S(1)}, bf16[344,512]{1,0:T(8,128)(2,1)S(1)}, u32[]{:S(2)}, u32[]{:S(2)}) collective-permute-start(bf16[344,512]{1,0:T(8,128)(2,1)S(1)} %get-tuple-element.87), channel_id=1, source_target_pairs={{0,1},{1,0},{2,3},{3,2},{4,5},{5,4},{6,7},{7,6},{8,9},{9,8},{10,11... | collective-permute-start | bytes 1056776 | tf_op jit(solution)/shard_map/ppermute | solution.py:174
  129.4 10.0 %collective-permute-start.23 = (bf16[344,512]{1,0:T(8,128)(2,1)S(1)}, bf16[344,512]{1,0:T(8,128)(2,1)S(1)}, u32[]{:S(2)}, u32[]{:S(2)}) collective-permute-start(bf16[344,512]{1,0:T(8,128)(2,1)S(1)} %get-tuple-element.84), channel_id=1, source_target_pairs={{0,1},{1,0},{2,3},{3,2},{4,5},{5,4},{6,7},{7,6},{8,9},{9,8},{10,11... | collective-permute-start | bytes 1056776 | tf_op jit(solution)/shard_map/ppermute | solution.py:174
  129.9 10.6 %collective-permute-start.26 = (bf16[344,512]{1,0:T(8,128)(2,1)S(1)}, bf16[344,512]{1,0:T(8,128)(2,1)S(1)}, u32[]{:S(2)}, u32[]{:S(2)}) collective-permute-start(bf16[344,512]{1,0:T(8,128)(2,1)S(1)} %get-tuple-element.85), channel_id=1, source_target_pairs={{0,1},{1,0},{2,3},{3,2},{4,5},{5,4},{6,7},{7,6},{8,9},{9,8},{10,11... | collective-permute-start | bytes 1056776 | tf_op jit(solution)/shard_map/ppermute | solution.py:174
  136.1 7.0 %collective-permute-start.7 = (bf16[344,512]{1,0:T(8,128)(2,1)S(1)}, bf16[344,512]{1,0:T(8,128)(2,1)S(1)}, u32[]{:S(2)}, u32[]{:S(2)}) collective-permute-start(bf16[344,512]{1,0:T(8,128)(2,1)S(1)} %get-tuple-element.86), channel_id=1, source_target_pairs={{0,1},{1,0},{2,3},{3,2},{4,5},{5,4},{6,7},{7,6},{8,9},{9,8},{10,11... | collective-permute-start | bytes 1056776 | tf_op jit(solution)/shard_map/ppermute | solution.py:174
  136.2 11.2 %collective-permute-start.10 = (bf16[344,512]{1,0:T(8,128)(2,1)S(1)}, bf16[344,512]{1,0:T(8,128)(2,1)S(1)}, u32[]{:S(2)}, u32[]{:S(2)}) collective-permute-start(bf16[344,512]{1,0:T(8,128)(2,1)S(1)} %get-tuple-element.82), channel_id=1, source_target_pairs={{0,1},{1,0},{2,3},{3,2},{4,5},{5,4},{6,7},{7,6},{8,9},{9,8},{10,11... | collective-permute-start | bytes 1056776 | tf_op jit(solution)/shard_map/ppermute | solution.py:174
  137.2 11.3 %collective-permute-start.13 = (bf16[344,512]{1,0:T(8,128)(2,1)S(1)}, bf16[344,512]{1,0:T(8,128)(2,1)S(1)}, u32[]{:S(2)}, u32[]{:S(2)}) collective-permute-start(bf16[344,512]{1,0:T(8,128)(2,1)S(1)} %get-tuple-element.83), channel_id=1, source_target_pairs={{0,1},{1,0},{2,3},{3,2},{4,5},{5,4},{6,7},{7,6},{8,9},{9,8},{10,11... | collective-permute-start | bytes 1056776 | tf_op jit(solution)/shard_map/ppermute | solution.py:174
  141.6 9.5 %collective-permute-start.27 = (bf16[176,512]{1,0:T(8,128)(2,1)S(1)}, bf16[176,512]{1,0:T(8,128)(2,1)S(1)}, u32[]{:S(2)}, u32[]{:S(2)}) collective-permute-start(bf16[176,512]{1,0:T(8,128)(2,1)S(1)} %get-tuple-element.79), channel_id=1, source_target_pairs={{0,2},{1,3},{2,0},{3,1},{4,6},{5,7},{6,4},{7,5},{8,10},{9,11},{10,... | collective-permute-start | bytes 540680 | tf_op jit(solution)/shard_map/ppermute | solution.py:174
  142.2 11.0 %collective-permute-start.28 = (bf16[176,512]{1,0:T(8,128)(2,1)S(1)}, bf16[176,512]{1,0:T(8,128)(2,1)S(1)}, u32[]{:S(2)}, u32[]{:S(2)}) collective-permute-start(bf16[176,512]{1,0:T(8,128)(2,1)S(1)} %get-tuple-element.81), channel_id=1, source_target_pairs={{0,4},{1,5},{2,6},{3,7},{4,0},{5,1},{6,2},{7,3},{8,12},{9,13},{10,... | collective-permute-start | bytes 540680 | tf_op jit(solution)/shard_map/ppermute | solution.py:174
  143.1 10.1 %collective-permute-start.29 = (bf16[176,512]{1,0:T(8,128)(2,1)S(1)}, bf16[176,512]{1,0:T(8,128)(2,1)S(1)}, u32[]{:S(2)}, u32[]{:S(2)}) collective-permute-start(bf16[176,512]{1,0:T(8,128)(2,1)S(1)} %get-tuple-element.80), channel_id=1, source_target_pairs={{0,6},{1,7},{2,4},{3,5},{4,2},{5,3},{6,0},{7,1},{8,14},{9,15},{10,... | collective-permute-start | bytes 540680 | tf_op jit(solution)/shard_map/ppermute | solution.py:174
  149.7 7.6 %collective-permute-start.14 = (bf16[176,512]{1,0:T(8,128)(2,1)S(1)}, bf16[176,512]{1,0:T(8,128)(2,1)S(1)}, u32[]{:S(2)}, u32[]{:S(2)}) collective-permute-start(bf16[176,512]{1,0:T(8,128)(2,1)S(1)} %get-tuple-element.76), channel_id=1, source_target_pairs={{0,2},{1,3},{2,0},{3,1},{4,6},{5,7},{6,4},{7,5},{8,10},{9,11},{10,... | collective-permute-start | bytes 540680 | tf_op jit(solution)/shard_map/ppermute | solution.py:174
  150.2 10.2 %collective-permute-start.15 = (bf16[176,512]{1,0:T(8,128)(2,1)S(1)}, bf16[176,512]{1,0:T(8,128)(2,1)S(1)}, u32[]{:S(2)}, u32[]{:S(2)}) collective-permute-start(bf16[176,512]{1,0:T(8,128)(2,1)S(1)} %get-tuple-element.78), channel_id=1, source_target_pairs={{0,4},{1,5},{2,6},{3,7},{4,0},{5,1},{6,2},{7,3},{8,12},{9,13},{10,... | collective-permute-start | bytes 540680 | tf_op jit(solution)/shard_map/ppermute | solution.py:174
  151.2 9.2 %collective-permute-start.16 = (bf16[176,512]{1,0:T(8,128)(2,1)S(1)}, bf16[176,512]{1,0:T(8,128)(2,1)S(1)}, u32[]{:S(2)}, u32[]{:S(2)}) collective-permute-start(bf16[176,512]{1,0:T(8,128)(2,1)S(1)} %get-tuple-element.77), channel_id=1, source_target_pairs={{0,6},{1,7},{2,4},{3,5},{4,2},{5,3},{6,0},{7,1},{8,14},{9,15},{10,... | collective-permute-start | bytes 540680 | tf_op jit(solution)/shard_map/ppermute | solution.py:174
  160.9 10.2 %collective-permute-start.33 = (bf16[176,1024]{1,0:T(8,128)(2,1)S(1)}, bf16[176,1024]{1,0:T(8,128)(2,1)S(1)}, u32[]{:S(2)}, u32[]{:S(2)}) collective-permute-start(bf16[176,1024]{1,0:T(8,128)(2,1)S(1)} %multiply_convert_fusion.1.refs_1_.refs_5_), channel_id=1, source_target_pairs={{0,8},{1,9},{2,10},{3,11},{4,12},{5,13},{6,14},{7,15},{8,0},{9,1},... | collective-permute-start | bytes 1081352 | tf_op jit(solution)/shard_map/ppermute | solution.py:174
  163.5 9.1 %collective-permute-start.30 = (bf16[176,1024]{1,0:T(8,128)(2,1)S(1)}, bf16[176,1024]{1,0:T(8,128)(2,1)S(1)}, u32[]{:S(2)}, u32[]{:S(2)}) collective-permute-start(bf16[176,1024]{1,0:T(8,128)(2,1)S(1)} %multiply_convert_fusion.1.refs_1_.refs_5_), channel_id=1, source_target_pairs={{0,2},{1,3},{2,0},{3,1},{4,6},{5,7},{6,4},{7,5},{8,10},{9,11},{10,... | collective-permute-start | bytes 1081352 | tf_op jit(solution)/shard_map/ppermute | solution.py:174
  165.0 11.3 %collective-permute-start.31 = (bf16[176,1024]{1,0:T(8,128)(2,1)S(1)}, bf16[176,1024]{1,0:T(8,128)(2,1)S(1)}, u32[]{:S(2)}, u32[]{:S(2)}) collective-permute-start(bf16[176,1024]{1,0:T(8,128)(2,1)S(1)} %multiply_convert_fusion.1.refs_1_.refs_5_), channel_id=1, source_target_pairs={{0,4},{1,5},{2,6},{3,7},{4,0},{5,1},{6,2},{7,3},{8,12},{9,13},{10,... | collective-permute-start | bytes 1081352 | tf_op jit(solution)/shard_map/ppermute | solution.py:174
  171.1 11.3 %collective-permute-start.35 = (bf16[176,1024]{1,0:T(8,128)(2,1)S(1)}, bf16[176,1024]{1,0:T(8,128)(2,1)S(1)}, u32[]{:S(2)}, u32[]{:S(2)}) collective-permute-start(bf16[176,1024]{1,0:T(8,128)(2,1)S(1)} %collective-permute-done.33.refs_1_.refs_9_), channel_id=1, source_target_pairs={{0,4},{1,5},{2,6},{3,7},{4,0},{5,1},{6,2},{7,3},{8,12},{9,13},{10,... | collective-permute-start | bytes 1081352 | tf_op jit(solution)/shard_map/ppermute | solution.py:174
  172.6 16.2 %collective-permute-start.32 = (bf16[176,1024]{1,0:T(8,128)(2,1)S(1)}, bf16[176,1024]{1,0:T(8,128)(2,1)S(1)}, u32[]{:S(2)}, u32[]{:S(2)}) collective-permute-start(bf16[176,1024]{1,0:T(8,128)(2,1)S(1)} %collective-permute-done.30.refs_2_.refs_6_), channel_id=1, source_target_pairs={{0,4},{1,5},{2,6},{3,7},{4,0},{5,1},{6,2},{7,3},{8,12},{9,13},{10,... | collective-permute-start | bytes 1081352 | tf_op jit(solution)/shard_map/ppermute | solution.py:174
  174.0 18.5 %collective-permute-start.40 = (bf16[176,1024]{1,0:T(8,128)(2,1)S(1)}, bf16[176,1024]{1,0:T(8,128)(2,1)S(1)}, u32[]{:S(2)}, u32[]{:S(2)}) collective-permute-start(bf16[176,1024]{1,0:T(8,128)(2,1)S(1)} %multiply_convert_fusion.1.refs_1_.refs_5_), channel_id=1, source_target_pairs={{0,24},{1,25},{2,26},{3,27},{4,28},{5,29},{6,30},{7,31},{8,16},{9,... | collective-permute-start | bytes 1081352 | tf_op jit(solution)/shard_map/ppermute | solution.py:174
  175.2 30.1 %collective-permute-start.37 = (bf16[176,1024]{1,0:T(8,128)(2,1)S(1)}, bf16[176,1024]{1,0:T(8,128)(2,1)S(1)}, u32[]{:S(2)}, u32[]{:S(2)}) collective-permute-start(bf16[176,1024]{1,0:T(8,128)(2,1)S(1)} %multiply_convert_fusion.1.refs_1_.refs_5_), channel_id=1, source_target_pairs={{0,16},{1,17},{2,18},{3,19},{4,20},{5,21},{6,22},{7,23},{8,24},{9,... | collective-permute-start | bytes 1081352 | tf_op jit(solution)/shard_map/ppermute | solution.py:174
  176.3 29.5 %collective-permute-start.34 = (bf16[176,1024]{1,0:T(8,128)(2,1)S(1)}, bf16[176,1024]{1,0:T(8,128)(2,1)S(1)}, u32[]{:S(2)}, u32[]{:S(2)}) collective-permute-start(bf16[176,1024]{1,0:T(8,128)(2,1)S(1)} %collective-permute-done.33.refs_1_.refs_9_), channel_id=1, source_target_pairs={{0,2},{1,3},{2,0},{3,1},{4,6},{5,7},{6,4},{7,5},{8,10},{9,11},{10,... | collective-permute-start | bytes 1081352 | tf_op jit(solution)/shard_map/ppermute | solution.py:174
  182.5 25.1 %collective-permute-start.36 = (bf16[176,1024]{1,0:T(8,128)(2,1)S(1)}, bf16[176,1024]{1,0:T(8,128)(2,1)S(1)}, u32[]{:S(2)}, u32[]{:S(2)}) collective-permute-start(bf16[176,1024]{1,0:T(8,128)(2,1)S(1)} %collective-permute-done.35.refs_3_.refs_11_), channel_id=1, source_target_pairs={{0,2},{1,3},{2,0},{3,1},{4,6},{5,7},{6,4},{7,5},{8,10},{9,11},{10,... | collective-permute-start | bytes 1081352 | tf_op jit(solution)/shard_map/ppermute | solution.py:174
  192.5 25.8 %collective-permute-start.41 = (bf16[176,1024]{1,0:T(8,128)(2,1)S(1)}, bf16[176,1024]{1,0:T(8,128)(2,1)S(1)}, u32[]{:S(2)}, u32[]{:S(2)}) collective-permute-start(bf16[176,1024]{1,0:T(8,128)(2,1)S(1)} %collective-permute-done.40.refs_4_.refs_16_), channel_id=1, source_target_pairs={{0,2},{1,3},{2,0},{3,1},{4,6},{5,7},{6,4},{7,5},{8,10},{9,11},{10,... | collective-permute-start | bytes 1081352 | tf_op jit(solution)/shard_map/ppermute | solution.py:174
  193.6 17.9 %collective-permute-start.42 = (bf16[176,1024]{1,0:T(8,128)(2,1)S(1)}, bf16[176,1024]{1,0:T(8,128)(2,1)S(1)}, u32[]{:S(2)}, u32[]{:S(2)}) collective-permute-start(bf16[176,1024]{1,0:T(8,128)(2,1)S(1)} %collective-permute-done.40.refs_4_.refs_16_), channel_id=1, source_target_pairs={{0,4},{1,5},{2,6},{3,7},{4,0},{5,1},{6,2},{7,3},{8,12},{9,13},{10,... | collective-permute-start | bytes 1081352 | tf_op jit(solution)/shard_map/ppermute | solution.py:174
  205.4 10.0 %collective-permute-start.38 = (bf16[176,1024]{1,0:T(8,128)(2,1)S(1)}, bf16[176,1024]{1,0:T(8,128)(2,1)S(1)}, u32[]{:S(2)}, u32[]{:S(2)}) collective-permute-start(bf16[176,1024]{1,0:T(8,128)(2,1)S(1)} %collective-permute-done.37.refs_1_.refs_13_), channel_id=1, source_target_pairs={{0,2},{1,3},{2,0},{3,1},{4,6},{5,7},{6,4},{7,5},{8,10},{9,11},{10,... | collective-permute-start | bytes 1081352 | tf_op jit(solution)/shard_map/ppermute | solution.py:174
  205.8 12.5 %collective-permute-start.39 = (bf16[176,1024]{1,0:T(8,128)(2,1)S(1)}, bf16[176,1024]{1,0:T(8,128)(2,1)S(1)}, u32[]{:S(2)}, u32[]{:S(2)}) collective-permute-start(bf16[176,1024]{1,0:T(8,128)(2,1)S(1)} %collective-permute-done.37.refs_1_.refs_13_), channel_id=1, source_target_pairs={{0,4},{1,5},{2,6},{3,7},{4,0},{5,1},{6,2},{7,3},{8,12},{9,13},{10,... | collective-permute-start | bytes 1081352 | tf_op jit(solution)/shard_map/ppermute | solution.py:174
  211.4 12.7 %collective-permute-start.44 = (bf16[176,1024]{1,0:T(8,128)(2,1)S(1)}, bf16[176,1024]{1,0:T(8,128)(2,1)S(1)}, u32[]{:S(2)}, u32[]{:S(2)}) collective-permute-start(bf16[176,1024]{1,0:T(8,128)(2,1)S(1)} %collective-permute-done.42.refs_6_.refs_18_), channel_id=1, source_target_pairs={{0,2},{1,3},{2,0},{3,1},{4,6},{5,7},{6,4},{7,5},{8,10},{9,11},{10,... | collective-permute-start | bytes 1081352 | tf_op jit(solution)/shard_map/ppermute | solution.py:174
  215.3 8.8 %collective-permute-start.43 = (bf16[176,1024]{1,0:T(8,128)(2,1)S(1)}, bf16[176,1024]{1,0:T(8,128)(2,1)S(1)}, u32[]{:S(2)}, u32[]{:S(2)}) collective-permute-start(bf16[176,1024]{1,0:T(8,128)(2,1)S(1)} %collective-permute-done.38.refs_2_.refs_14_), channel_id=1, source_target_pairs={{0,4},{1,5},{2,6},{3,7},{4,0},{5,1},{6,2},{7,3},{8,12},{9,13},{10,... | collective-permute-start | bytes 1081352 | tf_op jit(solution)/shard_map/ppermute | solution.py:174
  233.9 4.8 %collective-permute-start.49 = (f32[4,4,176]{2,1,0:T(4,128)S(1)}, f32[4,4,176]{2,1,0:T(4,128)S(1)}, u32[]{:S(2)}, u32[]{:S(2)}) collective-permute-start(f32[4,4,176]{2,1,0:T(4,128)S(1)} %log_add_fusion.1), channel_id=1, source_target_pairs={{0,16},{1,17},{2,18},{3,19},{4,20},{5,21},{6,22},{7,23},{8,24},{9,... | collective-permute-start | bytes 33800 | tf_op jit(solution)/shard_map/ppermute | solution.py:174
  236.0 5.5 %collective-permute-start.50 = (f32[4,4,176]{2,1,0:T(4,128)S(1)}, f32[4,4,176]{2,1,0:T(4,128)S(1)}, u32[]{:S(2)}, u32[]{:S(2)}) collective-permute-start(f32[4,4,176]{2,1,0:T(4,128)S(1)} %log_add_fusion.1), channel_id=1, source_target_pairs={{0,24},{1,25},{2,26},{3,27},{4,28},{5,29},{6,30},{7,31},{8,16},{9,... | collective-permute-start | bytes 33800 | tf_op jit(solution)/shard_map/ppermute | solution.py:174
  (39 other events, 354.1 us)
